TPU v7x, 32 devices: a whole 2x2x4 slice. The times are simulated.
32 devices in a mesh: sp: 4 (over z), fsdp: 8 (over y, x, core).
Axes of the slice: x: 2, y: 2, z: 4, core: 2. Of those that a mesh axis runs over, the one named last changes fastest.
Arguments:
- tokens: bfloat16 [4, 8, 256, 768], P(None, 'fsdp', 'sp'), may hold values from -6 to 6
- lengths: int32 [4], replicated, may hold values from 512 to 2048, as said below
- cotangent: bfloat16 [4, 8, 256, 768], P(None, 'fsdp', 'sp'), may hold values from -6 to 6
- pre_gain: bfloat16 [768], P('fsdp'), may hold values from 0.5 to 1.5
- query_weight: bfloat16 [768, 768], P('fsdp'), may hold values from -0.21875 to 0.21875
- key_weight: bfloat16 [768, 768], P('fsdp'), may hold values from -0.21875 to 0.21875
- value_weight: bfloat16 [768, 768], P('fsdp'), may hold values from -0.21875 to 0.21875
- gate_weight: bfloat16 [768, 768], P('fsdp'), may hold values from -0.21875 to 0.21875
- rate_weight: bfloat16 [768, 12], P('fsdp'), may hold values from -0.21875 to 0.21875
- out_weight: bfloat16 [768, 768], P('fsdp'), may hold values from -0.21875 to 0.21875
- post_gain: bfloat16 [768], P('fsdp'), may hold values from 0.5 to 1.5
- ffn_gate: bfloat16 [768, 2048], P('fsdp'), may hold values from -0.21875 to 0.21875
- ffn_up: bfloat16 [768, 2048], P('fsdp'), may hold values from -0.21875 to 0.21875
- ffn_down: bfloat16 [2048, 768], P('fsdp'), may hold values from -0.125 to 0.125
- inner_first: float32 [12, 64, 256], P('sp'), may hold values from -0.75 to 0.75
- inner_first_bias: float32 [12, 256], P('sp'), may hold values from -1.75 to 1.75
- inner_second: float32 [12, 256, 64], P('sp'), may hold values from -0.375 to 0.375
- inner_second_bias: float32 [12, 64], P('sp'), may hold values from -1.75 to 1.75
- inner_gain: float32 [12, 64], P('sp'), may hold values from 0.5 to 1.5
- inner_shift: float32 [12, 64], P('sp'), may hold values from -1.75 to 1.75
Outputs:
- output: bfloat16 [4, 8, 256, 768], P(None, 'fsdp', 'sp')
- tokens_grad: bfloat16 [4, 8, 256, 768], P(None, 'fsdp', 'sp')
- pre_gain_grad: float32 [768], P('fsdp')
- query_weight_grad: float32 [768, 768], P('fsdp')
- key_weight_grad: float32 [768, 768], P('fsdp')
- value_weight_grad: float32 [768, 768], P('fsdp')
- gate_weight_grad: float32 [768, 768], P('fsdp')
- rate_weight_grad: float32 [768, 12], P('fsdp')
- out_weight_grad: float32 [768, 768], P('fsdp')
- post_gain_grad: float32 [768], P('fsdp')
- ffn_gate_grad: float32 [768, 2048], P('fsdp')
- ffn_up_grad: float32 [768, 2048], P('fsdp')
- ffn_down_grad: float32 [2048, 768], P('fsdp')
- inner_first_grad: float32 [12, 64, 256], P('sp')
- inner_first_bias_grad: float32 [12, 256], P('sp')
- inner_second_grad: float32 [12, 256, 64], P('sp')
- inner_second_bias_grad: float32 [12, 64], P('sp')
- inner_gain_grad: float32 [12, 64], P('sp')
- inner_shift_grad: float32 [12, 64], P('sp')
Inputs may be any that keep to these rules, and one draw needn't show every extreme that they name: `lengths`: every micro-batch holds 512 or more tokens followed by padding; in every draw one micro-batch is full (2048 tokens).
All inputs are finite; a program needn't handle non-finite values.
Results may differ from a plain program's by a relative error of at most 0.019.
Values may be sent and summed in bfloat16 or wider, within the bound.
No kernel may reach another device: no remote copies, remote signals or barrier semaphores. Data moves between devices by JAX's collectives and lax.ppermute only.
A program may use at most 128 MiB of HBM per device.

v0:
```python
import jax
import jax.numpy as jnp
from jax import lax
from jax.sharding import PartitionSpec as P

MINI = 16
MICRO = 4


EPS = 1e-06
RATE = 1.0 / 1024.0
GELU_C = 0.7978845608028654
GELU_K = 0.044715


def from_behind(block, axis, distance):
    devices = range(lax.axis_size(axis))
    route = [(i - distance, i) for i in devices if i - distance in devices]
    return lax.ppermute(block, axis, route)


def einsum_high(formula, left, right):
    return jnp.einsum(formula, left, right, precision=lax.Precision.HIGHEST)


def dot_plain(left, right):
    return jnp.dot(left, right, preferred_element_type=jnp.float32)


def dot_left(left, right):
    return lax.dot_general(
        left, right, (((0,), (0,)), ((), ())), preferred_element_type=jnp.float32
    )


def dot_right(left, right):
    return lax.dot_general(
        left, right, (((1,), (1,)), ((), ())), preferred_element_type=jnp.float32
    )


def rms_back(grad_scaled, inputs, scale):
    return scale * (
        grad_scaled - inputs * scale * scale * jnp.mean(grad_scaled * inputs, -1, keepdims=True)
    )


def gelu_pair(inputs):
    tangent = jnp.tanh(GELU_C * (inputs + GELU_K * inputs * inputs * inputs))
    values_out = 0.5 * inputs * (1.0 + tangent)
    slope = 0.5 * (1.0 + tangent) + 0.5 * inputs * (1.0 - tangent * tangent) * GELU_C * (
        1.0 + 3.0 * GELU_K * inputs * inputs
    )
    return (values_out, slope)


def inner_norm(inputs, inner_gain, inner_shift):
    centred = inputs - jnp.mean(inputs, -1, keepdims=True)
    spread = lax.rsqrt(jnp.mean(centred * centred, -1, keepdims=True) + EPS)
    normal = centred * spread
    return (normal * inner_gain[:, None, :] + inner_shift[:, None, :], normal, spread)


def mini_step(inner_state, block_in, inner_gain, inner_shift, causal):
    weight_one, bias_one, weight_two, bias_two = inner_state
    query_block, key_block, value_block, rate_block = block_in
    first_pre = einsum_high("gme,gef->gmf", key_block, weight_one) + bias_one[:, None, :]
    first_act, first_slope = gelu_pair(first_pre)
    second_pre = einsum_high("gmf,gfe->gme", first_act, weight_two) + bias_two[:, None, :]
    fitted, normal, spread = inner_norm(second_pre, inner_gain, inner_shift)
    mismatch = fitted - (value_block - key_block)
    grad_normal = mismatch * inner_gain[:, None, :]
    grad_second = spread * (
        grad_normal
        - jnp.mean(grad_normal, -1, keepdims=True)
        - normal * jnp.mean(grad_normal * normal, -1, keepdims=True)
    )
    grad_first = einsum_high("gme,gfe->gmf", grad_second, weight_two) * first_slope
    scaled_first = rate_block[:, :, None] * grad_first
    scaled_second = rate_block[:, :, None] * grad_second
    mask_one = (einsum_high("gme,gne->gmn", query_block, key_block) + 1.0) * causal
    query_pre = (
        einsum_high("gme,gef->gmf", query_block, weight_one)
        + bias_one[:, None, :]
        - einsum_high("gmn,gnf->gmf", mask_one, scaled_first)
    )
    query_act = gelu_pair(query_pre)[0]
    mask_two = (einsum_high("gmf,gnf->gmn", query_act, first_act) + 1.0) * causal
    query_out = (
        einsum_high("gmf,gfe->gme", query_act, weight_two)
        + bias_two[:, None, :]
        - einsum_high("gmn,gne->gme", mask_two, scaled_second)
    )
    mixed_block = query_block + inner_norm(query_out, inner_gain, inner_shift)[0]
    next_state = (
        weight_one - einsum_high("gme,gmf->gef", key_block, scaled_first),
        bias_one - jnp.sum(scaled_first, 1),
        weight_two - einsum_high("gmf,gme->gfe", first_act, scaled_second),
        bias_two - jnp.sum(scaled_second, 1),
    )
    return (next_state, mixed_block)


def piece_mixer(
    inner_state, query_heads, key_heads, value_heads, rate_heads, inner_gain, inner_shift
):
    piece_len = query_heads.shape[0]
    group_count = query_heads.shape[1]
    head_width = query_heads.shape[2]
    block_count = piece_len // MINI

    def arrange(tensor):
        return tensor.reshape(block_count, MINI, group_count, head_width).transpose(0, 2, 1, 3)

    rate_blocks = rate_heads.reshape(block_count, MINI, group_count).transpose(0, 2, 1)
    causal = (
        lax.broadcasted_iota(jnp.int32, (MINI, MINI), 0)
        >= lax.broadcasted_iota(jnp.int32, (MINI, MINI), 1)
    ).astype(jnp.float32)

    def advance(carried, block_in):
        return mini_step(carried, block_in, inner_gain, inner_shift, causal)

    final_state, mixed_blocks = lax.scan(
        jax.checkpoint(advance),
        inner_state,
        (arrange(query_heads), arrange(key_heads), arrange(value_heads), rate_blocks),
    )
    return (
        mixed_blocks.transpose(0, 2, 1, 3).reshape(piece_len, group_count, head_width),
        final_state,
    )


def pack_state(inner_state):
    weight_one, bias_one, weight_two, bias_two = inner_state
    group_count = weight_one.shape[0]
    return jnp.concatenate(
        [
            weight_one.reshape(group_count, -1),
            bias_one,
            weight_two.reshape(group_count, -1),
            bias_two,
        ],
        axis=1,
    )


def unpack_state(packed, head_width, inner_width):
    group_count = packed.shape[0]
    first_end = head_width * inner_width
    bias_end = first_end + inner_width
    second_end = bias_end + inner_width * head_width
    return (
        packed[:, :first_end].reshape(group_count, head_width, inner_width),
        packed[:, first_end:bias_end],
        packed[:, bias_end:second_end].reshape(group_count, inner_width, head_width),
        packed[:, second_end:],
    )


def pick(array_in, slot_index):
    return lax.dynamic_index_in_dim(array_in, slot_index, 0, keepdims=False)


def place(buffer, update, slot_index):
    return lax.dynamic_update_index_in_dim(buffer, update, slot_index, 0)


def accumulate(total, term):
    return term if total is None else total + term


def fetch_front(gain_in, query_in, key_in, value_in, gate_in, rate_in):
    return (
        lax.all_gather(gain_in, "fsdp", axis=0, tiled=True),
        lax.all_gather(query_in, "fsdp", axis=0, tiled=True),
        lax.all_gather(key_in, "fsdp", axis=0, tiled=True),
        lax.all_gather(value_in, "fsdp", axis=0, tiled=True),
        lax.all_gather(gate_in, "fsdp", axis=0, tiled=True),
        lax.all_gather(rate_in, "fsdp", axis=0, tiled=True),
    )


def fetch_rear(out_in, gain_in, gate_in, up_in, down_in):
    return (
        lax.all_gather(out_in, "fsdp", axis=0, tiled=True),
        lax.all_gather(gain_in, "fsdp", axis=0, tiled=True),
        lax.all_gather(gate_in, "fsdp", axis=0, tiled=True),
        lax.all_gather(up_in, "fsdp", axis=0, tiled=True),
        lax.all_gather(down_in, "fsdp", axis=0, tiled=True),
    )


def shards(
    tokens,
    lengths,
    cotangent,
    pre_gain,
    query_weight,
    key_weight,
    value_weight,
    gate_weight,
    rate_weight,
    out_weight,
    post_gain,
    ffn_gate,
    ffn_up,
    ffn_down,
    inner_first,
    inner_first_bias,
    inner_second,
    inner_second_bias,
    inner_gain,
    inner_shift,
):
    piece_rows = tokens.shape[2]
    model_width = tokens.shape[3]
    head_width = inner_gain.shape[1]
    inner_width = inner_first.shape[2]
    head_count = model_width // head_width
    sp_count = lax.axis_size("sp")
    fsdp_count = lax.axis_size("fsdp")
    sp_index = lax.axis_index("sp")
    fsdp_index = lax.axis_index("fsdp")
    head_shape = (piece_rows, head_count, head_width)
    front_saved = []
    heads_query = []
    heads_key = []
    heads_value = []
    heads_rate = []
    for micro_index in range(MICRO):
        front_now = fetch_front(
            pre_gain, query_weight, key_weight, value_weight, gate_weight, rate_weight
        )
        gain_full, query_full, key_full, value_full, gate_full, rate_full = front_now
        token_rows = tokens[micro_index, 0].astype(jnp.float32)
        scale_one = lax.rsqrt(jnp.mean(token_rows * token_rows, -1, keepdims=True) + EPS)
        normed = (token_rows * scale_one * gain_full.astype(jnp.float32)).astype(jnp.bfloat16)
        query_rows = dot_plain(normed, query_full).astype(jnp.bfloat16)
        key_rows = dot_plain(normed, key_full).astype(jnp.bfloat16)
        value_rows = dot_plain(normed, value_full).astype(jnp.bfloat16)
        gate_logit = dot_plain(normed, gate_full)
        rate_sig = jax.nn.sigmoid(dot_plain(normed, rate_full))
        rate_rows = (RATE * rate_sig).astype(jnp.bfloat16)
        query_heads, key_heads, value_heads, rate_heads = (
            lax.all_to_all(
                query_rows.reshape(head_shape), "sp", split_axis=1, concat_axis=0, tiled=True
            ),
            lax.all_to_all(
                key_rows.reshape(head_shape), "sp", split_axis=1, concat_axis=0, tiled=True
            ),
            lax.all_to_all(
                value_rows.reshape(head_shape), "sp", split_axis=1, concat_axis=0, tiled=True
            ),
            lax.all_to_all(
                rate_rows.reshape(piece_rows, head_count, 1),
                "sp",
                split_axis=1,
                concat_axis=0,
                tiled=True,
            ),
        )
        heads_query.append(query_heads)
        heads_key.append(key_heads)
        heads_value.append(value_heads)
        heads_rate.append(rate_heads)
        front_saved.append((scale_one, normed, gate_logit, rate_sig))
    queries_all = jnp.stack(heads_query).astype(jnp.float32)
    keys_all = jnp.stack(heads_key).astype(jnp.float32)
    values_all = jnp.stack(heads_value).astype(jnp.float32)
    rates_all = jnp.stack(heads_rate)[:, :, :, 0].astype(jnp.float32)
    init_packed = pack_state((inner_first, inner_first_bias, inner_second, inner_second_bias))
    turn_count = fsdp_count + MICRO - 1

    def forward_turn(turn_index, carried):
        outgoing, mixed_all, starts_all = carried
        incoming = from_behind(outgoing, "fsdp", 1)
        slot_index = turn_index - fsdp_index
        active = (slot_index >= 0) & (slot_index < MICRO)
        slot_safe = jnp.clip(slot_index, 0, MICRO - 1)
        start_packed = jnp.where(fsdp_index == 0, init_packed, incoming)

        def forward_compute_piece(operand):
            mixed_buffer, starts_buffer = operand
            result_rows, final_state = piece_mixer(
                unpack_state(start_packed, head_width, inner_width),
                pick(queries_all, slot_safe),
                pick(keys_all, slot_safe),
                pick(values_all, slot_safe),
                pick(rates_all, slot_safe),
                inner_gain,
                inner_shift,
            )
            return (
                pack_state(final_state),
                place(mixed_buffer, result_rows, slot_safe),
                place(starts_buffer, start_packed, slot_safe),
            )

        def forward_pass_along(operand):
            return (incoming, operand[0], operand[1])

        return lax.cond(active, forward_compute_piece, forward_pass_along, (mixed_all, starts_all))

    mixed_start = jnp.zeros(queries_all.shape, jnp.float32)
    starts_start = jnp.zeros((MICRO,) + init_packed.shape, jnp.float32)
    mixed_all, starts_all = lax.fori_loop(
        0, turn_count, forward_turn, (jnp.zeros_like(init_packed), mixed_start, starts_start)
    )[1:]
    outputs = []
    rear_saved = []
    for micro_index in range(MICRO):
        rear_now = fetch_rear(out_weight, post_gain, ffn_gate, ffn_up, ffn_down)
        out_full, post_full, gate_ffn, up_ffn, down_ffn = rear_now
        mixed_rows = lax.all_to_all(
            mixed_all[micro_index].astype(jnp.bfloat16),
            "sp",
            split_axis=0,
            concat_axis=1,
            tiled=True,
        ).reshape(piece_rows, model_width)
        gate_logit = front_saved[micro_index][2]
        gate_act, gate_slope = gelu_pair(gate_logit)
        gated = (gate_act * mixed_rows.astype(jnp.float32)).astype(jnp.bfloat16)
        token_rows = tokens[micro_index, 0].astype(jnp.float32)
        middle = token_rows + dot_plain(gated, out_full)
        scale_two = lax.rsqrt(jnp.mean(middle * middle, -1, keepdims=True) + EPS)
        normed_two = (middle * scale_two * post_full.astype(jnp.float32)).astype(jnp.bfloat16)
        gate_pre = dot_plain(normed_two, gate_ffn)
        up_pre = dot_plain(normed_two, up_ffn)
        gate_sig = jax.nn.sigmoid(gate_pre)
        silu_act = gate_pre * gate_sig
        hidden = (silu_act * up_pre).astype(jnp.bfloat16)
        outputs.append((middle + dot_plain(hidden, down_ffn)).astype(jnp.bfloat16))
        rear_saved.append(
            (
                mixed_rows,
                gate_act,
                gate_slope,
                gated,
                middle,
                scale_two,
                normed_two,
                gate_pre,
                up_pre,
                gate_sig,
                silu_act,
                hidden,
            )
        )
    position_base = fsdp_index * (piece_rows * sp_count) + sp_index * piece_rows
    row_ids = lax.broadcasted_iota(jnp.int32, (piece_rows, 1), 0) + position_base
    mixed_grads = []
    middle_grads = []
    gate_grads = []
    rear_totals = [None, None, None, None, None]
    for micro_index in range(MICRO):
        rear_now = fetch_rear(out_weight, post_gain, ffn_gate, ffn_up, ffn_down)
        out_full, post_full, gate_ffn, up_ffn, down_ffn = rear_now
        (
            mixed_rows,
            gate_act,
            gate_slope,
            gated,
            middle,
            scale_two,
            normed_two,
            gate_pre,
            up_pre,
            gate_sig,
            silu_act,
            hidden,
        ) = rear_saved[micro_index]
        live = (row_ids < lengths[micro_index]).astype(jnp.float32)
        grad_out = cotangent[micro_index, 0].astype(jnp.float32) * live
        grad_low = grad_out.astype(jnp.bfloat16)
        down_grad = dot_left(hidden, grad_low)
        grad_hidden = dot_right(grad_low, down_ffn)
        grad_gate_pre = (
            grad_hidden * up_pre * gate_sig * (1.0 + gate_pre * (1.0 - gate_sig))
        ).astype(jnp.bfloat16)
        grad_up_pre = (grad_hidden * silu_act).astype(jnp.bfloat16)
        gate_ffn_grad = dot_left(normed_two, grad_gate_pre)
        up_ffn_grad = dot_left(normed_two, grad_up_pre)
        grad_normed_two = dot_right(grad_gate_pre, gate_ffn) + dot_right(grad_up_pre, up_ffn)
        post_grad = jnp.sum(grad_normed_two * middle * scale_two, 0)
        grad_middle = grad_out + rms_back(
            grad_normed_two * post_full.astype(jnp.float32), middle, scale_two
        )
        grad_branch = grad_middle.astype(jnp.bfloat16)
        out_grad = dot_left(gated, grad_branch)
        grad_gated = dot_right(grad_branch, out_full)
        grad_mixed = (grad_gated * gate_act).astype(jnp.bfloat16)
        grad_gate_logit = (grad_gated * mixed_rows.astype(jnp.float32) * gate_slope).astype(
            jnp.bfloat16
        )
        mixed_grads.append(
            lax.all_to_all(
                grad_mixed.reshape(head_shape), "sp", split_axis=1, concat_axis=0, tiled=True
            )
        )
        middle_grads.append(grad_middle)
        gate_grads.append(grad_gate_logit)
        terms = (out_grad, post_grad, gate_ffn_grad, up_ffn_grad, down_grad)
        rear_totals = [accumulate(total, term) for total, term in zip(rear_totals, terms)]
    mixed_grad_all = jnp.stack(mixed_grads).astype(jnp.float32)

    def backward_turn(turn_index, carried):
        outgoing = carried[0]
        incoming = from_behind(outgoing.astype(jnp.bfloat16), "fsdp", -1).astype(outgoing.dtype)
        slot_index = turn_index - (fsdp_count - 1 - fsdp_index)
        active = (slot_index >= 0) & (slot_index < MICRO)
        slot_safe = jnp.clip(slot_index, 0, MICRO - 1)

        def backward_compute_piece(operand):
            grad_q_all, grad_k_all, grad_v_all, grad_r_all, gain_total, shift_total, init_total = (
                operand
            )
            start_state = unpack_state(pick(starts_all, slot_safe), head_width, inner_width)
            pullback = jax.vjp(
                piece_mixer,
                start_state,
                pick(queries_all, slot_safe),
                pick(keys_all, slot_safe),
                pick(values_all, slot_safe),
                pick(rates_all, slot_safe),
                inner_gain,
                inner_shift,
            )[1]
            grad_state, grad_q, grad_k, grad_v, grad_r, grad_gain, grad_shift = pullback(
                (pick(mixed_grad_all, slot_safe), unpack_state(incoming, head_width, inner_width))
            )
            grad_packed = pack_state(grad_state)
            on_first = (fsdp_index == 0).astype(jnp.float32)
            return (
                grad_packed,
                place(grad_q_all, grad_q, slot_safe),
                place(grad_k_all, grad_k, slot_safe),
                place(grad_v_all, grad_v, slot_safe),
                place(grad_r_all, grad_r, slot_safe),
                gain_total + grad_gain,
                shift_total + grad_shift,
                init_total + on_first * grad_packed,
            )

        def backward_pass_along(operand):
            return (incoming,) + operand

        return lax.cond(active, backward_compute_piece, backward_pass_along, carried[1:])

    backward_start = (
        jnp.zeros_like(init_packed),
        jnp.zeros_like(queries_all),
        jnp.zeros_like(keys_all),
        jnp.zeros_like(values_all),
        jnp.zeros_like(rates_all),
        jnp.zeros_like(inner_gain),
        jnp.zeros_like(inner_shift),
        jnp.zeros_like(init_packed),
    )
    backward_end = lax.fori_loop(0, turn_count, backward_turn, backward_start)
    grad_q_all, grad_k_all, grad_v_all, grad_r_all, gain_total, shift_total, init_total = (
        backward_end[1:]
    )
    front_totals = [None, None, None, None, None, None]
    token_grads = []
    for micro_index in range(MICRO):
        front_now = fetch_front(
            pre_gain, query_weight, key_weight, value_weight, gate_weight, rate_weight
        )
        gain_full, query_full, key_full, value_full, gate_full, rate_full = front_now
        scale_one, normed, gate_logit, rate_sig = front_saved[micro_index]
        grad_query, grad_key, grad_value, grad_rate = (
            lax.all_to_all(
                grad_q_all[micro_index].astype(jnp.bfloat16),
                "sp",
                split_axis=0,
                concat_axis=1,
                tiled=True,
            ),
            lax.all_to_all(
                grad_k_all[micro_index].astype(jnp.bfloat16),
                "sp",
                split_axis=0,
                concat_axis=1,
                tiled=True,
            ),
            lax.all_to_all(
                grad_v_all[micro_index].astype(jnp.bfloat16),
                "sp",
                split_axis=0,
                concat_axis=1,
                tiled=True,
            ),
            lax.all_to_all(
                grad_r_all[micro_index][:, :, None].astype(jnp.bfloat16),
                "sp",
                split_axis=0,
                concat_axis=1,
                tiled=True,
            ),
        )
        grad_query = grad_query.reshape(piece_rows, model_width)
        grad_key = grad_key.reshape(piece_rows, model_width)
        grad_value = grad_value.reshape(piece_rows, model_width)
        grad_rate_logit = (
            grad_rate.reshape(piece_rows, head_count).astype(jnp.float32)
            * RATE
            * rate_sig
            * (1.0 - rate_sig)
        ).astype(jnp.bfloat16)
        grad_gate_logit = gate_grads[micro_index]
        grad_normed = (
            dot_right(grad_query, query_full)
            + dot_right(grad_key, key_full)
            + dot_right(grad_value, value_full)
            + dot_right(grad_gate_logit, gate_full)
            + dot_right(grad_rate_logit, rate_full)
        )
        token_rows = tokens[micro_index, 0].astype(jnp.float32)
        gain_grad = jnp.sum(grad_normed * token_rows * scale_one, 0)
        token_grads.append(
            (
                middle_grads[micro_index]
                + rms_back(grad_normed * gain_full.astype(jnp.float32), token_rows, scale_one)
            ).astype(jnp.bfloat16)
        )
        terms = (
            gain_grad,
            dot_left(normed, grad_query),
            dot_left(normed, grad_key),
            dot_left(normed, grad_value),
            dot_left(normed, grad_gate_logit),
            dot_left(normed, grad_rate_logit),
        )
        front_totals = [accumulate(total, term) for total, term in zip(front_totals, terms)]
    owned = (
        lax.psum_scatter(
            front_totals[0].astype(jnp.bfloat16), "fsdp", scatter_dimension=0, tiled=True
        ).astype(jnp.float32),
        lax.psum_scatter(
            front_totals[1].astype(jnp.bfloat16), "fsdp", scatter_dimension=0, tiled=True
        ).astype(jnp.float32),
        lax.psum_scatter(
            front_totals[2].astype(jnp.bfloat16), "fsdp", scatter_dimension=0, tiled=True
        ).astype(jnp.float32),
        lax.psum_scatter(
            front_totals[3].astype(jnp.bfloat16), "fsdp", scatter_dimension=0, tiled=True
        ).astype(jnp.float32),
        lax.psum_scatter(
            front_totals[4].astype(jnp.bfloat16), "fsdp", scatter_dimension=0, tiled=True
        ).astype(jnp.float32),
        lax.psum_scatter(
            front_totals[5].astype(jnp.bfloat16), "fsdp", scatter_dimension=0, tiled=True
        ).astype(jnp.float32),
        lax.psum_scatter(
            rear_totals[0].astype(jnp.bfloat16), "fsdp", scatter_dimension=0, tiled=True
        ).astype(jnp.float32),
        lax.psum_scatter(
            rear_totals[1].astype(jnp.bfloat16), "fsdp", scatter_dimension=0, tiled=True
        ).astype(jnp.float32),
        lax.psum_scatter(
            rear_totals[2].astype(jnp.bfloat16), "fsdp", scatter_dimension=0, tiled=True
        ).astype(jnp.float32),
        lax.psum_scatter(
            rear_totals[3].astype(jnp.bfloat16), "fsdp", scatter_dimension=0, tiled=True
        ).astype(jnp.float32),
        lax.psum_scatter(
            rear_totals[4].astype(jnp.bfloat16), "fsdp", scatter_dimension=0, tiled=True
        ).astype(jnp.float32),
    )
    owned = (
        lax.psum(owned[0].astype(jnp.bfloat16), "sp").astype(jnp.float32),
        lax.psum(owned[1].astype(jnp.bfloat16), "sp").astype(jnp.float32),
        lax.psum(owned[2].astype(jnp.bfloat16), "sp").astype(jnp.float32),
        lax.psum(owned[3].astype(jnp.bfloat16), "sp").astype(jnp.float32),
        lax.psum(owned[4].astype(jnp.bfloat16), "sp").astype(jnp.float32),
        lax.psum(owned[5].astype(jnp.bfloat16), "sp").astype(jnp.float32),
        lax.psum(owned[6].astype(jnp.bfloat16), "sp").astype(jnp.float32),
        lax.psum(owned[7].astype(jnp.bfloat16), "sp").astype(jnp.float32),
        lax.psum(owned[8].astype(jnp.bfloat16), "sp").astype(jnp.float32),
        lax.psum(owned[9].astype(jnp.bfloat16), "sp").astype(jnp.float32),
        lax.psum(owned[10].astype(jnp.bfloat16), "sp").astype(jnp.float32),
    )
    init_grads = unpack_state(init_total, head_width, inner_width)
    inner_sums = (
        lax.psum(init_grads[0].astype(jnp.bfloat16), "fsdp").astype(jnp.float32),
        lax.psum(init_grads[1].astype(jnp.bfloat16), "fsdp").astype(jnp.float32),
        lax.psum(init_grads[2].astype(jnp.bfloat16), "fsdp").astype(jnp.float32),
        lax.psum(init_grads[3].astype(jnp.bfloat16), "fsdp").astype(jnp.float32),
        lax.psum(gain_total.astype(jnp.bfloat16), "fsdp").astype(jnp.float32),
        lax.psum(shift_total.astype(jnp.bfloat16), "fsdp").astype(jnp.float32),
    )
    output_array = jnp.stack(outputs)[:, None]
    token_grad_array = jnp.stack(token_grads)[:, None]
    return (
        output_array,
        token_grad_array,
        owned[0],
        owned[1],
        owned[2],
        owned[3],
        owned[4],
        owned[5],
        owned[6],
        owned[7],
        owned[8],
        owned[9],
        owned[10],
        inner_sums[0],
        inner_sums[1],
        inner_sums[2],
        inner_sums[3],
        inner_sums[4],
        inner_sums[5],
    )


def solution(mesh):
    return jax.shard_map(
        shards,
        mesh=mesh,
        in_specs=(
            P(None, "fsdp", "sp", None),
            P(),
            P(None, "fsdp", "sp", None),
            P("fsdp"),
            P("fsdp", None),
            P("fsdp", None),
            P("fsdp", None),
            P("fsdp", None),
            P("fsdp", None),
            P("fsdp", None),
            P("fsdp"),
            P("fsdp", None),
            P("fsdp", None),
            P("fsdp", None),
            P("sp", None, None),
            P("sp", None),
            P("sp", None, None),
            P("sp", None),
            P("sp", None),
            P("sp", None),
        ),
        out_specs=(
            P(None, "fsdp", "sp", None),
            P(None, "fsdp", "sp", None),
            P("fsdp"),
            P("fsdp", None),
            P("fsdp", None),
            P("fsdp", None),
            P("fsdp", None),
            P("fsdp", None),
            P("fsdp", None),
            P("fsdp"),
            P("fsdp", None),
            P("fsdp", None),
            P("fsdp", None),
            P("sp", None, None),
            P("sp", None),
            P("sp", None, None),
            P("sp", None),
            P("sp", None),
            P("sp", None),
        ),
        check_vma=False,
    )
```

profile of v0, /device:TPU:0, one launch (start us, length us, event | category | flops | bytes accessed | tf_op | source)
XLA Modules:
  0.0 5798.5 jit_solution(13606911383818385668)
XLA Ops:
  200.8 568.8 %while.143 = (s32[]{:T(128)}, f32[3,33088]{1,0:T(4,128)S(1)}, bf16[4,256,3,64]{3,2,1,0:T(4,128)(2,1)}, f32[4,3,33088]{2,1,0:T(4,128)}, s32[]{:T(128)}, /*index=5...) while((s32[]{:T(128)}, f32[3,33088]{1,0:T(4,128)S(1)}, ...), condition=%wide.region_17.18_spmd, body=%wide.region_4.17_spmd.sunk | while | flops 73244008 | bytes 12668220 | solution.py:308
  203.6 69.9 %conditional.4 = ((f32[3,33088]{1,0:T(4,128)S(1)}, bf16[4,256,3,64]{3,2,1,0:T(4,128)(2,1)}, f32[4,3,33088]{2,1,0:T(4,128)})) conditional(s32[]{:T(128)} %convert_element_type.1386, (f32[3,33088]{1,0:T(4,128)S(1)}, bf16[4,256,3,64]{3,2,1,0:T(4,128)(2,1)}, f32[4,3,33088]{2,1,0:T(4,128)}) %tuple.339, (pred[]{:T(512)}, f32[3,33088]{1,0:T(4,128)S(1)}, ...), branch_computations={%region_5.5_spmd, %region_6.16_spmd} | conditional | flops 73244000 | bytes 10285529 | solution.py:304
  208.1 63.9 %while.140 = (s32[]{:T(128)}, f32[3,64,256]{2,1,0:T(8,128)S(1)}, f32[3,256]{1,0:T(4,128)S(1)}, f32[3,256,64]{1,2,0:T(8,128)S(1)}, f32[3,64]{1,0:T(4,128)S(1)}, /...) while((s32[]{:T(128)}, f32[3,64,256]{2,1,0:T(8,128)S(1)}, ...), condition=%wide.region_16.15_spmd.clone.clone, body=%wide.region_7.14_spmd.clone.clone.sunk | while | flops 72846944 | bytes 2866717 | solution.py:124
  276.5 70.0 %conditional.4 = ((f32[3,33088]{1,0:T(4,128)S(1)}, bf16[4,256,3,64]{3,2,1,0:T(4,128)(2,1)}, f32[4,3,33088]{2,1,0:T(4,128)})) conditional(s32[]{:T(128)} %convert_element_type.1386, (f32[3,33088]{1,0:T(4,128)S(1)}, bf16[4,256,3,64]{3,2,1,0:T(4,128)(2,1)}, f32[4,3,33088]{2,1,0:T(4,128)}) %tuple.339, (pred[]{:T(512)}, f32[3,33088]{1,0:T(4,128)S(1)}, ...), branch_computations={%region_5.5_spmd, %region_6.16_spmd} | conditional | flops 73244000 | bytes 10285529 | solution.py:304
  281.0 63.9 %while.140 = (s32[]{:T(128)}, f32[3,64,256]{2,1,0:T(8,128)S(1)}, f32[3,256]{1,0:T(4,128)S(1)}, f32[3,256,64]{1,2,0:T(8,128)S(1)}, f32[3,64]{1,0:T(4,128)S(1)}, /...) while((s32[]{:T(128)}, f32[3,64,256]{2,1,0:T(8,128)S(1)}, ...), condition=%wide.region_16.15_spmd.clone.clone, body=%wide.region_7.14_spmd.clone.clone.sunk | while | flops 72846944 | bytes 2866717 | solution.py:124
  350.4 70.0 %conditional.4 = ((f32[3,33088]{1,0:T(4,128)S(1)}, bf16[4,256,3,64]{3,2,1,0:T(4,128)(2,1)}, f32[4,3,33088]{2,1,0:T(4,128)})) conditional(s32[]{:T(128)} %convert_element_type.1386, (f32[3,33088]{1,0:T(4,128)S(1)}, bf16[4,256,3,64]{3,2,1,0:T(4,128)(2,1)}, f32[4,3,33088]{2,1,0:T(4,128)}) %tuple.339, (pred[]{:T(512)}, f32[3,33088]{1,0:T(4,128)S(1)}, ...), branch_computations={%region_5.5_spmd, %region_6.16_spmd} | conditional | flops 73244000 | bytes 10285529 | solution.py:304
  354.9 63.9 %while.140 = (s32[]{:T(128)}, f32[3,64,256]{2,1,0:T(8,128)S(1)}, f32[3,256]{1,0:T(4,128)S(1)}, f32[3,256,64]{1,2,0:T(8,128)S(1)}, f32[3,64]{1,0:T(4,128)S(1)}, /...) while((s32[]{:T(128)}, f32[3,64,256]{2,1,0:T(8,128)S(1)}, ...), condition=%wide.region_16.15_spmd.clone.clone, body=%wide.region_7.14_spmd.clone.clone.sunk | while | flops 72846944 | bytes 2866717 | solution.py:124
  428.6 70.0 %conditional.4 = ((f32[3,33088]{1,0:T(4,128)S(1)}, bf16[4,256,3,64]{3,2,1,0:T(4,128)(2,1)}, f32[4,3,33088]{2,1,0:T(4,128)})) conditional(s32[]{:T(128)} %convert_element_type.1386, (f32[3,33088]{1,0:T(4,128)S(1)}, bf16[4,256,3,64]{3,2,1,0:T(4,128)(2,1)}, f32[4,3,33088]{2,1,0:T(4,128)}) %tuple.339, (pred[]{:T(512)}, f32[3,33088]{1,0:T(4,128)S(1)}, ...), branch_computations={%region_5.5_spmd, %region_6.16_spmd} | conditional | flops 73244000 | bytes 10285529 | solution.py:304
  433.1 63.9 %while.140 = (s32[]{:T(128)}, f32[3,64,256]{2,1,0:T(8,128)S(1)}, f32[3,256]{1,0:T(4,128)S(1)}, f32[3,256,64]{1,2,0:T(8,128)S(1)}, f32[3,64]{1,0:T(4,128)S(1)}, /...) while((s32[]{:T(128)}, f32[3,64,256]{2,1,0:T(8,128)S(1)}, ...), condition=%wide.region_16.15_spmd.clone.clone, body=%wide.region_7.14_spmd.clone.clone.sunk | while | flops 72846944 | bytes 2866717 | solution.py:124
  509.3 79.0 %collective-permute-start.1 = (f32[3,33088]{1,0:T(4,128)S(1)}, f32[3,33088]{1,0:T(4,128)S(1)}, u32[]{:S(2)}, u32[]{:S(2)}) collective-permute-start(f32[3,33088]{1,0:T(4,128)S(1)} %get-tuple-element.3603), channel_id=1, source_target_pairs={{0,1},{1,2},{2,3},{3,4},{4,5},{5,6},{6,7},{8,9},{9,10},{10,11},{11... | collective-permute-start | bytes 1191176 | tf_op jit(solution)/shard_map/while/body/eval_jaxpr/ppermute | solution.py:19
  600.7 79.1 %collective-permute-start.1 = (f32[3,33088]{1,0:T(4,128)S(1)}, f32[3,33088]{1,0:T(4,128)S(1)}, u32[]{:S(2)}, u32[]{:S(2)}) collective-permute-start(f32[3,33088]{1,0:T(4,128)S(1)} %get-tuple-element.3603), channel_id=1, source_target_pairs={{0,1},{1,2},{2,3},{3,4},{4,5},{5,6},{6,7},{8,9},{9,10},{10,11},{11... | collective-permute-start | bytes 1191176 | tf_op jit(solution)/shard_map/while/body/eval_jaxpr/ppermute | solution.py:19
  692.0 65.2 %collective-permute-start.1 = (f32[3,33088]{1,0:T(4,128)S(1)}, f32[3,33088]{1,0:T(4,128)S(1)}, u32[]{:S(2)}, u32[]{:S(2)}) collective-permute-start(f32[3,33088]{1,0:T(4,128)S(1)} %get-tuple-element.3603), channel_id=1, source_target_pairs={{0,1},{1,2},{2,3},{3,4},{4,5},{5,6},{6,7},{8,9},{9,10},{10,11},{11... | collective-permute-start | bytes 1191176 | tf_op jit(solution)/shard_map/while/body/eval_jaxpr/ppermute | solution.py:19
  912.7 4300.2 %while.144 = (s32[]{:T(128)}, f32[3,33088]{1,0:T(4,128)}, bf16[4,256,3,64]{3,2,1,0:T(4,128)(2,1)}, bf16[4,256,3,64]{3,2,1,0:T(4,128)(2,1)}, bf16[4,256,3,64]{3,2...) while((s32[]{:T(128)}, f32[3,33088]{1,0:T(4,128)}, ...), condition=%wide.region_63.64_spmd, body=%wide.region_26.63_spmd.sunk | while | flops 248695952 | bytes 26357412 | solution.py:462
  915.5 71.8 %collective-permute-done = bf16[3,33088]{1,0:T(4,128)(2,1)S(1)} collective-permute-done((bf16[3,33088]{1,0:T(4,128)(2,1)S(1)}, bf16[3,33088]{1,0:T(4,128)(2,1)S(1)}, u32[]{:S(2)}, u32[]{:S(2)}) %collective-permute-start) | collective-permute-done | bytes 198560 | tf_op jit(solution)/shard_map/while/body/eval_jaxpr/ppermute | solution.py:19
  1009.7 56.3 collective-permute-done
  1088.4 67.7 %collective-permute-done = bf16[3,33088]{1,0:T(4,128)(2,1)S(1)} collective-permute-done((bf16[3,33088]{1,0:T(4,128)(2,1)S(1)}, bf16[3,33088]{1,0:T(4,128)(2,1)S(1)}, u32[]{:S(2)}, u32[]{:S(2)}) %collective-permute-start) | collective-permute-done | bytes 198560 | tf_op jit(solution)/shard_map/while/body/eval_jaxpr/ppermute | solution.py:19
  1177.6 56.6 collective-permute-done
  1237.4 2509.4 %collective-permute-done = bf16[3,33088]{1,0:T(4,128)(2,1)S(1)} collective-permute-done((bf16[3,33088]{1,0:T(4,128)(2,1)S(1)}, bf16[3,33088]{1,0:T(4,128)(2,1)S(1)}, u32[]{:S(2)}, u32[]{:S(2)}) %collective-permute-start) | collective-permute-done | bytes 198560 | tf_op jit(solution)/shard_map/while/body/eval_jaxpr/ppermute | solution.py:19
  3747.7 358.3 %conditional.5 = ((f32[3,33088]{1,0:T(4,128)}, bf16[4,256,3,64]{3,2,1,0:T(4,128)(2,1)}, bf16[4,256,3,64]{3,2,1,0:T(4,128)(2,1)}, bf16[4,256,3,64]{3,2,1,0:T(4,12...) conditional(s32[]{:T(128)} %convert_element_type.1387, ...), branch_computations={%region_27.27_spmd, %region_28.62_spmd} | conditional | flops 248497424 | bytes 24371640 | solution.py:450
  3755.3 77.3 %while.141 = (s32[]{:T(128)}, f32[3,64,256]{2,1,0:T(8,128)S(1)}, f32[3,256]{1,0:T(4,128)S(1)}, f32[3,256,64]{1,2,0:T(8,128)S(1)}, f32[3,64]{1,0:T(4,128)S(1)}, /...) while((s32[]{:T(128)}, f32[3,64,256]{2,1,0:T(8,128)S(1)}, ...), condition=%wide.region_36.35_spmd, body=%wide.region_29.34_spmd.sunk | while | flops 47812656 | bytes 2678453 | solution.py:124
  3837.5 258.7 %while.142 = (s32[]{:T(128)}, f32[3,64]{1,0:T(4,128)S(1)}, f32[3,64]{1,0:T(4,128)S(1)}, f32[3,64,256]{2,1,0:T(8,128)S(1)}, f32[3,256]{1,0:T(4,128)S(1)}, /*index...) while((s32[]{:T(128)}, f32[3,64]{1,0:T(4,128)S(1)}, ...), condition=%wide.region_62.61_spmd.clone, body=%wide.region_37.60_spmd.clone.sunk | while | flops 200485856 | bytes 8887464 | solution.py:124
  4116.7 358.3 %conditional.5 = ((f32[3,33088]{1,0:T(4,128)}, bf16[4,256,3,64]{3,2,1,0:T(4,128)(2,1)}, bf16[4,256,3,64]{3,2,1,0:T(4,128)(2,1)}, bf16[4,256,3,64]{3,2,1,0:T(4,12...) conditional(s32[]{:T(128)} %convert_element_type.1387, ...), branch_computations={%region_27.27_spmd, %region_28.62_spmd} | conditional | flops 248497424 | bytes 24371640 | solution.py:450
  4124.4 77.3 %while.141 = (s32[]{:T(128)}, f32[3,64,256]{2,1,0:T(8,128)S(1)}, f32[3,256]{1,0:T(4,128)S(1)}, f32[3,256,64]{1,2,0:T(8,128)S(1)}, f32[3,64]{1,0:T(4,128)S(1)}, /...) while((s32[]{:T(128)}, f32[3,64,256]{2,1,0:T(8,128)S(1)}, ...), condition=%wide.region_36.35_spmd, body=%wide.region_29.34_spmd.sunk | while | flops 47812656 | bytes 2678453 | solution.py:124
  4206.6 258.7 %while.142 = (s32[]{:T(128)}, f32[3,64]{1,0:T(4,128)S(1)}, f32[3,64]{1,0:T(4,128)S(1)}, f32[3,64,256]{2,1,0:T(8,128)S(1)}, f32[3,256]{1,0:T(4,128)S(1)}, /*index...) while((s32[]{:T(128)}, f32[3,64]{1,0:T(4,128)S(1)}, ...), condition=%wide.region_62.61_spmd.clone, body=%wide.region_37.60_spmd.clone.sunk | while | flops 200485856 | bytes 8887464 | solution.py:124
  4485.6 358.3 %conditional.5 = ((f32[3,33088]{1,0:T(4,128)}, bf16[4,256,3,64]{3,2,1,0:T(4,128)(2,1)}, bf16[4,256,3,64]{3,2,1,0:T(4,128)(2,1)}, bf16[4,256,3,64]{3,2,1,0:T(4,12...) conditional(s32[]{:T(128)} %convert_element_type.1387, ...), branch_computations={%region_27.27_spmd, %region_28.62_spmd} | conditional | flops 248497424 | bytes 24371640 | solution.py:450
  4493.2 77.3 %while.141 = (s32[]{:T(128)}, f32[3,64,256]{2,1,0:T(8,128)S(1)}, f32[3,256]{1,0:T(4,128)S(1)}, f32[3,256,64]{1,2,0:T(8,128)S(1)}, f32[3,64]{1,0:T(4,128)S(1)}, /...) while((s32[]{:T(128)}, f32[3,64,256]{2,1,0:T(8,128)S(1)}, ...), condition=%wide.region_36.35_spmd, body=%wide.region_29.34_spmd.sunk | while | flops 47812656 | bytes 2678453 | solution.py:124
  4575.4 258.7 %while.142 = (s32[]{:T(128)}, f32[3,64]{1,0:T(4,128)S(1)}, f32[3,64]{1,0:T(4,128)S(1)}, f32[3,64,256]{2,1,0:T(8,128)S(1)}, f32[3,256]{1,0:T(4,128)S(1)}, /*index...) while((s32[]{:T(128)}, f32[3,64]{1,0:T(4,128)S(1)}, ...), condition=%wide.region_62.61_spmd.clone, body=%wide.region_37.60_spmd.clone.sunk | while | flops 200485856 | bytes 8887464 | solution.py:124
  4854.6 358.3 %conditional.5 = ((f32[3,33088]{1,0:T(4,128)}, bf16[4,256,3,64]{3,2,1,0:T(4,128)(2,1)}, bf16[4,256,3,64]{3,2,1,0:T(4,128)(2,1)}, bf16[4,256,3,64]{3,2,1,0:T(4,12...) conditional(s32[]{:T(128)} %convert_element_type.1387, ...), branch_computations={%region_27.27_spmd, %region_28.62_spmd} | conditional | flops 248497424 | bytes 24371640 | solution.py:450
  4862.2 77.3 %while.141 = (s32[]{:T(128)}, f32[3,64,256]{2,1,0:T(8,128)S(1)}, f32[3,256]{1,0:T(4,128)S(1)}, f32[3,256,64]{1,2,0:T(8,128)S(1)}, f32[3,64]{1,0:T(4,128)S(1)}, /...) while((s32[]{:T(128)}, f32[3,64,256]{2,1,0:T(8,128)S(1)}, ...), condition=%wide.region_36.35_spmd, body=%wide.region_29.34_spmd.sunk | while | flops 47812656 | bytes 2678453 | solution.py:124
  4944.4 258.7 %while.142 = (s32[]{:T(128)}, f32[3,64]{1,0:T(4,128)S(1)}, f32[3,64]{1,0:T(4,128)S(1)}, f32[3,64,256]{2,1,0:T(8,128)S(1)}, f32[3,256]{1,0:T(4,128)S(1)}, /*index...) while((s32[]{:T(128)}, f32[3,64]{1,0:T(4,128)S(1)}, ...), condition=%wide.region_62.61_spmd.clone, body=%wide.region_37.60_spmd.clone.sunk | while | flops 200485856 | bytes 8887464 | solution.py:124
  5594.1 49.9 reduce-scatter.24.cloned.1.call-done
  5725.8 54.9 all-reduce.14.cloned.1.call-done
  (8577 shorter events, 2656.9 us)
Async XLA Ops:
  7.2 73.0 %all-gather.12.cloned.1.call-start = ((), (), s32[]{:S(2)}) async-start(), calls=%async_computation.50 | async-start | bytes 1327104 | tf_op jit(solution)/shard_map/all_gather | solution.py:177
  8.0 106.0 %all-gather.14.cloned.1.call-start = ((), (), s32[]{:S(2)}) async-start(), calls=%async_computation.51 | async-start | bytes 1327104 | tf_op jit(solution)/shard_map/all_gather | solution.py:178
  8.7 142.6 %all-gather.16.cloned.1.call-start = ((), (), s32[]{:S(2)}) async-start(), calls=%async_computation.52 | async-start | bytes 1327104 | tf_op jit(solution)/shard_map/all_gather | solution.py:179
  9.4 806.8 %all-gather.10.cloned.1.call-start = ((), (), s32[]{:S(2)}) async-start(), calls=%async_computation.49 | async-start | bytes 1327104 | tf_op jit(solution)/shard_map/all_gather | solution.py:180
  10.0 808.7 %all-gather.18.cloned.1.call-start = ((), (), s32[]{:S(2)}) async-start(), calls=%async_computation.53 | async-start | bytes 1327104 | tf_op jit(solution)/shard_map/all_gather | solution.py:187
  10.6 818.3 %all-gather.20.cloned.1.call-start = ((), (), s32[]{:S(2)}) async-start(), calls=%async_computation.54 | async-start | bytes 3538944 | tf_op jit(solution)/shard_map/all_gather | solution.py:189
  11.2 821.1 %all-gather.22.cloned.1.call-start = ((), (), s32[]{:S(2)}) async-start(), calls=%async_computation.55 | async-start | bytes 3538944 | tf_op jit(solution)/shard_map/all_gather | solution.py:190
  47.4 788.2 %all-gather.24.cloned.1.call-start = ((), (), s32[]{:S(2)}) async-start(), calls=%async_computation.56 | async-start | bytes 3538944 | tf_op jit(solution)/shard_map/all_gather | solution.py:191
  509.3 80.5 %collective-permute-start.1 = (f32[3,33088]{1,0:T(4,128)S(1)}, f32[3,33088]{1,0:T(4,128)S(1)}, u32[]{:S(2)}, u32[]{:S(2)}) collective-permute-start(f32[3,33088]{1,0:T(4,128)S(1)} %get-tuple-element.3603), channel_id=1, source_target_pairs={{0,1},{1,2},{2,3},{3,4},{4,5},{5,6},{6,7},{8,9},{9,10},{10,11},{11... | collective-permute-start | bytes 1191176 | tf_op jit(solution)/shard_map/while/body/eval_jaxpr/ppermute | solution.py:19
  600.7 80.6 %collective-permute-start.1 = (f32[3,33088]{1,0:T(4,128)S(1)}, f32[3,33088]{1,0:T(4,128)S(1)}, u32[]{:S(2)}, u32[]{:S(2)}) collective-permute-start(f32[3,33088]{1,0:T(4,128)S(1)} %get-tuple-element.3603), channel_id=1, source_target_pairs={{0,1},{1,2},{2,3},{3,4},{4,5},{5,6},{6,7},{8,9},{9,10},{10,11},{11... | collective-permute-start | bytes 1191176 | tf_op jit(solution)/shard_map/while/body/eval_jaxpr/ppermute | solution.py:19
  692.0 66.7 %collective-permute-start.1 = (f32[3,33088]{1,0:T(4,128)S(1)}, f32[3,33088]{1,0:T(4,128)S(1)}, u32[]{:S(2)}, u32[]{:S(2)}) collective-permute-start(f32[3,33088]{1,0:T(4,128)S(1)} %get-tuple-element.3603), channel_id=1, source_target_pairs={{0,1},{1,2},{2,3},{3,4},{4,5},{5,6},{6,7},{8,9},{9,10},{10,11},{11... | collective-permute-start | bytes 1191176 | tf_op jit(solution)/shard_map/while/body/eval_jaxpr/ppermute | solution.py:19
  772.0 11.1 all-to-all-start.19
  802.9 12.7 all-to-all-start.18
  914.2 73.1 %collective-permute-start = (bf16[3,33088]{1,0:T(4,128)(2,1)S(1)}, bf16[3,33088]{1,0:T(4,128)(2,1)S(1)}, u32[]{:S(2)}, u32[]{:S(2)}) collective-permute-start(bf16[3,33088]{1,0:T(4,128)(2,1)S(1)} %convert_element_type.1388), channel_id=1, source_target_pairs={{1,0},{2,1},{3,2},{4,3},{5,4},{6,5},{7,6},{9,8},{10,9},{11,10},{12... | collective-permute-start | bytes 595592 | tf_op jit(solution)/shard_map/while/body/eval_jaxpr/ppermute | solution.py:19
  989.4 17.1 collective-permute-start
  1008.4 57.6 collective-permute-start
  1068.0 17.1 collective-permute-start
  1087.1 69.0 %collective-permute-start = (bf16[3,33088]{1,0:T(4,128)(2,1)S(1)}, bf16[3,33088]{1,0:T(4,128)(2,1)S(1)}, u32[]{:S(2)}, u32[]{:S(2)}) collective-permute-start(bf16[3,33088]{1,0:T(4,128)(2,1)S(1)} %convert_element_type.1388), channel_id=1, source_target_pairs={{1,0},{2,1},{3,2},{4,3},{5,4},{6,5},{7,6},{9,8},{10,9},{11,10},{12... | collective-permute-start | bytes 595592 | tf_op jit(solution)/shard_map/while/body/eval_jaxpr/ppermute | solution.py:19
  1158.1 16.2 collective-permute-start
  1176.3 57.9 collective-permute-start
  1236.1 2510.7 %collective-permute-start = (bf16[3,33088]{1,0:T(4,128)(2,1)S(1)}, bf16[3,33088]{1,0:T(4,128)(2,1)S(1)}, u32[]{:S(2)}, u32[]{:S(2)}) collective-permute-start(bf16[3,33088]{1,0:T(4,128)(2,1)S(1)} %convert_element_type.1388), channel_id=1, source_target_pairs={{1,0},{2,1},{3,2},{4,3},{5,4},{6,5},{7,6},{9,8},{10,9},{11,10},{12... | collective-permute-start | bytes 595592 | tf_op jit(solution)/shard_map/while/body/eval_jaxpr/ppermute | solution.py:19
  5247.6 175.9 %reduce-scatter.28.cloned.1.call-start = ((), (), s32[]{:S(2)}) async-start(), calls=%async_computation.65 | async-start | bytes 221184
  5256.2 168.7 %all-reduce.12.cloned.1.call-start = ((), (), s32[]{:S(2)}) async-start(), calls=%async_computation.66 | async-start | bytes 589824 | tf_op jit(solution)/shard_map/psum | solution.py:590
  5257.9 183.5 %reduce-scatter.18.cloned.1.call-start = ((), (), s32[]{:S(2)}) async-start(), calls=%async_computation.60 | async-start | bytes 1327104 | tf_op jit(solution)/shard_map/reduce_scatter | solution.py:551
  5282.8 158.6 %reduce-scatter.20.cloned.1.call-start = ((), (), s32[]{:S(2)}) async-start(), calls=%async_computation.61 | async-start | bytes 1327104 | tf_op jit(solution)/shard_map/reduce_scatter | solution.py:557
  5325.8 138.7 %reduce-scatter.12.cloned.1.call-start = ((), (), s32[]{:S(2)}) async-start(), calls=%async_computation.57 | async-start | bytes 1327104 | tf_op jit(solution)/shard_map/reduce_scatter | solution.py:542
  5354.8 149.6 %reduce-scatter.14.cloned.1.call-start = ((), (), s32[]{:S(2)}) async-start(), calls=%async_computation.58 | async-start | bytes 1327104 | tf_op jit(solution)/shard_map/reduce_scatter | solution.py:545
  5383.0 161.6 %reduce-scatter.16.cloned.1.call-start = ((), (), s32[]{:S(2)}) async-start(), calls=%async_computation.59 | async-start | bytes 1327104 | tf_op jit(solution)/shard_map/reduce_scatter | solution.py:548
  5392.7 201.4 %reduce-scatter.22.cloned.1.call-start = ((), (), s32[]{:S(2)}) async-start(), calls=%async_computation.62 | async-start | bytes 3538944 | tf_op jit(solution)/shard_map/reduce_scatter | solution.py:563
  5398.7 245.3 %reduce-scatter.24.cloned.1.call-start = ((), (), s32[]{:S(2)}) async-start(), calls=%async_computation.63 | async-start | bytes 3538944 | tf_op jit(solution)/shard_map/reduce_scatter | solution.py:566
  5405.3 288.2 %reduce-scatter.26.cloned.1.call-start = ((), (), s32[]{:S(2)}) async-start(), calls=%async_computation.64 | async-start | bytes 3538944 | tf_op jit(solution)/shard_map/reduce_scatter | solution.py:569
  5412.4 368.3 %all-reduce.14.cloned.1.call-start = ((), (), s32[]{:S(2)}) async-start(), calls=%async_computation.67 | async-start | bytes 3833856 | tf_op jit(solution)/shard_map/psum | solution.py:575
  (268 other events, 8485.7 us)
Sparse Core Ops, SparseCore 0:
  9.9 26.8 all-gather.11
  38.7 24.0 all-gather.13
  64.7 24.0 all-gather.15
  90.6 24.0 all-gather.9
  116.4 24.0 all-gather.17
  142.3 32.3 all-gather.19
  176.5 32.5 all-gather.21
  211.0 38.6 all-gather.23
  5256.3 30.7 reduce-scatter.27
  5290.5 53.2 all-reduce.11
  5347.3 36.9 reduce-scatter.17
  5387.4 36.7 reduce-scatter.19
  5427.7 36.7 reduce-scatter.11
  5467.6 36.7 reduce-scatter.13
  5507.8 36.7 reduce-scatter.15
  5547.8 46.2 reduce-scatter.21
  5597.7 46.2 reduce-scatter.23
  5647.2 46.2 reduce-scatter.25
  5696.7 83.9 all-reduce.13
where the time goes:
time: 5830 us; the launch traced here: 5800 us
  waiting for transfers between devices  3280 us (56%)
  matrix products  1010 us (17%)
  local copies, waits for them, and re-layouts  620 us (11%)
  starting transfers between devices  446 us (8%)
  other arithmetic  341 us (6%)
    ppermute x22, waiting for transfers between devices, from_behind(): return lax.ppermute(block, axis, route)  2850 us
    dot_general x3008, matrix products, einsum_high(): return jnp.einsum(formula, left, right, precision=lax.Precision.HIGHEST)  880 us
    ppermute x22, starting transfers between devices, from_behind(): return lax.ppermute(block, axis, route)  285 us
    squeeze x448, local copies, waits for them, and re-layouts, piece_mixer(): lax.scan(jax.checkpoint(advance), inner_state, (arrange(query_heads), arr...  258 us
    dynamic_update_slice x256, local copies, waits for them, and re-layouts, piece_mixer(): lax.scan(jax.checkpoint(advance), inner_state, (arrange(query_heads), arr...  164 us

commit v1 on v0

v1 whole, which is shorter than its diff:
```python
import functools

import jax
import jax.numpy as jnp
from jax import lax
from jax.experimental import pallas as pl
from jax.experimental.pallas import tpu as pltpu
from jax.sharding import PartitionSpec as P

MINI = 16
EPS = 1e-06
RATE = 1.0 / 1024.0
GELU_C = 0.7978845608028654
GELU_K = 0.044715
VMEM_BYTES = 56 * 1024 * 1024
f32 = jnp.float32
bf16 = jnp.bfloat16

def nn(x,y): return lax.dot_general(x.astype(bf16),y.astype(bf16),(((1,),(0,)),((),())),preferred_element_type=f32)
def nt(x,y): return lax.dot_general(x.astype(bf16),y.astype(bf16),(((1,),(1,)),((),())),preferred_element_type=f32)
def tn(x,y): return lax.dot_general(x.astype(bf16),y.astype(bf16),(((0,),(0,)),((),())),preferred_element_type=f32)
def gelu1(z):
    t=jnp.tanh(GELU_C*z*(1.0+GELU_K*(z*z)))
    return 0.5*z*(1.0+t)
def gelu2(z):
    z2=z*z
    t=jnp.tanh(z*(GELU_C+(GELU_C*GELU_K)*z2))
    h=0.5+0.5*t
    return z*h, h+0.5*z*(1.0-t*t)*(GELU_C+(3.0*GELU_C*GELU_K)*z2)
def gelu3(z):
    z2=z*z
    t=jnp.tanh(z*(GELU_C+(GELU_C*GELU_K)*z2))
    h=0.5+0.5*t
    u=GELU_C+(3.0*GELU_C*GELU_K)*z2
    c=1.0-t*t
    return z*h, h+0.5*z*c*u, c*(u+z*((3.0*GELU_C*GELU_K)*z-t*u*u))

def cat(*xs): return jnp.concatenate(xs,0)
def rs(x): return jnp.sum(x,-1,keepdims=True)*(1.0/64)

def interleave(gens):
    gens=list(gens)
    while gens:
        alive=[]
        for g in gens:
            try:
                next(g); alive.append(g)
            except StopIteration: pass
        gens=alive

def masks():
    lower=lax.broadcasted_iota(jnp.int32,(MINI,MINI),0)>=lax.broadcasted_iota(jnp.int32,(MINI,MINI),1)
    return lower.astype(f32), jnp.where(lower,0.0,1.0)

def fwd_kernel(slots,count,unroll,q_ref,k_ref,v_ref,e_ref,w1_ref,b1_ref,w2_ref,b2_ref,gain_ref,shift_ref,
    mix_ref,w1s_ref,w2s_ref,z1_ref,h_ref,q1_ref,n_ref,g_ref,nq_ref,s_ref,sq_ref,
    W1,B1,W2,B2,Z,ZQ,AP,EP):
    lower,upper=masks()
    steps=q_ref.shape[1]//MINI
    pid=pl.program_id(0)
    @pl.when(pid==0)
    def _():
        for j in range(slots):
            W1[j]=w1_ref[j]; B1[j]=b1_ref[j]; W2[j]=w2_ref[j]; B2[j]=b2_ref[j]
            Z[j]=nn(k_ref[j,:MINI],w1_ref[j])+b1_ref[j]
            ZQ[j]=jnp.zeros((MINI,256),f32); AP[j]=jnp.zeros((MINI,256),bf16); EP[j]=jnp.zeros((MINI,64),bf16)
    def chain(j,i):
        t=pid*count+i
        rows=pl.ds(pl.multiple_of(t*MINI,MINI),MINI)
        prow=pl.ds(pl.multiple_of(jnp.maximum(t-1,0)*MINI,MINI),MINI)
        nrow=pl.ds(pl.multiple_of(jnp.minimum(t+1,steps-1)*MINI,MINI),MINI)
        brow=pl.ds(pl.multiple_of(i*MINI,MINI),MINI)
        gain=gain_ref[j]; shift=shift_ref[j]; g2=gain*gain; mg=rs(g2)
        z1=Z[j]; q1=ZQ[j]; w2=W2[j]; b2=B2[j]
        w2b=w2.astype(bf16)
        Ap=AP[j]; Ep=EP[j]
        A,Ad=gelu2(z1); AQ=gelu1(q1)
        Ab=A.astype(bf16); AQb=AQ.astype(bf16)
        z1_ref[j,brow]=z1.astype(bf16)
        yield
        zz=nt(cat(Ab,AQb),w2b)
        z=zz[:MINI]+b2; qb=zz[MINI:]+b2
        yield
        P2=upper*(nt(AQb,Ap)+1.0)
        K=k_ref[j,rows]; Q=q_ref[j,rows]; Kn=k_ref[j,nrow]
        w1=W1[j]; w1b=w1.astype(bf16); b1=B1[j]
        w1s_ref[j,i]=w1b; w2s_ref[j,i]=w2b
        KQ=cat(Kn,Q)
        KK=nt(KQ,K)+1.0
        L=cat(KK[:MINI].astype(bf16),(lower*KK[MINI:]).astype(bf16),K.T)
        base=nn(KQ,w1b)+b1
        U=gain*(shift-v_ref[j,rows].astype(f32)+K.astype(f32)); mU=rs(U)
        e=e_ref[j,rows]
        yield
        Q2=qb+nn(P2,Ep)
        yield
        zg=z*g2
        mz=rs(z); p0=rs(z*z); p1=rs(zg); p2=rs(z*zg); p3=rs(z*U)
        s=lax.rsqrt(p0-mz*mz+EPS)
        m1=s*(p1-mz*mg)+mU
        m2=s*(s*(p2-2.0*mz*p1+mz*mz*mg)+(p3-mz*mU))
        N=s*(z-mz)
        G=s*(N*(g2-m2)+(U-m1))
        Gb=G.astype(bf16)
        yield
        H=nn(Gb,w2b)
        E2=e*G; E2b=E2.astype(bf16)
        n_ref[j,rows]=N; g_ref[j,rows]=G; s_ref[j,rows]=s
        EP[j]=E2b; AP[j]=Ab
        yield
        W2[j]=w2-tn(E2b,Ab)
        B2[j]=b2-jnp.sum(E2,0,keepdims=True)
        yield
        E1=(e*Ad)*H; E1b=E1.astype(bf16)
        X=nn(L,E1b)
        Z[j]=base[:MINI]-X[:MINI]
        Q1=base[MINI:]-X[MINI:2*MINI]
        ZQ[j]=Q1
        W1[j]=w1-X[2*MINI:]
        B1[j]=b1-jnp.sum(E1,0,keepdims=True)
        h_ref[j,brow]=H.astype(bf16); q1_ref[j,brow]=Q1.astype(bf16)
        yield
        mq=rs(Q2); vq=rs(Q2*Q2)
        sq=lax.rsqrt(vq-mq*mq+EPS)
        Nq=sq*(Q2-mq)
        Qp=q_ref[j,prow].astype(f32)
        mix_ref[j,prow]=(Qp+Nq*gain+shift).astype(bf16)
        nq_ref[j,prow]=Nq; sq_ref[j,prow]=sq
    @pl.loop(0,count//unroll)
    def _(i):
        for u in range(unroll):
            interleave(chain(j,i*unroll+u) for j in range(slots))
    @pl.when(pid==pl.num_programs(0)-1)
    def _():
        for j in range(slots):
            prow=pl.ds((steps-1)*MINI,MINI)
            AQb=gelu1(ZQ[j]).astype(bf16)
            Q2=nt(AQb,W2[j])+B2[j]+nn(upper*(nt(AQb,AP[j])+1.0),EP[j])
            mq=rs(Q2); vq=rs(Q2*Q2)
            sq=lax.rsqrt(vq-mq*mq+EPS)
            Nq=sq*(Q2-mq)
            mix_ref[j,prow]=(q_ref[j,prow].astype(f32)+Nq*gain_ref[j]+shift_ref[j]).astype(bf16)
            nq_ref[j,prow]=Nq; sq_ref[j,prow]=sq

def fwd_call(q,k,v,e,w1,b1,w2,b2,gain,shift,block=256,unroll=1,**kw):
    slots,length,_=q.shape
    count=block//MINI; nb=length//block; steps=length//MINI
    row=lambda w: pl.BlockSpec((slots,block,w),lambda i:(0,i,0))
    full=lambda s: pl.BlockSpec(s,lambda i:(0,)*len(s),pipeline_mode=pl.Buffered(1))
    r64=full((slots,length,64)); r1=full((slots,length,1))
    st=pl.BlockSpec((slots,count,64,256),lambda i:(0,i,0,0))
    S=jax.ShapeDtypeStruct
    return pl.pallas_call(functools.partial(fwd_kernel,slots,count,unroll),
        grid=(nb,),
        in_specs=[r64]*3+[r1]+[full(a.shape) for a in (w1,b1,w2,b2,gain,shift)],
        out_specs=[r64,st,st,row(256),row(256),row(256),r64,r64,r64,r1,r1],
        out_shape=[S((slots,length,64),bf16),S((slots,steps,64,256),bf16),S((slots,steps,64,256),bf16)]+[S((slots,length,256),bf16)]*3+[S((slots,length,64),f32)]*3+[S((slots,length,1),f32)]*2,
        scratch_shapes=[pltpu.VMEM((slots,64,256),f32),pltpu.VMEM((slots,1,256),f32),pltpu.VMEM((slots,64,256),f32),pltpu.VMEM((slots,1,64),f32),pltpu.VMEM((slots,MINI,256),f32),pltpu.VMEM((slots,MINI,256),f32),pltpu.VMEM((slots,MINI,256),bf16),pltpu.VMEM((slots,MINI,64),bf16)],
        compiler_params=pltpu.CompilerParams(dimension_semantics=("arbitrary",),vmem_limit_bytes=VMEM_BYTES),
        name="inner_forward",**kw)(q,k,v,e,w1,b1,w2,b2,gain,shift)


def bwd_kernel(slots,count,unroll,q_ref,k_ref,v_ref,e_ref,do_ref,n_ref,g_ref,nq_ref,s_ref,sq_ref,w1s_ref,w2s_ref,z1_ref,h_ref,q1_ref,gain_ref,shift_ref,
    dq_ref,dk_ref,dv_ref,de_ref,dw1_ref,db1_ref,dw2_ref,db2_ref,dgn_ref,dsh_ref,
    DW1,DB1,G2,DB2,KD,DGN,DSH,DGQ,DSQ,
    sA,sAd,sHA,sGZ,sE1,sE2,sW1,sW2,sR1,sR2,sDA,sQ1,sQ2,sAQ,sb1,sb2):
    lower,_=masks()
    steps=q_ref.shape[1]//MINI
    pid=pl.program_id(0); nb=pl.num_programs(0)
    @pl.when(pid==0)
    def _():
        for r in (DW1,DB1,G2,DB2,KD,DGN,DSH,DGQ,DSQ):
            r[...]=jnp.zeros(r.shape,r.dtype)
        for r in (sA,sAd,sHA,sGZ,sE1,sE2,sW1,sW2,sR1,sR2,sDA,sQ1,sQ2,sAQ,sb1,sb2):
            r[0]=jnp.zeros(r.shape[1:],r.dtype)
    def crit(j,p,t):
        rows=pl.ds(pl.multiple_of(jnp.minimum(t,steps-1)*MINI,MINI),MINI)
        prow=pl.ds(pl.multiple_of(jnp.maximum(t-1,0)*MINI,MINI),MINI)
        gain=gain_ref[j]; shift=shift_ref[j]; g2=gain*gain; mg=rs(g2)
        e=e_ref[j,rows]
        nE1=sR1[p,j]+KD[j]
        dgZ1=(-e)*nE1
        dH=dgZ1*sAd[p,j]
        dHb=dH.astype(bf16)
        w2b=sW2[p,j]
        G2f=G2[j]; G2b=G2f.astype(bf16)
        Ab=sA[p,j]; E2b=sE2[p,j]
        yield
        a1=nt(Ab,G2b)
        yP=nt(dHb,w2b)
        yield
        N=n_ref[j,rows]; G=g_ref[j,rows]; s=s_ref[j,rows]
        K=k_ref[j,rows]; Q=q_ref[j,rows]; Kp=k_ref[j,prow]
        T=shift-v_ref[j,rows].astype(f32)+K.astype(f32)
        U=gain*T
        gN=N*g2
        c1=rs(gN); c2=rs(gN*N); mU=rs(U); UN=rs(U*N)
        a=gN+U; ma=c1+mU; m2=c2+UN
        a2=nn(E2b,G2b)
        E1b=sE1[p,j]; dQ1b=sQ1[p,j]
        DW=DW1[j]; DWb=DW.astype(bf16)
        KDb=nn(Kp,DWb)+DB1[j]
        yield
        a3=nt(E1b,DWb)
        X1=(lower*nt(dQ1b,E1b)).astype(bf16)
        L2=cat((nt(Kp,cat(Q,K))+1.0).astype(bf16),cat(Q,K).T)
        yield
        nE2=sR2[p,j]+a1+DB2[j]
        y=yP-e*nE2
        yg=y*g2; yn=y*N
        ym=rs(y); yN=rs(yn); yG=rs(y*G); ygm=rs(yg); ygN=rs(yg*N)
        mdy=s*ym; mdyN=s*yN
        da=s*y-mdy-N*mdyN
        sN=s*ygN-mdy*c1-mdyN*c2-2.0*m2*mdyN
        mN=s*ygm-mdy*mg-mdyN*c1-ma*mdyN-m2*mdy
        kap=yG+sN
        dN=da*g2-a*mdyN-(s*m2)*y
        dZc=s*(dN-mN-N*kap)
        dZb=dZc.astype(bf16)
        dT=da*gain
        yield
        dA=nn(dZb,w2b)+sDA[p,j]-a2
        yield
        G2[j]=G2f+tn(cat(sQ2[p,j],G.astype(bf16),dZb),cat(sAQ[p,j],dHb,Ab))
        DB2[j]=DB2[j]+sb2[p,j]+jnp.sum(dZc,0,keepdims=True)
        dQs=nn(X1,K); dKs=tn(X1,Q)
        dv_ref[j,rows]=(-dT).astype(bf16)
        dO=do_ref[j,rows].astype(f32)
        DGN[j]=DGN[j]+da*(2.0*gain*N+T)
        DSH[j]=DSH[j]+dT
        de_ref[j,rows]=-(jnp.sum(nE1*sGZ[p,j],-1,keepdims=True)+jnp.sum(nE2*G,-1,keepdims=True))
        yield
        dZ1=dA*sAd[p,j]+dgZ1*sHA[p,j]
        dZ1b=dZ1.astype(bf16)
        dd=cat(dQ1b,dZ1b)
        X=nn(L2,dd)
        KD[j]=KDb+X[:MINI]
        DW1[j]=DW+X[MINI:]
        DB1[j]=DB1[j]+sb1[p,j]+jnp.sum(dZ1,0,keepdims=True)
        yield
        qk=nt(dd,sW1[p,j])
        dq_ref[j,rows]=(dO+qk[:MINI]-dQs).astype(bf16)
        dk_ref[j,rows]=(qk[MINI:]-dKs-a3+dT).astype(bf16)
    def qside(j,p,t,i):
        rows=pl.ds(pl.multiple_of(t*MINI,MINI),MINI)
        brow=pl.ds(pl.multiple_of(i*MINI,MINI),MINI)
        gain=gain_ref[j]
        dO=do_ref[j,rows].astype(f32); Nq=nq_ref[j,rows]
        dNq=dO*gain
        dQ2=sq_ref[j,rows]*(dNq-rs(dNq)-Nq*rs(dNq*Nq))
        dQ2b=dQ2.astype(bf16)
        A,Ad,Add=gelu3(z1_ref[j,brow].astype(f32))
        AQ,AQd=gelu2(q1_ref[j,brow].astype(f32))
        H=h_ref[j,brow].astype(f32); e=e_ref[j,rows]
        Ab=A.astype(bf16); AQb=AQ.astype(bf16)
        gZ1=H*Ad
        E1b=(e*gZ1).astype(bf16); E2b=(e*g_ref[j,rows]).astype(bf16)
        w1b=w1s_ref[j,i]; w2b=w2s_ref[j,i]
        yield
        sA[p,j]=Ab; sAd[p,j]=Ad; sHA[p,j]=H*Add; sGZ[p,j]=gZ1; sE1[p,j]=E1b; sE2[p,j]=E2b; sW1[p,j]=w1b; sW2[p,j]=w2b; sAQ[p,j]=AQb
        sQ2[p,j]=dQ2b; sb2[p,j]=jnp.sum(dQ2,0,keepdims=True)
        DGQ[j]=DGQ[j]+dO*Nq; DSQ[j]=DSQ[j]+dO
        Q=q_ref[j,rows]; K=k_ref[j,rows]
        P1=(lower*(nt(Q,K)+1.0)).astype(bf16)
        P2=(lower*(nt(AQb,Ab)+1.0)).astype(bf16)
        yield
        X2=(lower*nt(dQ2b,E2b)).astype(bf16)
        yield
        b1=nn(dQ2b,w2b)
        yield
        sR2[p,j]=tn(P2,dQ2b)
        yield
        dAQ=b1-nn(X2,Ab)
        sDA[p,j]=-tn(X2,AQb)
        yield
        yield
        dQ1=dAQ*AQd
        dQ1b=dQ1.astype(bf16)
        sQ1[p,j]=dQ1b; sb1[p,j]=jnp.sum(dQ1,0,keepdims=True)
        sR1[p,j]=tn(P1,dQ1b)
    @pl.loop(0,count//unroll)
    def _(i):
        for u in range(unroll):
            ii=count-1-(i*unroll+u)
            t=(nb-1-pid)*count+ii
            interleave([crit(j,u%2,t+1) for j in range(slots)]+[qside(j,(u+1)%2,t,ii) for j in range(slots)])
    @pl.when(pid==nb-1)
    def _():
        interleave([crit(j,0,jnp.int32(0)) for j in range(slots)])
        for j in range(slots):
            dw1_ref[j]=DW1[j]; db1_ref[j]=DB1[j]; dw2_ref[j]=G2[j]; db2_ref[j]=DB2[j]
            dgn_ref[j]=jnp.sum(DGN[j]+DGQ[j],0,keepdims=True); dsh_ref[j]=jnp.sum(DSH[j]+DSQ[j],0,keepdims=True)

def bwd_call(q,k,v,e,dO,n,g,nq,s,sq,w1s,w2s,z1,h,q1,gain,shift,block=256,unroll=2,**kw):
    slots,length,_=q.shape
    count=block//MINI; nb=length//block; steps=length//MINI
    row=lambda w: pl.BlockSpec((slots,block,w),lambda i:(0,nb-1-i,0))
    full=lambda s: pl.BlockSpec(s,lambda i:(0,)*len(s),pipeline_mode=pl.Buffered(1))
    r64=full((slots,length,64)); r1=full((slots,length,1))
    st=pl.BlockSpec((slots,count,64,256),lambda i:(0,nb-1-i,0,0))
    S=jax.ShapeDtypeStruct
    outs=[((slots,64,256),f32),((slots,1,256),f32),((slots,64,256),f32),((slots,1,64),f32),((slots,1,64),f32),((slots,1,64),f32)]
    V=lambda *s,d=f32: pltpu.VMEM(s,d)
    return pl.pallas_call(functools.partial(bwd_kernel,slots,count,unroll),
        grid=(nb,),
        in_specs=[r64]*3+[r1]+[r64]*4+[r1]*2+[st,st]+[row(256)]*3+[full(gain.shape)]*2,
        out_specs=[r64]*3+[r1]+[full(o[0]) for o in outs],
        out_shape=[S((slots,length,64),bf16)]*3+[S((slots,length,1),f32)]+[S(*o) for o in outs],
        scratch_shapes=[V(slots,64,256),V(slots,1,256),V(slots,64,256),V(slots,1,64),V(slots,MINI,256),V(slots,MINI,64),V(slots,MINI,64),V(slots,MINI,64),V(slots,MINI,64),
          V(2,slots,MINI,256,d=bf16),V(2,slots,MINI,256),V(2,slots,MINI,256),V(2,slots,MINI,256),V(2,slots,MINI,256,d=bf16),V(2,slots,MINI,64,d=bf16),
          V(2,slots,64,256,d=bf16),V(2,slots,64,256,d=bf16),V(2,slots,MINI,256),V(2,slots,MINI,64),V(2,slots,MINI,256),V(2,slots,MINI,256,d=bf16),V(2,slots,MINI,64,d=bf16),V(2,slots,MINI,256,d=bf16),V(2,slots,1,256),V(2,slots,1,64)],
        compiler_params=pltpu.CompilerParams(dimension_semantics=("arbitrary",),vmem_limit_bytes=VMEM_BYTES),
        name="inner_backward",**kw)(q,k,v,e,dO,n,g,nq,s,sq,w1s,w2s,z1,h,q1,gain,shift)


def rms_back(grad_scaled, inputs, scale):
    return scale * (
        grad_scaled - inputs * scale * scale * jnp.mean(grad_scaled * inputs, -1, keepdims=True)
    )


def gather(block):
    return lax.all_gather(block, "fsdp", axis=0, tiled=True)


def scatter_sum(block, axis):
    return lax.psum_scatter(block.astype(bf16), axis, scatter_dimension=0, tiled=True).astype(f32)


def swap(block, axes):
    return lax.all_to_all(block, axes, split_axis=0, concat_axis=0, tiled=True)


def pad_to(array_in, size, dim):
    widths = [(0, 0)] * array_in.ndim
    widths[dim] = (0, size - array_in.shape[dim])
    return jnp.pad(array_in, widths)


def shards(
    tokens,
    lengths,
    cotangent,
    pre_gain,
    query_weight,
    key_weight,
    value_weight,
    gate_weight,
    rate_weight,
    out_weight,
    post_gain,
    ffn_gate,
    ffn_up,
    ffn_down,
    inner_first,
    inner_first_bias,
    inner_second,
    inner_second_bias,
    inner_gain,
    inner_shift,
):
    micro, _, rows, width = tokens.shape
    local, head, inner = inner_first.shape
    ff = ffn_gate.shape[1]
    Z = lax.axis_size("sp")
    S = lax.axis_size("fsdp")
    z = lax.axis_index("sp")
    d = lax.axis_index("fsdp")
    groups = S // micro
    slots = -(-local // groups)
    order = [[g for g in range(h, local, groups)] for h in range(groups)]
    flat = [g for part in order for g in part]
    span = 3 * head
    tiles = -(-slots * span // 128)
    piece = Z * rows
    length = S * piece
    total = micro * rows
    own = query_weight.shape[0]
    extra = local * span
    packed_width = -(-(extra + local + 2) // 128) * 128

    def columns(weight, count):
        return lax.dynamic_slice_in_dim(weight, z * count, count, 1)

    q_w, k_w, v_w = (
        columns(w, local * head).reshape(own, local, head)
        for w in (query_weight, key_weight, value_weight)
    )
    r_w = columns(rate_weight, local)
    parts = []
    for g in flat:
        parts += [q_w[:, g], k_w[:, g], v_w[:, g]]
    parts += [r_w, pre_gain[:, None], post_gain[:, None]]
    packed = pad_to(jnp.concatenate(parts, 1), packed_width, 1)
    front = gather(packed)
    all_tokens = lax.all_gather(tokens[:, 0], "sp", axis=0)
    rear_in = (out_weight, gate_weight, ffn_gate, ffn_up, ffn_down)
    rear_in, front, all_tokens = lax.optimization_barrier((rear_in, front, all_tokens))
    pre_full = front[:, extra + local].astype(f32)[None]
    post_full = front[:, extra + local + 1].astype(f32)[None]
    token_rows = all_tokens.reshape(Z * total, width).astype(f32)
    scale_one = lax.rsqrt(jnp.mean(token_rows * token_rows, -1, keepdims=True) + EPS)
    normed = (token_rows * scale_one * pre_full).astype(bf16)
    projected = nn(normed, front)
    rate_sig = jax.nn.sigmoid(projected[:, extra : extra + local])
    rate_rows = (RATE * rate_sig).astype(bf16).reshape(Z, micro, rows, local)
    low = projected.astype(bf16).reshape(Z, micro, rows, packed_width)
    rate_tiles = slots * piece // 128

    def pack_tiles(pieces, rates):
        body = pieces.reshape(S, piece, tiles, 128).transpose(0, 2, 1, 3)
        tail = pad_to(rates.reshape(S, rate_tiles, 128), 16 * (-(-rate_tiles // 16)), 1)
        return jnp.concatenate([body.reshape(S, tiles * piece, 128), tail], 1)

    low_parts = []
    rate_parts = []
    start = 0
    for part in order:
        stop = min(start + tiles * 128, packed_width)
        low_parts.append(pad_to(low[..., start:stop], tiles * 128, 3))
        start += len(part) * span
        here = [rate_rows[..., g : g + 1] for g in part] + [jnp.zeros_like(rate_rows[..., :1])] * (slots - len(part))
        rate_parts.append(jnp.concatenate(here, 3))
    send_low = jnp.stack(low_parts).transpose(0, 2, 1, 3, 4).reshape(S, piece, tiles * 128)
    send_rate = jnp.stack(rate_parts).transpose(0, 2, 4, 1, 3).reshape(S, slots, piece)
    arrived = swap(pack_tiles(send_low, send_rate), "fsdp")
    body = arrived[:, : tiles * piece].reshape(S, tiles, piece, 128)

    def chain_rows(index):
        out = []
        for j in range(slots):
            lane = j * span + index * head
            out.append(body[:, lane // 128, :, lane % 128 : lane % 128 + head].reshape(length, head))
        return jnp.stack(out)

    q, k, v = chain_rows(0), chain_rows(1), chain_rows(2)
    e = arrived[:, tiles * piece : tiles * piece + rate_tiles].reshape(S, slots, piece)
    e = e.transpose(1, 0, 2).reshape(slots, length, 1).astype(f32)

    half = d // micro
    heads_here = [jnp.minimum(half + j * groups, local - 1) for j in range(slots)]

    def of_slots(array_in):
        return jnp.stack([lax.dynamic_index_in_dim(array_in, g, 0, keepdims=False) for g in heads_here])

    w1 = of_slots(inner_first)
    b1 = of_slots(inner_first_bias)[:, None]
    w2 = of_slots(inner_second)
    w2 = (w2 - jnp.mean(w2, -1, keepdims=True)).transpose(0, 2, 1)
    b2 = of_slots(inner_second_bias)[:, None]
    b2 = b2 - jnp.mean(b2, -1, keepdims=True)
    gain = of_slots(inner_gain)[:, None]
    shift = of_slots(inner_shift)[:, None]
    mix, w1s, w2s, z1, h, q1, n, g_, nq, s, sq = fwd_call(q, k, v, e, w1, b1, w2, b2, gain, shift, unroll=2)

    out_in, gate_in, fgate_in, fup_in, down_in = rear_in
    rear = gather(jnp.concatenate([out_in, gate_in, fgate_in, fup_in], 1))
    out_full = rear[:, :width]
    gate_full = rear[:, width : 2 * width]
    fgate_full = rear[:, 2 * width : 2 * width + ff]
    fup_full = rear[:, 2 * width + ff :]
    down_full = gather(down_in)

    def to_tokens(chains):
        send = chains.reshape(slots, S, Z, rows, head).transpose(1, 2, 3, 0, 4)
        got = swap(send.reshape(S * Z, rows, slots * head), ("fsdp", "sp"))
        got = got.reshape(groups, micro, Z, rows, slots, head).transpose(1, 3, 2, 4, 0, 5)
        return got.reshape(total, Z, slots * groups, head)[:, :, :local].reshape(total, width)

    def to_chains(block):
        send = pad_to(block.reshape(micro, rows, Z, local, head), slots * groups, 3)
        send = send.reshape(micro, rows, Z, slots, groups, head).transpose(4, 0, 2, 1, 3, 5)
        got = swap(send.reshape(S * Z, rows, slots * head), ("fsdp", "sp"))
        return got.reshape(length, slots, head).transpose(1, 0, 2)

    mixed_rows = to_tokens(mix).astype(f32)
    own_tokens = tokens.reshape(total, width).astype(f32)
    own_normed = lax.dynamic_slice_in_dim(normed, z * total, total, 0)
    gate_logit = nn(own_normed, gate_full)
    gate_act, gate_slope = gelu2(gate_logit)
    gated = (gate_act * mixed_rows).astype(bf16)
    middle = own_tokens + nn(gated, out_full)
    scale_two = lax.rsqrt(jnp.mean(middle * middle, -1, keepdims=True) + EPS)
    normed_two = (middle * scale_two * post_full).astype(bf16)
    gate_pre = nn(normed_two, fgate_full)
    up_pre = nn(normed_two, fup_full)
    gate_sig = jax.nn.sigmoid(gate_pre)
    silu_act = gate_pre * gate_sig
    hidden = (silu_act * up_pre).astype(bf16)
    output = (middle + nn(hidden, down_full)).astype(bf16)

    position = d * piece + z * rows + lax.broadcasted_iota(jnp.int32, (micro, rows), 1)
    live = (position < lengths[:, None]).astype(f32).reshape(total, 1)
    grad_out = cotangent.reshape(total, width).astype(f32) * live
    grad_low = grad_out.astype(bf16)
    grad_hidden = nt(grad_low, down_full)
    grad_gate_pre = (grad_hidden * up_pre * gate_sig * (1.0 + gate_pre * (1.0 - gate_sig))).astype(bf16)
    grad_up_pre = (grad_hidden * silu_act).astype(bf16)
    grad_normed_two = nt(grad_gate_pre, fgate_full) + nt(grad_up_pre, fup_full)
    grad_middle = grad_out + rms_back(grad_normed_two * post_full, middle, scale_two)
    grad_branch = grad_middle.astype(bf16)
    grad_gated = nt(grad_branch, out_full)
    grad_mixed = (grad_gated * gate_act).astype(bf16)
    grad_gate_logit = (grad_gated * mixed_rows * gate_slope).astype(bf16)
    d_mix = to_chains(grad_mixed)
    rear_grad = jnp.concatenate(
        [
            tn(gated, grad_branch).astype(bf16),
            tn(own_normed, grad_gate_logit).astype(bf16),
            tn(normed_two, grad_gate_pre).astype(bf16),
            tn(normed_two, grad_up_pre).astype(bf16),
        ],
        1,
    )
    down_grad = tn(hidden, grad_low)
    rear_sum = scatter_sum(rear_grad, "fsdp")
    down_sum = scatter_sum(down_grad, "fsdp")
    rear_sum = lax.psum(rear_sum.astype(bf16), "sp").astype(f32)
    down_sum = lax.psum(down_sum.astype(bf16), "sp").astype(f32)
    grad_normed_gate = nt(grad_gate_logit, gate_full)

    dq, dk, dv, de, dw1, db1, dw2, db2, dgn, dsh = bwd_call(
        q, k, v, e, d_mix, n, g_, nq, s, sq, w1s, w2s, z1, h, q1, gain, shift
    )
    dw2 = dw2 - jnp.mean(dw2, 1, keepdims=True)
    db2 = db2 - jnp.mean(db2, -1, keepdims=True)
    small = jnp.concatenate([db1[:, 0], db2[:, 0], dgn[:, 0], dsh[:, 0], jnp.zeros((slots, head), f32)], 1)
    inner_rows = jnp.concatenate([dw1, dw2, pad_to(small.reshape(slots, 2, inner), 8, 1)], 1)
    spread = jnp.zeros((local,) + inner_rows.shape[1:], f32)
    for j in range(slots):
        here = jnp.arange(local)[:, None, None] == half + j * groups
        spread = spread + jnp.where(here, inner_rows[j][None], 0.0)
    inner_sum = lax.psum(spread.astype(bf16), "fsdp").astype(f32)

    grads = jnp.stack([dq, dk, dv], 2).transpose(1, 0, 2, 3).reshape(S, piece, slots * span)
    rates_back = de[..., 0].astype(bf16).reshape(slots, S, piece).transpose(1, 0, 2)
    arrived = swap(pack_tiles(pad_to(grads, tiles * 128, 2), rates_back), "fsdp")
    body = arrived[:, : tiles * piece].reshape(groups, micro, tiles, Z, rows, 128)
    body = body.transpose(3, 1, 4, 0, 2, 5).reshape(Z * total, groups, tiles * 128)
    back = arrived[:, tiles * piece : tiles * piece + rate_tiles].reshape(groups, micro, slots, Z, rows)
    back = back.transpose(3, 1, 4, 2, 0).reshape(Z * total, slots * groups)[:, :local].astype(f32)
    grad_rate_logit = (back * RATE * rate_sig * (1.0 - rate_sig)).astype(bf16)
    grad_packed = pad_to(
        jnp.concatenate(
            [body[:, i, : len(part) * span] for i, part in enumerate(order) if part] + [grad_rate_logit], 1
        ),
        packed_width,
        1,
    )
    weight_grad = scatter_sum(tn(normed, grad_packed), "fsdp")
    weight_all = lax.all_gather(weight_grad.astype(bf16), "sp", axis=1).astype(f32)
    pieces = weight_all[..., :extra].reshape(own, Z, local, 3, head)
    pieces = jnp.stack([pieces[:, :, flat.index(g)] for g in range(local)], 2)
    query_grad, key_grad, value_grad = (pieces[:, :, :, i].reshape(own, width) for i in range(3))
    rate_grad = weight_all[..., extra : extra + local].reshape(own, Z * local)
    grad_normed = scatter_sum(nt(grad_packed, front), "sp") + grad_normed_gate
    own_scale = lax.dynamic_slice_in_dim(scale_one, z * total, total, 0)
    tokens_grad = (grad_middle + rms_back(grad_normed * pre_full, own_tokens, own_scale)).astype(bf16)

    out_grad = rear_sum[:, :width]
    gate_grad = rear_sum[:, width : 2 * width]
    fgate_grad = rear_sum[:, 2 * width : 2 * width + ff]
    fup_grad = rear_sum[:, 2 * width + ff :]

    def row_dot(grad, weight):
        return jnp.sum(grad * weight.astype(f32), -1)

    pre_grad = (
        row_dot(query_grad, query_weight)
        + row_dot(key_grad, key_weight)
        + row_dot(value_grad, value_weight)
        + row_dot(gate_grad, gate_weight)
        + row_dot(rate_grad, rate_weight)
    ) / pre_gain.astype(f32)
    post_grad = (row_dot(fgate_grad, ffn_gate) + row_dot(fup_grad, ffn_up)) / post_gain.astype(f32)

    tail = inner_sum[:, 2 * head : 2 * head + 2].reshape(local, 2 * inner)
    return (
        output.reshape(tokens.shape),
        tokens_grad.reshape(tokens.shape),
        pre_grad,
        query_grad,
        key_grad,
        value_grad,
        gate_grad,
        rate_grad,
        out_grad,
        post_grad,
        fgate_grad,
        fup_grad,
        down_sum,
        inner_sum[:, :head],
        tail[:, :inner],
        inner_sum[:, head : 2 * head].transpose(0, 2, 1),
        tail[:, inner : inner + head],
        tail[:, inner + head : inner + 2 * head],
        tail[:, inner + 2 * head : inner + 3 * head],
    )


def solution(mesh):
    return jax.shard_map(
        shards,
        mesh=mesh,
        in_specs=(
            P(None, "fsdp", "sp", None),
            P(),
            P(None, "fsdp", "sp", None),
            P("fsdp"),
            P("fsdp", None),
            P("fsdp", None),
            P("fsdp", None),
            P("fsdp", None),
            P("fsdp", None),
            P("fsdp", None),
            P("fsdp"),
            P("fsdp", None),
            P("fsdp", None),
            P("fsdp", None),
            P("sp", None, None),
            P("sp", None),
            P("sp", None, None),
            P("sp", None),
            P("sp", None),
            P("sp", None),
        ),
        out_specs=(
            P(None, "fsdp", "sp", None),
            P(None, "fsdp", "sp", None),
            P("fsdp"),
            P("fsdp", None),
            P("fsdp", None),
            P("fsdp", None),
            P("fsdp", None),
            P("fsdp", None),
            P("fsdp", None),
            P("fsdp"),
            P("fsdp", None),
            P("fsdp", None),
            P("fsdp", None),
            P("sp", None, None),
            P("sp", None),
            P("sp", None, None),
            P("sp", None),
            P("sp", None),
            P("sp", None),
        ),
        check_vma=False,
    )
```

time: 5830 us -> 710 us (0.12)
  waiting for transfers between devices: 3280 us -> 338 us
  matrix products: 1010 us -> 45 us
  local copies, waits for them, and re-layouts: 620 us -> 58.1 us
  starting transfers between devices: 446 us -> 15.1 us
  other arithmetic: 341 us -> 32.9 us
  Pallas kernels: 0 us -> 169 us
    ppermute x22 -> x0, waiting for transfers between devices: 2850 us -> none  [from_behind(): return lax.ppermute(block, axis, route)]
    dot_general x3116 -> x18, matrix products: 1010 us -> 45 us  [the longest x6 16.7 us: nn(): lax.dot_general(x.astype(bf16), y.astype(bf16), (((1,), (0,)), ((), ())),...]
    ppermute x22 -> x0, starting transfers between devices: 285 us -> none  [from_behind(): return lax.ppermute(block, axis, route)]
    squeeze x452 -> x5, local copies, waits for them, and re-layouts: 262 us -> 4.12 us  [the longest x2 4.11 us: shards(): body[:, i, :len(part) * span]]
    dynamic_update_slice x272 -> x0, local copies, waits for them, and re-layouts: 177 us -> none  [the longest x256 164 us: piece_mixer(): lax.scan(jax.checkpoint(advance), inner_state, (arrange(query_heads), arr...]
    pallas_call x0 -> x2, Pallas kernels: none -> 169 us  [the longest x1 93.8 us: bwd_call(): pl.pallas_call(functools.partial(bwd_kernel, slots, count, unroll), grid=...]
    reduce_sum x1024 -> x10, other arithmetic: 156 us -> 4.15 us  [the longest x6 3.88 us: row_dot(): return jnp.sum(grad * weight.astype(f32), -1)]
    all_to_all x40 -> x4, starting transfers between devices: 159 us -> 14.5 us  [swap(): return lax.all_to_all(block, axes, split_axis=0, concat_axis=0, tiled=True)]
where the time goes in v1:
time: 710 us; the launch traced here: 701 us
  waiting for transfers between devices  338 us (48%)
  Pallas kernels  169 us (24%)
  local copies, waits for them, and re-layouts  58.1 us (8%)
  matrix products  45 us (6%)
  other arithmetic  32.9 us (5%)
  blocking collectives  27.7 us (4%)
  between operations  15.6 us (2%)
  starting transfers between devices  15.1 us (2%)
    reduce_scatter x4, waiting for transfers between devices, scatter_sum(): lax.psum_scatter(block.astype(bf16), axis, scatter_dimension=0, tiled=True)  174 us
    pallas_call x1, Pallas kernels, bwd_call(): pl.pallas_call(functools.partial(bwd_kernel, slots, count, unroll), grid=...  93.8 us
    pallas_call x1, Pallas kernels, fwd_call(): pl.pallas_call(functools.partial(fwd_kernel, slots, count, unroll), grid=...  74.7 us
    all_to_all x4, waiting for transfers between devices, swap(): return lax.all_to_all(block, axes, split_axis=0, concat_axis=0, tiled=True)  74.5 us
    psum x1, waiting for transfers between devices, shards(): rear_sum = lax.psum(rear_sum.astype(bf16), 'sp').astype(f32)  64.5 us
    all_gather x1, waiting for transfers between devices, shards(): all_tokens = lax.all_gather(tokens[:, 0], 'sp', axis=0)  23.8 us
    dot_general x6, matrix products, nn(): lax.dot_general(x.astype(bf16), y.astype(bf16), (((1,), (0,)), ((), ())),...  16.7 us
    all_gather x1, blocking collectives, shards(): lax.all_gather(weight_grad.astype(bf16), 'sp', axis=1).astype(f32)  15.4 us
  transfers between devices with their start and end apart: 13, of which 10 were waited for; matrix products, arithmetic and copies ran while one was open for 13% of the time, Pallas kernels for 11%

profile of v1, /device:TPU:0, one launch (start us, length us, event | category | flops | bytes accessed | tf_op | source)
XLA Modules:
  0.0 700.9 jit_solution(7936059734523158550)
XLA Ops:
  13.3 12.3 %all_gather.18 = bf16[768,640]{1,0:T(8,128)(2,1)S(1)} all-gather(bf16[96,640]{1,0:T(8,128)(2,1)S(1)} %pad.28.clone), channel_id=1, replica_groups=mesh['sp'=4,'fsdp'=8] {'fsdp'}, dimensions={0}, use_global_device_ids=true | all-gather | bytes 1105920 | tf_op jit(solution)/shard_map/all_gather | solution.py:323
  25.6 23.8 %all-gather.10.cloned.1.call-done = bf16[16,1,64,768]{3,2,1,0:T(8,128)(2,1)} async-done(((bf16[4,1,64,768]{3,2,1,0:T(8,128)(2,1)}), bf16[16,1,64,768]{3,2,1,0:T(8,128)(2,1)}) %all-gather.10.cloned.1.call-update) | async-done | bytes 1572880 | tf_op jit(solution)/shard_map/all_gather | solution.py:396
  53.9 2.5 fusion.58
  59.3 3.9 reshape_reshape.6
  64.9 3.8 all-to-all-start
  72.6 25.9 %all-to-all-done = bf16[8,784,128]{2,1,0:T(8,128)(2,1)S(1)} async-done(((bf16[8,784,128]{2,1,0:T(8,128)(2,1)}), bf16[8,784,128]{2,1,0:T(8,128)(2,1)S(1)}, u32[]{:S(2)}, u32[]{:S(2)}) %all-to-all-start) | async-done | bytes 1605664 | tf_op jit(solution)/shard_map/all_to_all | solution.py:331
  104.8 74.7 %inner_forward.1 = (bf16[2,2048,64]{2,1,0:T(8,128)(2,1)}, bf16[2,128,64,256]{3,2,1,0:T(8,128)(2,1)}, bf16[2,128,64,256]{3,2,1,0:T(8,128)(2,1)}, bf16[2,2048,256]...) custom-call(bf16[2,2048,64]{2,1,0:T(8,128)(2,1)} %pad_maximum_fusion, ...), custom_call_target="tpu_custom_call" | custom-call | tf_op jit(solution)/shard_map/inner_forward/pallas_call | solution.py:153
  183.3 2.8 all-to-all-start.1
  186.4 14.0 %all-to-all-done.1 = bf16[32,64,128]{2,1,0:T(8,128)(2,1)S(1)} async-done(((bf16[32,64,128]{2,1,0:T(8,128)(2,1)}), bf16[32,64,128]{2,1,0:T(8,128)(2,1)S(1)}, u32[]{:S(2)}, u32[]{:S(2)}) %all-to-all-start.1) | async-done | bytes 524320 | tf_op jit(solution)/shard_map/all_to_all | solution.py:331
  202.9 4.5 fusion.59
  209.6 2.7 multiply_reduce_fusion.4
  212.5 3.0 fusion.6
  215.5 2.7 multiply_convert_fusion.1
  226.6 4.3 all-to-all-start.2
  231.4 13.8 %all-to-all-done.2 = bf16[32,64,128]{2,1,0:T(8,128)(2,1)S(1)} async-done(((bf16[32,64,128]{2,1,0:T(8,128)(2,1)}), bf16[32,64,128]{2,1,0:T(8,128)(2,1)S(1)}, u32[]{:S(2)}, u32[]{:S(2)}) %all-to-all-start.2) | async-done | bytes 524320 | tf_op jit(solution)/shard_map/all_to_all | solution.py:331
  246.8 93.8 %inner_backward.1 = (bf16[2,2048,64]{2,1,0:T(8,128)(2,1)}, bf16[2,2048,64]{2,1,0:T(8,128)(2,1)}, bf16[2,2048,64]{2,1,0:T(8,128)(2,1)}, f32[2,2048,1]{2,1,0:T(8,1...) custom-call(bf16[2,2048,64]{2,1,0:T(8,128)(2,1)} %pad_maximum_fusion, ...), custom_call_target="tpu_custom_call" | custom-call | tf_op jit(solution)/shard_map/inner_backward/pallas_call | solution.py:304
  340.6 2.6 maximum_bitcast_fusion
  353.1 3.7 all-to-all-start.3
  358.2 20.7 %all-to-all-done.3 = bf16[8,784,128]{2,1,0:T(8,128)(2,1)S(1)} async-done(((bf16[8,784,128]{2,1,0:T(8,128)(2,1)}), bf16[8,784,128]{2,1,0:T(8,128)(2,1)S(1)}, u32[]{:S(2)}, u32[]{:S(2)}) %all-to-all-start.3) | async-done | bytes 1605664 | tf_op jit(solution)/shard_map/all_to_all | solution.py:331
  381.6 2.5 reshape.343
  390.1 4.0 convolution_convert_fusion.6
  394.1 2.7 convolution_convert_fusion
  400.1 2.6 convolution_convert_fusion.5
  407.6 3.8 pad_maximum_fusion
  412.5 4.1 convolution_convert_fusion.3
  416.8 3.6 fusion.27
  424.9 32.0 %reduce-scatter.7.cloned.1.call-done = bf16[96,640]{1,0:T(8,128)(2,1)} async-done(((bf16[768,640]{1,0:T(8,128)(2,1)}), bf16[96,640]{1,0:T(8,128)(2,1)}) %reduce-scatter.7.cloned.1.call-update) | async-done | bytes 122896 | tf_op jit(solution)/shard_map/reduce_scatter | solution.py:327
  456.9 15.4 %all-gather.1 = bf16[96,2560]{1,0:T(8,128)(2,1)S(1)} all-gather(bf16[96,640]{1,0:T(8,128)(2,1)} %reduce-scatter.7.cloned.1.call-done), channel_id=3, replica_groups=mesh['sp'=4,'fsdp'=8] {'sp'}, dimensions={1}, use_global_device_ids=true | all-gather | bytes 614400 | tf_op jit(solution)/shard_map/all_gather | solution.py:551
  475.2 31.3 %reduce-scatter.11.cloned.1.call-done = bf16[256,768]{1,0:T(8,128)(2,1)} async-done(((bf16[2048,768]{1,0:T(8,128)(2,1)}), bf16[256,768]{1,0:T(8,128)(2,1)}) %reduce-scatter.11.cloned.1.call-update) | async-done | bytes 393232 | tf_op jit(solution)/shard_map/reduce_scatter | solution.py:327
  506.4 76.6 %reduce-scatter.9.cloned.1.call-done = bf16[96,5632]{1,0:T(8,128)(2,1)} async-done(((bf16[768,5632]{1,0:T(8,128)(2,1)}), bf16[96,5632]{1,0:T(8,128)(2,1)}) %reduce-scatter.9.cloned.1.call-update) | async-done | bytes 1081360 | tf_op jit(solution)/shard_map/reduce_scatter | solution.py:327
  586.3 34.4 %reduce-scatter.5.cloned.1.call-done = bf16[256,768]{1,0:T(8,128)(2,1)} async-done(((bf16[1024,768]{1,0:T(8,128)(2,1)}), bf16[256,768]{1,0:T(8,128)(2,1)}) %reduce-scatter.5.cloned.1.call-update) | async-done | bytes 393232 | tf_op jit(solution)/shard_map/reduce_scatter | solution.py:327
  623.8 64.5 %all-reduce.14.cloned.1.call-done = (bf16[96,5632]{1,0:T(8,128)(2,1)}, bf16[256,768]{1,0:T(8,128)(2,1)}) async-done(((bf16[96,5632]{1,0:T(8,128)(2,1)}, bf16[256,768]{1,0:T(8,128)(2,1)}), (bf16[96,5632]{1,0:T(8,128)(2,1)}, bf16[256,768]{1,0:T(8,128)(2,1)})) %all-reduce.14.cloned.1.call-update) | async-done | bytes 1474576 | tf_op jit(solution)/shard_map/psum | solution.py:518
  (301 shorter events, 92.3 us)
Async XLA Ops:
  7.2 42.2 %all-gather.10.cloned.1.call-start = ((), (), s32[]{:S(2)}) async-start(), calls=%async_computation.15 | async-start | bytes 1966080 | tf_op jit(solution)/shard_map/all_gather | solution.py:396
  7.9 41.6 %copy-start.15 = (bf16[96,2048]{1,0:T(8,128)(2,1)S(1)}, bf16[96,2048]{1,0:T(8,128)(2,1)}, u32[]{:S(2)}) copy-start(bf16[96,2048]{1,0:T(8,128)(2,1)} %param.32) | copy-start | bytes 1179652
  7.9 41.6 %copy-start.17 = (bf16[96,2048]{1,0:T(8,128)(2,1)S(1)}, bf16[96,2048]{1,0:T(8,128)(2,1)}, u32[]{:S(2)}) copy-start(bf16[96,2048]{1,0:T(8,128)(2,1)} %param.31) | copy-start | bytes 1179652
  7.9 41.6 %copy-start.34 = (bf16[96,768]{1,0:T(8,128)(2,1)S(1)}, bf16[96,768]{1,0:T(8,128)(2,1)}, u32[]{:S(2)}) copy-start(bf16[96,768]{1,0:T(8,128)(2,1)} %param.27) | copy-start | bytes 442372
  8.0 195.0 %all-gather.8.cloned.1.call-start = ((), (), s32[]{:S(2)}) async-start(), calls=%async_computation.9 | async-start | bytes 3538944 | tf_op jit(solution)/shard_map/all_gather | solution.py:323
  9.2 16.4 %copy-start.30 = (bf16[96,768]{0,1:T(8,128)(2,1)}, bf16[96,768]{0,1:T(8,128)(2,1)S(1)}, u32[]{:S(2)}) copy-start(bf16[96,768]{0,1:T(8,128)(2,1)S(1)} %copy.184) | copy-start | bytes 442372
  10.3 15.3 %copy-start.26 = (bf16[96,768]{0,1:T(8,128)(2,1)}, bf16[96,768]{0,1:T(8,128)(2,1)S(1)}, u32[]{:S(2)}) copy-start(bf16[96,768]{0,1:T(8,128)(2,1)S(1)} %copy.185) | copy-start | bytes 442372
  11.5 14.1 %copy-start.28 = (bf16[96,768]{0,1:T(8,128)(2,1)}, bf16[96,768]{0,1:T(8,128)(2,1)S(1)}, u32[]{:S(2)}) copy-start(bf16[96,768]{0,1:T(8,128)(2,1)S(1)} %copy.186) | copy-start | bytes 442372
  25.6 28.3 %copy-start.14 = (bf16[768,640]{1,0:T(8,128)(2,1)}, bf16[768,640]{1,0:T(8,128)(2,1)S(1)}, u32[]{:S(2)}) copy-start(bf16[768,640]{1,0:T(8,128)(2,1)S(1)} %all_gather.18) | copy-start | bytes 2949124
  25.6 26.1 %copy-start.57 = (f32[3,256]{1,0:T(4,128)S(1)}, f32[3,256]{1,0:T(4,128)}, u32[]{:S(2)}) copy-start(f32[3,256]{1,0:T(4,128)} %param.35) | copy-start | bytes 9220
  25.6 26.1 %copy-start.58 = (f32[3,64]{1,0:T(4,128)S(1)}, f32[3,64]{1,0:T(4,128)}, u32[]{:S(2)}) copy-start(f32[3,64]{1,0:T(4,128)} %param.39) | copy-start | bytes 2308
  25.6 26.1 %copy-start.59 = (f32[3,64]{1,0:T(4,128)S(1)}, f32[3,64]{1,0:T(4,128)}, u32[]{:S(2)}) copy-start(f32[3,64]{1,0:T(4,128)} %param.38) | copy-start | bytes 2308
  49.4 157.9 %all-gather.6.cloned.1.call-start = ((), (), s32[]{:S(2)}) async-start(), calls=%async_computation.8 | async-start | bytes 9732096 | tf_op jit(solution)/shard_map/all_gather | solution.py:323
  64.9 33.5 %all-to-all-start = ((bf16[8,784,128]{2,1,0:T(8,128)(2,1)}), bf16[8,784,128]{2,1,0:T(8,128)(2,1)S(1)}, u32[]{:S(2)}, u32[]{:S(2)}) async-start(bf16[8,784,128]{2,1,0:T(8,128)(2,1)} %fusion.16), calls=%async_computation | async-start | bytes 3211264 | tf_op jit(solution)/shard_map/all_to_all | solution.py:331
  183.3 17.1 %all-to-all-start.1 = ((bf16[32,64,128]{2,1,0:T(8,128)(2,1)}), bf16[32,64,128]{2,1,0:T(8,128)(2,1)S(1)}, u32[]{:S(2)}, u32[]{:S(2)}) async-start(bf16[32,64,128]{2,1,0:T(8,128)(2,1)} %reshape.331), calls=%async_computation.1 | async-start | bytes 1048576 | tf_op jit(solution)/shard_map/all_to_all | solution.py:331
  186.4 16.5 %copy-start.7 = (bf16[256,768]{1,0:T(8,128)(2,1)}, bf16[256,768]{1,0:T(8,128)(2,1)S(1)}, u32[]{:S(2)}) copy-start(bf16[256,768]{1,0:T(8,128)(2,1)S(1)} %fusion.42) | copy-start | bytes 1179652
  207.4 8.1 %copy-start.62 = (bf16[768,5632]{1,0:T(8,128)(2,1)S(1)}, bf16[768,5632]{1,0:T(8,128)(2,1)}, u32[]{:S(2)}) copy-start(bf16[768,5632]{1,0:T(8,128)(2,1)} %all-gather.6.cloned.1.call-done) | copy-start | bytes 25952260
  212.3 8.4 %copy-start.9 = (f32[256,768]{1,0:T(8,128)}, f32[256,768]{1,0:T(8,128)S(1)}, u32[]{:S(2)}) copy-start(f32[256,768]{1,0:T(8,128)S(1)} %get-tuple-element.234) | copy-start | bytes 2359300
  226.6 18.6 %all-to-all-start.2 = ((bf16[32,64,128]{2,1,0:T(8,128)(2,1)}), bf16[32,64,128]{2,1,0:T(8,128)(2,1)S(1)}, u32[]{:S(2)}, u32[]{:S(2)}) async-start(bf16[32,64,128]{2,1,0:T(8,128)(2,1)} %reshape.337), calls=%async_computation.2 | async-start | bytes 1048576 | tf_op jit(solution)/shard_map/all_to_all | solution.py:331
  353.1 25.9 %all-to-all-start.3 = ((bf16[8,784,128]{2,1,0:T(8,128)(2,1)}), bf16[8,784,128]{2,1,0:T(8,128)(2,1)S(1)}, u32[]{:S(2)}, u32[]{:S(2)}) async-start(bf16[8,784,128]{2,1,0:T(8,128)(2,1)} %fusion.17), calls=%async_computation.3 | async-start | bytes 3211264 | tf_op jit(solution)/shard_map/all_to_all | solution.py:331
  356.8 63.6 %all-reduce.12.cloned.1.call-start = ((), (), s32[]{:S(2)}) async-start(), calls=%async_computation.14 | async-start | bytes 417792 | tf_op jit(solution)/shard_map/psum | solution.py:533
  358.1 98.8 %reduce-scatter.7.cloned.1.call-start = ((), (), s32[]{:S(2)}) async-start(), calls=%async_computation.11 | async-start | bytes 1105920 | tf_op jit(solution)/shard_map/reduce_scatter | solution.py:327
  394.1 112.4 %reduce-scatter.11.cloned.1.call-start = ((), (), s32[]{:S(2)}) async-start(), calls=%async_computation.13 | async-start | bytes 3538944 | tf_op jit(solution)/shard_map/reduce_scatter | solution.py:327
  396.8 186.2 %reduce-scatter.9.cloned.1.call-start = ((), (), s32[]{:S(2)}) async-start(), calls=%async_computation.12 | async-start | bytes 9732096 | tf_op jit(solution)/shard_map/reduce_scatter | solution.py:327
  411.5 209.2 %reduce-scatter.5.cloned.1.call-start = ((), (), s32[]{:S(2)}) async-start(), calls=%async_computation.10 | async-start | bytes 1966080 | tf_op jit(solution)/shard_map/reduce_scatter | solution.py:327
  416.6 271.7 %all-reduce.14.cloned.1.call-start = ((), (), s32[]{:S(2)}) async-start(), calls=%async_computation.16 | async-start | bytes 2949120 | tf_op jit(solution)/shard_map/psum | solution.py:518
  473.7 112.2 %copy-start.46 = (f32[96,12]{0,1:T(8,128)}, f32[96,12]{0,1:T(8,128)S(1)}, u32[]{:S(2)}) copy-start(f32[96,12]{0,1:T(8,128)S(1)} %reshape.348) | copy-start | bytes 13828
  583.2 37.5 %copy-start.21 = (bf16[4,1,64,768]{3,2,1,0:T(8,128)(2,1)S(1)}, bf16[4,1,64,768]{3,2,1,0:T(8,128)(2,1)}, u32[]{:S(2)}) copy-start(bf16[4,1,64,768]{3,2,1,0:T(8,128)(2,1)} %param.20) | copy-start | bytes 1179652
  583.2 37.4 %copy-start.48 = (f32[768]{0:T(1024)S(1)}, f32[768]{0:T(1024)}, u32[]{:S(2)}) copy-start(f32[768]{0:T(1024)} %copy-done.47) | copy-start | bytes 9220
  586.3 102.1 %copy-start.35 = (bf16[96,768]{1,0:T(8,128)(2,1)S(1)}, bf16[96,768]{1,0:T(8,128)(2,1)}, u32[]{:S(2)}) copy-start(bf16[96,768]{1,0:T(8,128)(2,1)} %param.27) | copy-start | bytes 442372
  622.8 67.6 %copy-start.16 = (bf16[96,2048]{1,0:T(8,128)(2,1)S(1)}, bf16[96,2048]{1,0:T(8,128)(2,1)}, u32[]{:S(2)}) copy-start(bf16[96,2048]{1,0:T(8,128)(2,1)} %param.32) | copy-start | bytes 1179652
  622.8 67.6 %copy-start.18 = (bf16[96,2048]{1,0:T(8,128)(2,1)S(1)}, bf16[96,2048]{1,0:T(8,128)(2,1)}, u32[]{:S(2)}) copy-start(bf16[96,2048]{1,0:T(8,128)(2,1)} %param.31) | copy-start | bytes 1179652
  (44 other events, 142.4 us)
Sparse Core Ops, SparseCore 0:
  9.6 39.7 all-gather.9
  51.3 43.4 all-gather.7
  96.7 57.7 all-gather.5
  361.0 55.8 all-reduce.11
  420.3 36.5 reduce-scatter.6
  460.1 46.2 reduce-scatter.10
  510.4 72.6 reduce-scatter.8
  585.3 35.3 reduce-scatter.4
  623.1 65.1 all-reduce.13

commit v2 on v1

--- a/solution.py
+++ b/solution.py
@@ -53,7 +53,7 @@
     return lower.astype(f32), jnp.where(lower,0.0,1.0)
 
 def fwd_kernel(slots,count,unroll,q_ref,k_ref,v_ref,e_ref,w1_ref,b1_ref,w2_ref,b2_ref,gain_ref,shift_ref,
-    mix_ref,w1s_ref,w2s_ref,z1_ref,h_ref,q1_ref,n_ref,g_ref,nq_ref,s_ref,sq_ref,
+    mix_ref,w1s_ref,w2s_ref,z1_ref,h_ref,q1_ref,n_ref,g_ref,nq_ref,
     W1,B1,W2,B2,Z,ZQ,AP,EP):
     lower,upper=masks()
     steps=q_ref.shape[1]//MINI
@@ -105,7 +105,7 @@
         yield
         H=nn(Gb,w2b)
         E2=e*G; E2b=E2.astype(bf16)
-        n_ref[j,rows]=N; g_ref[j,rows]=G; s_ref[j,rows]=s
+        n_ref[j,rows]=(z-mz).astype(bf16); g_ref[j,rows]=Gb
         EP[j]=E2b; AP[j]=Ab
         yield
         W2[j]=w2-tn(E2b,Ab)
@@ -125,7 +125,7 @@
         Nq=sq*(Q2-mq)
         Qp=q_ref[j,prow].astype(f32)
         mix_ref[j,prow]=(Qp+Nq*gain+shift).astype(bf16)
-        nq_ref[j,prow]=Nq; sq_ref[j,prow]=sq
+        nq_ref[j,prow]=(Q2-mq).astype(bf16)
     @pl.loop(0,count//unroll)
     def _(i):
         for u in range(unroll):
@@ -140,7 +140,7 @@
             sq=lax.rsqrt(vq-mq*mq+EPS)
             Nq=sq*(Q2-mq)
             mix_ref[j,prow]=(q_ref[j,prow].astype(f32)+Nq*gain_ref[j]+shift_ref[j]).astype(bf16)
-            nq_ref[j,prow]=Nq; sq_ref[j,prow]=sq
+            nq_ref[j,prow]=(Q2-mq).astype(bf16)
 
 def fwd_call(q,k,v,e,w1,b1,w2,b2,gain,shift,block=256,unroll=1,**kw):
     slots,length,_=q.shape
@@ -153,14 +153,14 @@
     return pl.pallas_call(functools.partial(fwd_kernel,slots,count,unroll),
         grid=(nb,),
         in_specs=[r64]*3+[r1]+[full(a.shape) for a in (w1,b1,w2,b2,gain,shift)],
-        out_specs=[r64,st,st,row(256),row(256),row(256),r64,r64,r64,r1,r1],
-        out_shape=[S((slots,length,64),bf16),S((slots,steps,64,256),bf16),S((slots,steps,64,256),bf16)]+[S((slots,length,256),bf16)]*3+[S((slots,length,64),f32)]*3+[S((slots,length,1),f32)]*2,
+        out_specs=[r64,st,st,row(256),row(256),row(256),r64,r64,r64],
+        out_shape=[S((slots,length,64),bf16),S((slots,steps,64,256),bf16),S((slots,steps,64,256),bf16)]+[S((slots,length,256),bf16)]*3+[S((slots,length,64),bf16)]*3,
         scratch_shapes=[pltpu.VMEM((slots,64,256),f32),pltpu.VMEM((slots,1,256),f32),pltpu.VMEM((slots,64,256),f32),pltpu.VMEM((slots,1,64),f32),pltpu.VMEM((slots,MINI,256),f32),pltpu.VMEM((slots,MINI,256),f32),pltpu.VMEM((slots,MINI,256),bf16),pltpu.VMEM((slots,MINI,64),bf16)],
         compiler_params=pltpu.CompilerParams(dimension_semantics=("arbitrary",),vmem_limit_bytes=VMEM_BYTES),
-        name="inner_forward",**kw)(q,k,v,e,w1,b1,w2,b2,gain,shift)
-
-
-def bwd_kernel(slots,count,unroll,q_ref,k_ref,v_ref,e_ref,do_ref,n_ref,g_ref,nq_ref,s_ref,sq_ref,w1s_ref,w2s_ref,z1_ref,h_ref,q1_ref,gain_ref,shift_ref,
+        name="inner_forward",cost_estimate=pl.CostEstimate(flops=90_000_000_000,bytes_accessed=40_000_000,transcendentals=0),**kw)(q,k,v,e,w1,b1,w2,b2,gain,shift)
+
+
+def bwd_kernel(slots,count,unroll,q_ref,k_ref,v_ref,e_ref,do_ref,n_ref,g_ref,nq_ref,w1s_ref,w2s_ref,z1_ref,h_ref,q1_ref,gain_ref,shift_ref,
     dq_ref,dk_ref,dv_ref,de_ref,dw1_ref,db1_ref,dw2_ref,db2_ref,dgn_ref,dsh_ref,
     DW1,DB1,G2,DB2,KD,DGN,DSH,DGQ,DSQ,
     sA,sAd,sHA,sGZ,sE1,sE2,sW1,sW2,sR1,sR2,sDA,sQ1,sQ2,sAQ,sb1,sb2):
@@ -189,7 +189,8 @@
         a1=nt(Ab,G2b)
         yP=nt(dHb,w2b)
         yield
-        N=n_ref[j,rows]; G=g_ref[j,rows]; s=s_ref[j,rows]
+        Zc=n_ref[j,rows].astype(f32); G=g_ref[j,rows].astype(f32)
+        s=lax.rsqrt(rs(Zc*Zc)+EPS); N=s*Zc
         K=k_ref[j,rows]; Q=q_ref[j,rows]; Kp=k_ref[j,prow]
         T=shift-v_ref[j,rows].astype(f32)+K.astype(f32)
         U=gain*T
@@ -221,7 +222,7 @@
         yield
         dA=nn(dZb,w2b)+sDA[p,j]-a2
         yield
-        G2[j]=G2f+tn(cat(sQ2[p,j],G.astype(bf16),dZb),cat(sAQ[p,j],dHb,Ab))
+        G2[j]=G2f+tn(cat(sQ2[p,j],g_ref[j,rows],dZb),cat(sAQ[p,j],dHb,Ab))
         DB2[j]=DB2[j]+sb2[p,j]+jnp.sum(dZc,0,keepdims=True)
         dQs=nn(X1,K); dKs=tn(X1,Q)
         dv_ref[j,rows]=(-dT).astype(bf16)
@@ -245,16 +246,17 @@
         rows=pl.ds(pl.multiple_of(t*MINI,MINI),MINI)
         brow=pl.ds(pl.multiple_of(i*MINI,MINI),MINI)
         gain=gain_ref[j]
-        dO=do_ref[j,rows].astype(f32); Nq=nq_ref[j,rows]
+        dO=do_ref[j,rows].astype(f32); Qc=nq_ref[j,rows].astype(f32)
+        sq=lax.rsqrt(rs(Qc*Qc)+EPS); Nq=sq*Qc
         dNq=dO*gain
-        dQ2=sq_ref[j,rows]*(dNq-rs(dNq)-Nq*rs(dNq*Nq))
+        dQ2=sq*(dNq-rs(dNq)-Nq*rs(dNq*Nq))
         dQ2b=dQ2.astype(bf16)
         A,Ad,Add=gelu3(z1_ref[j,brow].astype(f32))
         AQ,AQd=gelu2(q1_ref[j,brow].astype(f32))
         H=h_ref[j,brow].astype(f32); e=e_ref[j,rows]
         Ab=A.astype(bf16); AQb=AQ.astype(bf16)
         gZ1=H*Ad
-        E1b=(e*gZ1).astype(bf16); E2b=(e*g_ref[j,rows]).astype(bf16)
+        E1b=(e*gZ1).astype(bf16); E2b=(e*g_ref[j,rows].astype(f32)).astype(bf16)
         w1b=w1s_ref[j,i]; w2b=w2s_ref[j,i]
         yield
         sA[p,j]=Ab; sAd[p,j]=Ad; sHA[p,j]=H*Add; sGZ[p,j]=gZ1; sE1[p,j]=E1b; sE2[p,j]=E2b; sW1[p,j]=w1b; sW2[p,j]=w2b; sAQ[p,j]=AQb
@@ -291,7 +293,7 @@
             dw1_ref[j]=DW1[j]; db1_ref[j]=DB1[j]; dw2_ref[j]=G2[j]; db2_ref[j]=DB2[j]
             dgn_ref[j]=jnp.sum(DGN[j]+DGQ[j],0,keepdims=True); dsh_ref[j]=jnp.sum(DSH[j]+DSQ[j],0,keepdims=True)
 
-def bwd_call(q,k,v,e,dO,n,g,nq,s,sq,w1s,w2s,z1,h,q1,gain,shift,block=256,unroll=2,**kw):
+def bwd_call(q,k,v,e,dO,n,g,nq,w1s,w2s,z1,h,q1,gain,shift,block=256,unroll=2,**kw):
     slots,length,_=q.shape
     count=block//MINI; nb=length//block; steps=length//MINI
     row=lambda w: pl.BlockSpec((slots,block,w),lambda i:(0,nb-1-i,0))
@@ -303,14 +305,14 @@
     V=lambda *s,d=f32: pltpu.VMEM(s,d)
     return pl.pallas_call(functools.partial(bwd_kernel,slots,count,unroll),
         grid=(nb,),
-        in_specs=[r64]*3+[r1]+[r64]*4+[r1]*2+[st,st]+[row(256)]*3+[full(gain.shape)]*2,
+        in_specs=[r64]*3+[r1]+[r64]*4+[st,st]+[row(256)]*3+[full(gain.shape)]*2,
         out_specs=[r64]*3+[r1]+[full(o[0]) for o in outs],
         out_shape=[S((slots,length,64),bf16)]*3+[S((slots,length,1),f32)]+[S(*o) for o in outs],
         scratch_shapes=[V(slots,64,256),V(slots,1,256),V(slots,64,256),V(slots,1,64),V(slots,MINI,256),V(slots,MINI,64),V(slots,MINI,64),V(slots,MINI,64),V(slots,MINI,64),
           V(2,slots,MINI,256,d=bf16),V(2,slots,MINI,256),V(2,slots,MINI,256),V(2,slots,MINI,256),V(2,slots,MINI,256,d=bf16),V(2,slots,MINI,64,d=bf16),
           V(2,slots,64,256,d=bf16),V(2,slots,64,256,d=bf16),V(2,slots,MINI,256),V(2,slots,MINI,64),V(2,slots,MINI,256),V(2,slots,MINI,256,d=bf16),V(2,slots,MINI,64,d=bf16),V(2,slots,MINI,256,d=bf16),V(2,slots,1,256),V(2,slots,1,64)],
         compiler_params=pltpu.CompilerParams(dimension_semantics=("arbitrary",),vmem_limit_bytes=VMEM_BYTES),
-        name="inner_backward",**kw)(q,k,v,e,dO,n,g,nq,s,sq,w1s,w2s,z1,h,q1,gain,shift)
+        name="inner_backward",cost_estimate=pl.CostEstimate(flops=110_000_000_000,bytes_accessed=40_000_000,transcendentals=0),**kw)(q,k,v,e,dO,n,g,nq,w1s,w2s,z1,h,q1,gain,shift)
 
 
 def rms_back(grad_scaled, inputs, scale):
@@ -321,10 +323,6 @@
 
 def gather(block):
     return lax.all_gather(block, "fsdp", axis=0, tiled=True)
-
-
-def scatter_sum(block, axis):
-    return lax.psum_scatter(block.astype(bf16), axis, scatter_dimension=0, tiled=True).astype(f32)
 
 
 def swap(block, axes):
@@ -451,7 +449,7 @@
     b2 = b2 - jnp.mean(b2, -1, keepdims=True)
     gain = of_slots(inner_gain)[:, None]
     shift = of_slots(inner_shift)[:, None]
-    mix, w1s, w2s, z1, h, q1, n, g_, nq, s, sq = fwd_call(q, k, v, e, w1, b1, w2, b2, gain, shift, unroll=2)
+    mix, w1s, w2s, z1, h, q1, n, g_, nq = fwd_call(q, k, v, e, w1, b1, w2, b2, gain, shift, unroll=2)
 
     out_in, gate_in, fgate_in, fup_in, down_in = rear_in
     rear = gather(jnp.concatenate([out_in, gate_in, fgate_in, fup_in], 1))
@@ -509,32 +507,39 @@
             tn(own_normed, grad_gate_logit).astype(bf16),
             tn(normed_two, grad_gate_pre).astype(bf16),
             tn(normed_two, grad_up_pre).astype(bf16),
+            tn(hidden, grad_low).astype(bf16).reshape(width, ff),
         ],
         1,
     )
-    down_grad = tn(hidden, grad_low)
-    rear_sum = scatter_sum(rear_grad, "fsdp")
-    down_sum = scatter_sum(down_grad, "fsdp")
-    rear_sum = lax.psum(rear_sum.astype(bf16), "sp").astype(f32)
-    down_sum = lax.psum(down_sum.astype(bf16), "sp").astype(f32)
+    d_mix, rear_grad = lax.optimization_barrier((d_mix, rear_grad))
+    rear_part = lax.psum_scatter(rear_grad, "fsdp", scatter_dimension=0, tiled=True)
     grad_normed_gate = nt(grad_gate_logit, gate_full)
 
     dq, dk, dv, de, dw1, db1, dw2, db2, dgn, dsh = bwd_call(
-        q, k, v, e, d_mix, n, g_, nq, s, sq, w1s, w2s, z1, h, q1, gain, shift
-    )
+        q, k, v, e, d_mix, n, g_, nq, w1s, w2s, z1, h, q1, gain, shift
+    )
+    (dq, dk, dv, de, dw1, db1, dw2, db2), rear_part = lax.optimization_barrier(
+        ((dq, dk, dv, de, dw1, db1, dw2, db2), rear_part)
+    )
+    rear_sum = lax.psum(rear_part, "sp")
     dw2 = dw2 - jnp.mean(dw2, 1, keepdims=True)
     db2 = db2 - jnp.mean(db2, -1, keepdims=True)
     small = jnp.concatenate([db1[:, 0], db2[:, 0], dgn[:, 0], dsh[:, 0], jnp.zeros((slots, head), f32)], 1)
-    inner_rows = jnp.concatenate([dw1, dw2, pad_to(small.reshape(slots, 2, inner), 8, 1)], 1)
-    spread = jnp.zeros((local,) + inner_rows.shape[1:], f32)
-    for j in range(slots):
-        here = jnp.arange(local)[:, None, None] == half + j * groups
-        spread = spread + jnp.where(here, inner_rows[j][None], 0.0)
-    inner_sum = lax.psum(spread.astype(bf16), "fsdp").astype(f32)
+    inner_rows = jnp.concatenate([dw1, dw2, pad_to(small.reshape(slots, 2, inner), -(-(2 * head + 2) // S) * S - 2 * head, 1)], 1)
+    share = inner_rows.shape[1] // S
+    inner_send = inner_rows.astype(bf16).reshape(slots, S, share, 2, 128).transpose(1, 0, 3, 2, 4)
+    inner_send = inner_send.reshape(S, slots * 2 * share, 128)
 
     grads = jnp.stack([dq, dk, dv], 2).transpose(1, 0, 2, 3).reshape(S, piece, slots * span)
     rates_back = de[..., 0].astype(bf16).reshape(slots, S, piece).transpose(1, 0, 2)
-    arrived = swap(pack_tiles(pad_to(grads, tiles * 128, 2), rates_back), "fsdp")
+    packed_back = pack_tiles(pad_to(grads, tiles * 128, 2), rates_back)
+    used = packed_back.shape[1]
+    extent = -(-inner_send.shape[1] // 16) * 16
+    arrived = swap(jnp.concatenate([packed_back, pad_to(inner_send, extent, 1)], 1), "fsdp")
+    inner_part = arrived[:, used : used + inner_send.shape[1]].astype(f32)
+    inner_part = jnp.sum(inner_part.reshape(groups, micro, slots, 2, share, 128), 1)
+    inner_part = inner_part.transpose(1, 0, 3, 2, 4).reshape(slots * groups, share, 2 * 128)[:local]
+    inner_sum = lax.all_gather(inner_part.astype(bf16), "fsdp", axis=1, tiled=True).astype(f32)
     body = arrived[:, : tiles * piece].reshape(groups, micro, tiles, Z, rows, 128)
     body = body.transpose(3, 1, 4, 0, 2, 5).reshape(Z * total, groups, tiles * 128)
     back = arrived[:, tiles * piece : tiles * piece + rate_tiles].reshape(groups, micro, slots, Z, rows)
@@ -547,20 +552,25 @@
         packed_width,
         1,
     )
-    weight_grad = scatter_sum(tn(normed, grad_packed), "fsdp")
+    weight_parts = tn(normed, grad_packed).astype(bf16).reshape(S, own, packed_width)
+    weight_grad = jnp.sum(swap(weight_parts, "fsdp").astype(f32), 0)
+    rear_sum, weight_grad = lax.optimization_barrier((rear_sum, weight_grad))
+    rear_sum = rear_sum.astype(f32)
     weight_all = lax.all_gather(weight_grad.astype(bf16), "sp", axis=1).astype(f32)
     pieces = weight_all[..., :extra].reshape(own, Z, local, 3, head)
     pieces = jnp.stack([pieces[:, :, flat.index(g)] for g in range(local)], 2)
     query_grad, key_grad, value_grad = (pieces[:, :, :, i].reshape(own, width) for i in range(3))
     rate_grad = weight_all[..., extra : extra + local].reshape(own, Z * local)
-    grad_normed = scatter_sum(nt(grad_packed, front), "sp") + grad_normed_gate
+    normed_parts = nt(grad_packed, front).astype(bf16).reshape(Z, total, width)
+    grad_normed = jnp.sum(swap(normed_parts, "sp").astype(f32), 0) + grad_normed_gate
     own_scale = lax.dynamic_slice_in_dim(scale_one, z * total, total, 0)
     tokens_grad = (grad_middle + rms_back(grad_normed * pre_full, own_tokens, own_scale)).astype(bf16)
 
     out_grad = rear_sum[:, :width]
     gate_grad = rear_sum[:, width : 2 * width]
     fgate_grad = rear_sum[:, 2 * width : 2 * width + ff]
-    fup_grad = rear_sum[:, 2 * width + ff :]
+    fup_grad = rear_sum[:, 2 * width + ff : 2 * width + 2 * ff]
+    down_grad = rear_sum[:, 2 * width + 2 * ff :].reshape(-1, width)
 
     def row_dot(grad, weight):
         return jnp.sum(grad * weight.astype(f32), -1)
@@ -588,7 +598,7 @@
         post_grad,
         fgate_grad,
         fup_grad,
-        down_sum,
+        down_grad,
         inner_sum[:, :head],
         tail[:, :inner],
         inner_sum[:, head : 2 * head].transpose(0, 2, 1),

time: 710 us -> 519 us (0.73)
  waiting for transfers between devices: 338 us -> 94.6 us
  blocking collectives: 27.7 us -> 62.6 us
  Pallas kernels: 169 us -> 155 us
  local copies, waits for them, and re-layouts: 58.1 us -> 70.9 us
  starting transfers between devices: 15.1 us -> 24.5 us
  other arithmetic: 32.9 us -> 41.7 us
    reduce_scatter x4 -> x1, waiting for transfers between devices: 174 us -> 5.52 us  [shards(): lax.psum_scatter(rear_grad, 'fsdp', scatter_dimension=0, tiled=True)]
    psum x2 -> x1, waiting for transfers between devices: 64.5 us -> 2.71 us  [shards(): rear_sum = lax.psum(rear_part, 'sp')]
    all_gather x1, blocking collectives: 15.4 us -> 41.8 us  [shards(): lax.all_gather(weight_grad.astype(bf16), 'sp', axis=1).astype(f32)]
    all_to_all x4 -> x6, waiting for transfers between devices: 74.5 us -> 61.9 us  [swap(): return lax.all_to_all(block, axes, split_axis=0, concat_axis=0, tiled=True)]
    pallas_call x1, Pallas kernels: 93.8 us -> 82.6 us  [bwd_call(): pl.pallas_call(functools.partial(bwd_kernel, slots, count, unroll), grid=...]
    all_to_all x4 -> x6, starting transfers between devices: 14.5 us -> 23.9 us  [swap(): return lax.all_to_all(block, axes, split_axis=0, concat_axis=0, tiled=True)]
    all_gather x0 -> x1, blocking collectives: none -> 8.4 us  [shards(): lax.all_gather(inner_part.astype(bf16), 'fsdp', axis=1, tiled=True)]
    unnamed x142 -> x136, local copies, waits for them, and re-layouts: 13.8 us -> 16.5 us
  transfers between devices with their start and end apart: 13 -> 11, of which waited for: 10 -> 7; matrix products, arithmetic and copies ran while one was open for 13% -> 22% of each run, Pallas kernels for 11% -> 30%
where the time goes in v2:
time: 519 us; the launch traced here: 510 us
  Pallas kernels  155 us (30%)
  waiting for transfers between devices  94.6 us (18%)
  local copies, waits for them, and re-layouts  70.9 us (14%)
  blocking collectives  62.6 us (12%)
  matrix products  45.6 us (9%)
  other arithmetic  41.7 us (8%)
  starting transfers between devices  24.5 us (5%)
  between operations  15.4 us (3%)
    pallas_call x1, Pallas kernels, bwd_call(): pl.pallas_call(functools.partial(bwd_kernel, slots, count, unroll), grid=...  82.6 us
    pallas_call x1, Pallas kernels, fwd_call(): pl.pallas_call(functools.partial(fwd_kernel, slots, count, unroll), grid=...  72.3 us
    all_to_all x6, waiting for transfers between devices, swap(): return lax.all_to_all(block, axes, split_axis=0, concat_axis=0, tiled=True)  61.9 us
    all_gather x1, blocking collectives, shards(): lax.all_gather(weight_grad.astype(bf16), 'sp', axis=1).astype(f32)  41.8 us
    all_to_all x6, starting transfers between devices, swap(): return lax.all_to_all(block, axes, split_axis=0, concat_axis=0, tiled=True)  23.9 us
    all_gather x1, waiting for transfers between devices, shards(): all_tokens = lax.all_gather(tokens[:, 0], 'sp', axis=0)  23.7 us
    dot_general x6, matrix products, nn(): lax.dot_general(x.astype(bf16), y.astype(bf16), (((1,), (0,)), ((), ())),...  16.9 us
    unnamed x136, local copies, waits for them, and re-layouts  16.5 us
  transfers between devices with their start and end apart: 11, of which 7 were waited for; matrix products, arithmetic and copies ran while one was open for 22% of the time, Pallas kernels for 30%

profile of v2, /device:TPU:0, one launch (start us, length us, event | category | flops | bytes accessed | tf_op | source)
XLA Modules:
  0.0 510.3 jit_solution(12685101444825031342)
XLA Ops:
  13.3 12.4 %all_gather.21 = bf16[768,640]{1,0:T(8,128)(2,1)S(1)} all-gather(bf16[96,640]{1,0:T(8,128)(2,1)S(1)} %pad.33.clone), channel_id=1, replica_groups=mesh['sp'=4,'fsdp'=8] {'fsdp'}, dimensions={0}, use_global_device_ids=true | all-gather | bytes 1105920 | tf_op jit(solution)/shard_map/all_gather | solution.py:325
  25.7 23.7 %all-gather.10.cloned.1.call-done = bf16[16,1,64,768]{3,2,1,0:T(8,128)(2,1)} async-done(((bf16[4,1,64,768]{3,2,1,0:T(8,128)(2,1)}), bf16[16,1,64,768]{3,2,1,0:T(8,128)(2,1)}) %all-gather.10.cloned.1.call-update) | async-done | bytes 1572880 | tf_op jit(solution)/shard_map/all_gather | solution.py:394
  59.1 2.5 fusion.65
  64.6 3.9 reshape_reshape.6
  70.3 3.8 all-to-all-start
  78.0 21.0 %all-to-all-done = bf16[8,784,128]{2,1,0:T(8,128)(2,1)S(1)} async-done(((bf16[8,784,128]{2,1,0:T(8,128)(2,1)}), bf16[8,784,128]{2,1,0:T(8,128)(2,1)S(1)}, u32[]{:S(2)}, u32[]{:S(2)}) %all-to-all-start) | async-done | bytes 1605664 | tf_op jit(solution)/shard_map/all_to_all | solution.py:329
  105.4 72.3 %inner_forward.1 = (bf16[2,2048,64]{2,1,0:T(8,128)(2,1)}, bf16[2,128,64,256]{3,2,1,0:T(8,128)(2,1)}, bf16[2,128,64,256]{3,2,1,0:T(8,128)(2,1)}, bf16[2,2048,256]...) custom-call(bf16[2,2048,64]{2,1,0:T(8,128)(2,1)} %pad_maximum_fusion, ...), custom_call_target="tpu_custom_call" | custom-call | flops 89999998976 | bytes 40000000 | tf_op jit(solution)/shard_map/inner_forward/pallas_call | solution.py:153
  181.5 3.9 all-to-all-start.1
  185.7 14.0 %all-to-all-done.1 = bf16[32,64,128]{2,1,0:T(8,128)(2,1)S(1)} async-done(((bf16[32,64,128]{2,1,0:T(8,128)(2,1)}), bf16[32,64,128]{2,1,0:T(8,128)(2,1)S(1)}, u32[]{:S(2)}, u32[]{:S(2)}) %all-to-all-start.1) | async-done | bytes 524320 | tf_op jit(solution)/shard_map/all_to_all | solution.py:329
  202.2 4.2 fusion.66
  208.6 2.6 multiply_reduce_fusion.4
  211.4 3.2 fusion.10
  214.6 2.7 multiply_convert_fusion.1
  225.4 4.2 all-to-all-start.2
  238.4 4.5 reshape.358
  242.9 4.1 fusion.4
  247.0 2.8 fusion.3
  255.5 82.6 %inner_backward.1 = (bf16[2,2048,64]{2,1,0:T(8,128)(2,1)}, bf16[2,2048,64]{2,1,0:T(8,128)(2,1)}, bf16[2,2048,64]{2,1,0:T(8,128)(2,1)}, f32[2,2048,1]{2,1,0:T(8,1...) custom-call(bf16[2,2048,64]{2,1,0:T(8,128)(2,1)} %pad_maximum_fusion, ...), custom_call_target="tpu_custom_call" | custom-call | flops 109999996928 | bytes 40000000 | tf_op jit(solution)/shard_map/inner_backward/pallas_call | solution.py:306
  339.5 5.5 %reduce-scatter.2.cloned.1.call-done = bf16[96,7680]{1,0:T(8,128)(2,1)} async-done(((bf16[768,7680]{1,0:T(8,128)(2,1)}), bf16[96,7680]{1,0:T(8,128)(2,1)}) %reduce-scatter.2.cloned.1.call-update) | async-done | bytes 1474576 | tf_op jit(solution)/shard_map/reduce_scatter | solution.py:515
  352.5 2.6 maximum_bitcast_fusion
  362.1 3.7 all-to-all-start.3
  366.2 3.8 fusion.32
  370.1 18.8 %all-to-all-done.3 = bf16[8,864,128]{2,1,0:T(8,128)(2,1)S(1)} async-done(((bf16[8,864,128]{2,1,0:T(8,128)(2,1)}), bf16[8,864,128]{2,1,0:T(8,128)(2,1)S(1)}, u32[]{:S(2)}, u32[]{:S(2)}) %all-to-all-start.3) | async-done | bytes 1769504 | tf_op jit(solution)/shard_map/all_to_all | solution.py:329
  398.6 8.4 %all_gather.27 = bf16[3,136,256]{2,0,1:T(4,128)(2,1)S(1)} all-gather(bf16[3,17,256]{2,0,1:T(4,128)(2,1)S(1)} %bitcast.240), channel_id=1, replica_groups=mesh['sp'=4,'fsdp'=8] {'fsdp'}, dimensions={1}, use_global_device_ids=true | all-gather | bytes 235008 | tf_op jit(solution)/shard_map/all_gather | solution.py:542
  408.9 3.6 convolution_convert_fusion.6
  412.5 3.7 all-to-all-start.5
  418.9 3.9 convolution_convert_fusion.3
  422.8 8.0 %all-to-all-done.5 = bf16[8,96,640]{2,1,0:T(8,128)(2,1)S(1)} async-done(((bf16[8,96,640]{2,1,0:T(8,128)(2,1)}), bf16[8,96,640]{2,1,0:T(8,128)(2,1)S(1)}, u32[]{:S(2)}, u32[]{:S(2)}) %all-to-all-start.5) | async-done | bytes 983072 | tf_op jit(solution)/shard_map/all_to_all | solution.py:329
  430.8 4.6 all-to-all-start.4
  435.6 2.7 all-reduce.11.cloned.1.call-done
  438.3 41.8 %all-gather.1 = bf16[96,2560]{1,0:T(8,128)(2,1)S(1)} all-gather(bf16[96,640]{1,0:T(8,128)(2,1)S(1)} %convert_reduce_fusion.1), channel_id=3, replica_groups=mesh['sp'=4,'fsdp'=8] {'sp'}, dimensions={1}, use_global_device_ids=true | all-gather | bytes 614400 | tf_op jit(solution)/shard_map/all_gather | solution.py:559
  488.6 2.7 multiply_reduce_fusion.1
  (299 shorter events, 112.6 us)
Async XLA Ops:
  7.2 42.2 %all-gather.10.cloned.1.call-start = ((), (), s32[]{:S(2)}) async-start(), calls=%async_computation.11 | async-start | bytes 1966080 | tf_op jit(solution)/shard_map/all_gather | solution.py:394
  7.9 41.6 %copy-start.49 = (f32[3,256]{1,0:T(4,128)S(1)}, f32[3,256]{1,0:T(4,128)}, u32[]{:S(2)}) copy-start(f32[3,256]{1,0:T(4,128)} %param.35) | copy-start | bytes 9220
  7.9 42.2 %copy-start.50 = (f32[3,64]{1,0:T(4,128)S(1)}, f32[3,64]{1,0:T(4,128)}, u32[]{:S(2)}) copy-start(f32[3,64]{1,0:T(4,128)} %param.39) | copy-start | bytes 2308
  7.9 42.2 %copy-start.51 = (f32[3,64]{1,0:T(4,128)S(1)}, f32[3,64]{1,0:T(4,128)}, u32[]{:S(2)}) copy-start(f32[3,64]{1,0:T(4,128)} %param.38) | copy-start | bytes 2308
  8.0 42.7 %copy-start.35 = (f32[3,256,64]{1,2,0:T(8,128)S(1)}, f32[3,256,64]{1,2,0:T(8,128)}, u32[]{:S(2)}) copy-start(f32[3,256,64]{1,2,0:T(8,128)} %param.36) | copy-start | bytes 589828
  8.0 194.2 %all-gather.8.cloned.1.call-start = ((), (), s32[]{:S(2)}) async-start(), calls=%async_computation.8 | async-start | bytes 3538944 | tf_op jit(solution)/shard_map/all_gather | solution.py:325
  9.1 42.2 %copy-start.23 = (bf16[96,768]{0,1:T(8,128)(2,1)}, bf16[96,768]{0,1:T(8,128)(2,1)S(1)}, u32[]{:S(2)}) copy-start(bf16[96,768]{0,1:T(8,128)(2,1)S(1)} %copy.250) | copy-start | bytes 442372
  10.3 41.0 %copy-start.25 = (bf16[96,768]{0,1:T(8,128)(2,1)}, bf16[96,768]{0,1:T(8,128)(2,1)S(1)}, u32[]{:S(2)}) copy-start(bf16[96,768]{0,1:T(8,128)(2,1)S(1)} %copy.252) | copy-start | bytes 442372
  11.5 39.8 %copy-start.24 = (bf16[96,768]{0,1:T(8,128)(2,1)}, bf16[96,768]{0,1:T(8,128)(2,1)S(1)}, u32[]{:S(2)}) copy-start(bf16[96,768]{0,1:T(8,128)(2,1)S(1)} %copy.251) | copy-start | bytes 442372
  13.2 42.7 %copy-start.19 = (bf16[96,2048]{1,0:T(8,128)(2,1)S(1)}, bf16[96,2048]{1,0:T(8,128)(2,1)}, u32[]{:S(2)}) copy-start(bf16[96,2048]{1,0:T(8,128)(2,1)} %param.32) | copy-start | bytes 1179652
  13.3 42.7 %copy-start.20 = (bf16[96,2048]{1,0:T(8,128)(2,1)S(1)}, bf16[96,2048]{1,0:T(8,128)(2,1)}, u32[]{:S(2)}) copy-start(bf16[96,2048]{1,0:T(8,128)(2,1)} %param.31) | copy-start | bytes 1179652
  13.3 42.7 %copy-start.27 = (bf16[96,768]{1,0:T(8,128)(2,1)S(1)}, bf16[96,768]{1,0:T(8,128)(2,1)}, u32[]{:S(2)}) copy-start(bf16[96,768]{1,0:T(8,128)(2,1)} %param.27) | copy-start | bytes 442372
  25.7 33.4 %copy-start.16 = (bf16[768,640]{1,0:T(8,128)(2,1)}, bf16[768,640]{1,0:T(8,128)(2,1)S(1)}, u32[]{:S(2)}) copy-start(bf16[768,640]{1,0:T(8,128)(2,1)S(1)} %all_gather.21) | copy-start | bytes 2949124
  49.4 157.0 %all-gather.6.cloned.1.call-start = ((), (), s32[]{:S(2)}) async-start(), calls=%async_computation.7 | async-start | bytes 9732096 | tf_op jit(solution)/shard_map/all_gather | solution.py:325
  70.3 28.7 %all-to-all-start = ((bf16[8,784,128]{2,1,0:T(8,128)(2,1)}), bf16[8,784,128]{2,1,0:T(8,128)(2,1)S(1)}, u32[]{:S(2)}, u32[]{:S(2)}) async-start(bf16[8,784,128]{2,1,0:T(8,128)(2,1)} %fusion.22), calls=%async_computation | async-start | bytes 3211264 | tf_op jit(solution)/shard_map/all_to_all | solution.py:329
  177.8 7.6 %copy-start.53 = (s32[4]{0:T(128)S(1)}, s32[4]{0:T(128)}, u32[]{:S(2)}) copy-start(s32[4]{0:T(128)} %param.21) | copy-start | bytes 52
  177.8 7.7 %copy-start.21 = (bf16[4,1,64,768]{3,2,1,0:T(8,128)(2,1)S(1)}, bf16[4,1,64,768]{3,2,1,0:T(8,128)(2,1)}, u32[]{:S(2)}) copy-start(bf16[4,1,64,768]{3,2,1,0:T(8,128)(2,1)} %param.22) | copy-start | bytes 1179652
  181.5 18.2 %all-to-all-start.1 = ((bf16[32,64,128]{2,1,0:T(8,128)(2,1)}), bf16[32,64,128]{2,1,0:T(8,128)(2,1)S(1)}, u32[]{:S(2)}, u32[]{:S(2)}) async-start(bf16[32,64,128]{2,1,0:T(8,128)(2,1)} %reshape.350), calls=%async_computation.1 | async-start | bytes 1048576 | tf_op jit(solution)/shard_map/all_to_all | solution.py:329
  185.7 16.5 %copy-start.8 = (bf16[256,768]{1,0:T(8,128)(2,1)}, bf16[256,768]{1,0:T(8,128)(2,1)S(1)}, u32[]{:S(2)}) copy-start(bf16[256,768]{1,0:T(8,128)(2,1)S(1)} %fusion.47) | copy-start | bytes 1179652
  206.5 8.1 %copy-start.32 = (bf16[768,5632]{1,0:T(8,128)(2,1)S(1)}, bf16[768,5632]{1,0:T(8,128)(2,1)}, u32[]{:S(2)}) copy-start(bf16[768,5632]{1,0:T(8,128)(2,1)} %all-gather.6.cloned.1.call-done) | copy-start | bytes 25952260
  211.2 8.5 %copy-start.12 = (f32[256,768]{1,0:T(8,128)}, f32[256,768]{1,0:T(8,128)S(1)}, u32[]{:S(2)}) copy-start(f32[256,768]{1,0:T(8,128)S(1)} %get-tuple-element.272) | copy-start | bytes 2359300
  225.4 26.5 %all-to-all-start.2 = ((bf16[32,64,128]{2,1,0:T(8,128)(2,1)}), bf16[32,64,128]{2,1,0:T(8,128)(2,1)}, u32[]{:S(2)}, u32[]{:S(2)}) async-start(bf16[32,64,128]{2,1,0:T(8,128)(2,1)} %reshape.356), calls=%async_computation.2 | async-start | bytes 1048576 | tf_op jit(solution)/shard_map/all_to_all | solution.py:329
  229.6 115.4 %reduce-scatter.2.cloned.1.call-start = ((), (), s32[]{:S(2)}) async-start(), calls=%async_computation.9 | async-start | bytes 13271040 | tf_op jit(solution)/shard_map/reduce_scatter | solution.py:515
  362.1 26.8 %all-to-all-start.3 = ((bf16[8,864,128]{2,1,0:T(8,128)(2,1)}), bf16[8,864,128]{2,1,0:T(8,128)(2,1)S(1)}, u32[]{:S(2)}, u32[]{:S(2)}) async-start(bf16[8,864,128]{2,1,0:T(8,128)(2,1)} %fusion.21), calls=%async_computation.4 | async-start | bytes 3538944 | tf_op jit(solution)/shard_map/all_to_all | solution.py:329
  365.8 72.4 %all-reduce.11.cloned.1.call-start = ((), (), s32[]{:S(2)}) async-start(), calls=%async_computation.10 | async-start | bytes 2949120 | tf_op jit(solution)/shard_map/psum | solution.py:524
  396.0 12.0 %copy-start.34 = (f32[1024,3]{0,1:T(4,128)S(1)}, f32[1024,3]{0,1:T(4,128)}, u32[]{:S(2)}) copy-start(f32[1024,3]{0,1:T(4,128)} %copy-done.33) | copy-start | bytes 36868
  396.0 12.9 %copy-start.14 = (bf16[1024,768]{1,0:T(8,128)(2,1)S(1)}, bf16[1024,768]{1,0:T(8,128)(2,1)}, u32[]{:S(2)}) copy-start(bf16[1024,768]{1,0:T(8,128)(2,1)} %copy-done.13) | copy-start | bytes 4718596
  397.3 15.2 %copy-start.26 = (bf16[1024,384]{1,0:T(8,128)(2,1)}, bf16[1024,384]{1,0:T(8,128)(2,1)S(1)}, u32[]{:S(2)}) copy-start(bf16[1024,384]{1,0:T(8,128)(2,1)S(1)} %slice_bitcast_fusion) | copy-start | bytes 2359300
  412.5 18.3 %all-to-all-start.5 = ((bf16[8,96,640]{2,1,0:T(8,128)(2,1)}), bf16[8,96,640]{2,1,0:T(8,128)(2,1)S(1)}, u32[]{:S(2)}, u32[]{:S(2)}) async-start(bf16[8,96,640]{2,1,0:T(8,128)(2,1)} %bitcast.234), calls=%async_computation.6 | async-start | bytes 1966080 | tf_op jit(solution)/shard_map/all_to_all | solution.py:329
  430.8 69.2 %all-to-all-start.4 = ((bf16[4,256,768]{2,1,0:T(8,128)(2,1)}), bf16[4,256,768]{2,1,0:T(8,128)(2,1)S(1)}, u32[]{:S(2)}, u32[]{:S(2)}) async-start(bf16[4,256,768]{2,1,0:T(8,128)(2,1)} %bitcast.226), calls=%async_computation.5 | async-start | bytes 3145728 | tf_op jit(solution)/shard_map/all_to_all | solution.py:329
  481.5 12.1 %copy-start.39 = (f32[96,12]{0,1:T(8,128)}, f32[96,12]{0,1:T(8,128)S(1)}, u32[]{:S(2)}) copy-start(f32[96,12]{0,1:T(8,128)S(1)} %reshape.372) | copy-start | bytes 13828
  491.3 8.2 %copy-start.43 = (bf16[96]{0:T(256)(128)(2,1)S(1)}, bf16[96]{0:T(256)(128)(2,1)}, u32[]{:S(2)}) copy-start(bf16[96]{0:T(256)(128)(2,1)} %param.23) | copy-start | bytes 580
  (36 other events, 132.3 us)
Sparse Core Ops, SparseCore 0:
  9.6 39.7 all-gather.9
  51.3 34.7 all-gather.7
  88.0 66.4 all-gather.5
  255.6 89.3 reduce-scatter.1
  370.2 68.0 all-reduce.10

commit v3 on v2

--- a/solution.py
+++ b/solution.py
@@ -52,14 +52,29 @@
     lower=lax.broadcasted_iota(jnp.int32,(MINI,MINI),0)>=lax.broadcasted_iota(jnp.int32,(MINI,MINI),1)
     return lower.astype(f32), jnp.where(lower,0.0,1.0)
 
-def fwd_kernel(slots,count,unroll,q_ref,k_ref,v_ref,e_ref,w1_ref,b1_ref,w2_ref,b2_ref,gain_ref,shift_ref,
-    mix_ref,w1s_ref,w2s_ref,z1_ref,h_ref,q1_ref,n_ref,g_ref,nq_ref,
+def fwd_kernel(slots,count,unroll,piece,tiles,x_ref,w1_ref,b1_ref,w2_ref,b2_ref,gain_ref,shift_ref,
+    mix_ref,q_ref,k_ref,v_ref,e_ref,w1s_ref,w2s_ref,z1_ref,h_ref,q1_ref,n_ref,g_ref,nq_ref,
     W1,B1,W2,B2,Z,ZQ,AP,EP):
     lower,upper=masks()
     steps=q_ref.shape[1]//MINI
     pid=pl.program_id(0)
     @pl.when(pid==0)
     def _():
+        eye=lax.broadcasted_iota(jnp.int32,(128,128),0)==lax.broadcasted_iota(jnp.int32,(128,128),1)
+        @pl.loop(0,x_ref.shape[0])
+        def _(src):
+            base=pl.multiple_of(src*piece,piece)
+            for j in range(slots):
+                for index,ref in enumerate((q_ref,k_ref,v_ref)):
+                    lane=(3*j+index)*64
+                    top=lane//128*piece
+                    ref[j,pl.ds(base,piece)]=x_ref[src,top:top+piece,lane%128:lane%128+64]
+            rates=x_ref[src,tiles*piece:tiles*piece+16].astype(f32)
+            for j in range(slots):
+                for i in range(piece//128):
+                    n=j*(piece//128)+i
+                    column=jnp.sum(jnp.where(eye,rates[n:n+1],0.0),1,keepdims=True)
+                    e_ref[j,pl.ds(base+i*128,128)]=column
         for j in range(slots):
             W1[j]=w1_ref[j]; B1[j]=b1_ref[j]; W2[j]=w2_ref[j]; B2[j]=b2_ref[j]
             Z[j]=nn(k_ref[j,:MINI],w1_ref[j])+b1_ref[j]
@@ -124,7 +139,7 @@
         sq=lax.rsqrt(vq-mq*mq+EPS)
         Nq=sq*(Q2-mq)
         Qp=q_ref[j,prow].astype(f32)
-        mix_ref[j,prow]=(Qp+Nq*gain+shift).astype(bf16)
+        mix_ref[prow,64*j:64*j+64]=(Qp+Nq*gain+shift).astype(bf16)
         nq_ref[j,prow]=(Q2-mq).astype(bf16)
     @pl.loop(0,count//unroll)
     def _(i):
@@ -139,40 +154,52 @@
             mq=rs(Q2); vq=rs(Q2*Q2)
             sq=lax.rsqrt(vq-mq*mq+EPS)
             Nq=sq*(Q2-mq)
-            mix_ref[j,prow]=(q_ref[j,prow].astype(f32)+Nq*gain_ref[j]+shift_ref[j]).astype(bf16)
+            mix_ref[prow,64*j:64*j+64]=(q_ref[j,prow].astype(f32)+Nq*gain_ref[j]+shift_ref[j]).astype(bf16)
             nq_ref[j,prow]=(Q2-mq).astype(bf16)
 
-def fwd_call(q,k,v,e,w1,b1,w2,b2,gain,shift,block=256,unroll=1,**kw):
-    slots,length,_=q.shape
+def fwd_call(x,w1,b1,w2,b2,gain,shift,piece,tiles,block=256,unroll=2,**kw):
+    slots=w1.shape[0]; length=x.shape[0]*piece
     count=block//MINI; nb=length//block; steps=length//MINI
     row=lambda w: pl.BlockSpec((slots,block,w),lambda i:(0,i,0))
     full=lambda s: pl.BlockSpec(s,lambda i:(0,)*len(s),pipeline_mode=pl.Buffered(1))
-    r64=full((slots,length,64)); r1=full((slots,length,1))
+    r64=full((slots,length,64)); r1=full((slots,length,1)); rm_=full((length,64*slots))
     st=pl.BlockSpec((slots,count,64,256),lambda i:(0,i,0,0))
     S=jax.ShapeDtypeStruct
-    return pl.pallas_call(functools.partial(fwd_kernel,slots,count,unroll),
+    return pl.pallas_call(functools.partial(fwd_kernel,slots,count,unroll,piece,tiles),
         grid=(nb,),
-        in_specs=[r64]*3+[r1]+[full(a.shape) for a in (w1,b1,w2,b2,gain,shift)],
-        out_specs=[r64,st,st,row(256),row(256),row(256),r64,r64,r64],
-        out_shape=[S((slots,length,64),bf16),S((slots,steps,64,256),bf16),S((slots,steps,64,256),bf16)]+[S((slots,length,256),bf16)]*3+[S((slots,length,64),bf16)]*3,
+        in_specs=[full(a.shape) for a in (x,w1,b1,w2,b2,gain,shift)],
+        out_specs=[rm_,r64,r64,r64,r1,st,st,row(256),row(256),row(256),r64,r64,r64],
+        out_shape=[S((length,64*slots),bf16)]+[S((slots,length,64),bf16)]*3+[S((slots,length,1),f32)]+[S((slots,steps,64,256),bf16)]*2+[S((slots,length,256),bf16)]*3+[S((slots,length,64),bf16)]*3,
         scratch_shapes=[pltpu.VMEM((slots,64,256),f32),pltpu.VMEM((slots,1,256),f32),pltpu.VMEM((slots,64,256),f32),pltpu.VMEM((slots,1,64),f32),pltpu.VMEM((slots,MINI,256),f32),pltpu.VMEM((slots,MINI,256),f32),pltpu.VMEM((slots,MINI,256),bf16),pltpu.VMEM((slots,MINI,64),bf16)],
         compiler_params=pltpu.CompilerParams(dimension_semantics=("arbitrary",),vmem_limit_bytes=VMEM_BYTES),
-        name="inner_forward",cost_estimate=pl.CostEstimate(flops=90_000_000_000,bytes_accessed=40_000_000,transcendentals=0),**kw)(q,k,v,e,w1,b1,w2,b2,gain,shift)
-
-
-def bwd_kernel(slots,count,unroll,q_ref,k_ref,v_ref,e_ref,do_ref,n_ref,g_ref,nq_ref,w1s_ref,w2s_ref,z1_ref,h_ref,q1_ref,gain_ref,shift_ref,
-    dq_ref,dk_ref,dv_ref,de_ref,dw1_ref,db1_ref,dw2_ref,db2_ref,dgn_ref,dsh_ref,
-    DW1,DB1,G2,DB2,KD,DGN,DSH,DGQ,DSQ,
+        name="inner_forward",cost_estimate=pl.CostEstimate(flops=90_000_000_000,bytes_accessed=40_000_000,transcendentals=0),**kw)(x,w1,b1,w2,b2,gain,shift)
+
+
+def bwd_kernel(slots,count,unroll,piece,tiles,q_ref,k_ref,v_ref,e_ref,dx_ref,n_ref,g_ref,nq_ref,w1s_ref,w2s_ref,z1_ref,h_ref,q1_ref,gain_ref,shift_ref,
+    out_ref,dw1_ref,db1_ref,dw2_ref,db2_ref,dgn_ref,dsh_ref,
+    do_ref,de_ref,    DW1,DB1,G2,DB2,KD,DGN,DSH,DGQ,DSQ,
     sA,sAd,sHA,sGZ,sE1,sE2,sW1,sW2,sR1,sR2,sDA,sQ1,sQ2,sAQ,sb1,sb2):
     lower,_=masks()
     steps=q_ref.shape[1]//MINI
     pid=pl.program_id(0); nb=pl.num_programs(0)
     @pl.when(pid==0)
     def _():
+        @pl.loop(0,out_ref.shape[0])
+        def _(src):
+            rows=pl.ds(pl.multiple_of(src*piece,piece),piece)
+            for j in range(slots):
+                do_ref[j,rows]=dx_ref[rows,64*j:64*j+64]
         for r in (DW1,DB1,G2,DB2,KD,DGN,DSH,DGQ,DSQ):
             r[...]=jnp.zeros(r.shape,r.dtype)
         for r in (sA,sAd,sHA,sGZ,sE1,sE2,sW1,sW2,sR1,sR2,sDA,sQ1,sQ2,sAQ,sb1,sb2):
             r[0]=jnp.zeros(r.shape[1:],r.dtype)
+    def put(j,index,t,value):
+        t=jnp.minimum(t,steps-1)
+        lane=(3*j+index)*64
+        top=lane//128*piece
+        part=piece//MINI
+        rows=pl.ds(pl.multiple_of(top+lax.rem(t,part)*MINI,MINI),MINI)
+        out_ref[lax.div(t,part),rows,lane%128:lane%128+64]=value.astype(bf16)
     def crit(j,p,t):
         rows=pl.ds(pl.multiple_of(jnp.minimum(t,steps-1)*MINI,MINI),MINI)
         prow=pl.ds(pl.multiple_of(jnp.maximum(t-1,0)*MINI,MINI),MINI)
@@ -225,7 +252,7 @@
         G2[j]=G2f+tn(cat(sQ2[p,j],g_ref[j,rows],dZb),cat(sAQ[p,j],dHb,Ab))
         DB2[j]=DB2[j]+sb2[p,j]+jnp.sum(dZc,0,keepdims=True)
         dQs=nn(X1,K); dKs=tn(X1,Q)
-        dv_ref[j,rows]=(-dT).astype(bf16)
+        put(j,2,t,-dT)
         dO=do_ref[j,rows].astype(f32)
         DGN[j]=DGN[j]+da*(2.0*gain*N+T)
         DSH[j]=DSH[j]+dT
@@ -240,8 +267,8 @@
         DB1[j]=DB1[j]+sb1[p,j]+jnp.sum(dZ1,0,keepdims=True)
         yield
         qk=nt(dd,sW1[p,j])
-        dq_ref[j,rows]=(dO+qk[:MINI]-dQs).astype(bf16)
-        dk_ref[j,rows]=(qk[MINI:]-dKs-a3+dT).astype(bf16)
+        put(j,0,t,dO+qk[:MINI]-dQs)
+        put(j,1,t,qk[MINI:]-dKs-a3+dT)
     def qside(j,p,t,i):
         rows=pl.ds(pl.multiple_of(t*MINI,MINI),MINI)
         brow=pl.ds(pl.multiple_of(i*MINI,MINI),MINI)
@@ -289,11 +316,20 @@
     @pl.when(pid==nb-1)
     def _():
         interleave([crit(j,0,jnp.int32(0)) for j in range(slots)])
+        eye=lax.broadcasted_iota(jnp.int32,(128,128),0)==lax.broadcasted_iota(jnp.int32,(128,128),1)
+        @pl.loop(0,out_ref.shape[0])
+        def _(dst):
+            base=pl.multiple_of(dst*piece,piece)
+            rows=[jnp.sum(jnp.where(eye,de_ref[j,pl.ds(base+i*128,128)],0.0),0,keepdims=True) for j in range(slots) for i in range(piece//128)]
+            rows.append(jnp.zeros((16-len(rows),128),f32))
+            out_ref[dst,tiles*piece:tiles*piece+16]=cat(*rows).astype(bf16)
+            if tiles*128>slots*192:
+                out_ref[dst,(tiles-1)*piece:tiles*piece,(slots*192)%128:]=jnp.zeros((piece,128-(slots*192)%128),bf16)
         for j in range(slots):
             dw1_ref[j]=DW1[j]; db1_ref[j]=DB1[j]; dw2_ref[j]=G2[j]; db2_ref[j]=DB2[j]
             dgn_ref[j]=jnp.sum(DGN[j]+DGQ[j],0,keepdims=True); dsh_ref[j]=jnp.sum(DSH[j]+DSQ[j],0,keepdims=True)
 
-def bwd_call(q,k,v,e,dO,n,g,nq,w1s,w2s,z1,h,q1,gain,shift,block=256,unroll=2,**kw):
+def bwd_call(q,k,v,e,dO,n,g,nq,w1s,w2s,z1,h,q1,gain,shift,piece,tiles,block=256,unroll=2,**kw):
     slots,length,_=q.shape
     count=block//MINI; nb=length//block; steps=length//MINI
     row=lambda w: pl.BlockSpec((slots,block,w),lambda i:(0,nb-1-i,0))
@@ -301,14 +337,14 @@
     r64=full((slots,length,64)); r1=full((slots,length,1))
     st=pl.BlockSpec((slots,count,64,256),lambda i:(0,nb-1-i,0,0))
     S=jax.ShapeDtypeStruct
-    outs=[((slots,64,256),f32),((slots,1,256),f32),((slots,64,256),f32),((slots,1,64),f32),((slots,1,64),f32),((slots,1,64),f32)]
+    outs=[((length//piece,tiles*piece+16,128),bf16),((slots,64,256),f32),((slots,1,256),f32),((slots,64,256),f32),((slots,1,64),f32),((slots,1,64),f32),((slots,1,64),f32)]
     V=lambda *s,d=f32: pltpu.VMEM(s,d)
-    return pl.pallas_call(functools.partial(bwd_kernel,slots,count,unroll),
+    return pl.pallas_call(functools.partial(bwd_kernel,slots,count,unroll,piece,tiles),
         grid=(nb,),
-        in_specs=[r64]*3+[r1]+[r64]*4+[st,st]+[row(256)]*3+[full(gain.shape)]*2,
-        out_specs=[r64]*3+[r1]+[full(o[0]) for o in outs],
-        out_shape=[S((slots,length,64),bf16)]*3+[S((slots,length,1),f32)]+[S(*o) for o in outs],
-        scratch_shapes=[V(slots,64,256),V(slots,1,256),V(slots,64,256),V(slots,1,64),V(slots,MINI,256),V(slots,MINI,64),V(slots,MINI,64),V(slots,MINI,64),V(slots,MINI,64),
+        in_specs=[r64]*3+[r1,full(dO.shape)]+[r64]*3+[st,st]+[row(256)]*3+[full(gain.shape)]*2,
+        out_specs=[full(o[0]) for o in outs],
+        out_shape=[S(*o) for o in outs],
+        scratch_shapes=[V(slots,length,64,d=bf16),V(slots,length,1),V(slots,64,256),V(slots,1,256),V(slots,64,256),V(slots,1,64),V(slots,MINI,256),V(slots,MINI,64),V(slots,MINI,64),V(slots,MINI,64),V(slots,MINI,64),
           V(2,slots,MINI,256,d=bf16),V(2,slots,MINI,256),V(2,slots,MINI,256),V(2,slots,MINI,256),V(2,slots,MINI,256,d=bf16),V(2,slots,MINI,64,d=bf16),
           V(2,slots,64,256,d=bf16),V(2,slots,64,256,d=bf16),V(2,slots,MINI,256),V(2,slots,MINI,64),V(2,slots,MINI,256),V(2,slots,MINI,256,d=bf16),V(2,slots,MINI,64,d=bf16),V(2,slots,MINI,256,d=bf16),V(2,slots,1,256),V(2,slots,1,64)],
         compiler_params=pltpu.CompilerParams(dimension_semantics=("arbitrary",),vmem_limit_bytes=VMEM_BYTES),
@@ -333,6 +369,112 @@
     widths = [(0, 0)] * array_in.ndim
     widths[dim] = (0, size - array_in.shape[dim])
     return jnp.pad(array_in, widths)
+
+
+def back_kernel(layout, piece, tiles, a_ref, slope_ref, front_ref, grad_ref, parts_ref):
+    micro_step = pl.program_id(0)
+    groups, slots, local, micro = layout["groups"], layout["slots"], layout["local"], layout["micro"]
+    eye = lax.broadcasted_iota(jnp.int32, (128, 128), 0) == lax.broadcasted_iota(jnp.int32, (128, 128), 1)
+    lanes = lax.broadcasted_iota(jnp.int32, (piece, 64), 1)
+    rates = jnp.zeros((piece, 64), f32)
+    for h, part in enumerate(layout["order"]):
+        block = a_ref[h * micro + micro_step, tiles * piece : tiles * piece + 16].astype(f32)
+        for j, g in enumerate(part):
+            column = []
+            for i in range(piece // 128):
+                n = j * (piece // 128) + i
+                column.append(jnp.sum(jnp.where(eye, block[n : n + 1], 0.0), 1, keepdims=True))
+            rates = jnp.where(lanes == g, cat(*column), rates)
+    slope = slope_ref[:, 0].reshape(piece, slope_ref.shape[-1])
+    rates = rates * slope[:, :64]
+    halves = []
+    for h, part in enumerate(layout["order"]):
+        for lane in range(0, len(part) * 192, 64):
+            halves.append((h, lane))
+    halves.append(None)
+    chunks = []
+    for n in range(0, len(halves), 2):
+        pair = halves[n : n + 2]
+        if pair[0] is not None and len(pair) == 2 and pair[1] is not None:
+            (h, lane), (h2, lane2) = pair
+            if h == h2 and lane % 128 == 0:
+                top = lane // 128 * piece
+                chunks.append(a_ref[h * micro + micro_step, top : top + piece])
+                continue
+        values = []
+        for half in pair:
+            if half is None:
+                values.append(rates.astype(bf16))
+            else:
+                h, lane = half
+                top = lane // 128 * piece
+                values.append(a_ref[h * micro + micro_step, top : top + piece, lane % 128 : lane % 128 + 64])
+        if len(values) == 1:
+            values.append(jnp.zeros((piece, 64), bf16))
+        chunks.append(jnp.concatenate(values, 1))
+    grad = jnp.concatenate(chunks, 1)
+    product = nt(grad, front_ref[...]).astype(bf16)
+    rows = piece // grad_ref.shape[0]
+    grad_ref[:, 0] = grad.reshape(grad_ref.shape[0], rows, grad.shape[1])
+    parts_ref[:, 0] = product.reshape(parts_ref.shape[0], rows, product.shape[1])
+
+
+def back_call(arrived, slope, front, layout, piece, tiles):
+    Z, micro, rows, _ = slope.shape
+    width = front.shape[0]
+    packed = front.shape[1]
+    full = lambda s: pl.BlockSpec(s, lambda i: (0,) * len(s), pipeline_mode=pl.Buffered(1))
+    step = lambda w: pl.BlockSpec((Z, 1, rows, w), lambda i: (0, i, 0, 0))
+    return pl.pallas_call(
+        functools.partial(back_kernel, layout, piece, tiles),
+        grid=(micro,),
+        in_specs=[full(arrived.shape), step(slope.shape[-1]), full(front.shape)],
+        out_specs=[step(packed), step(width)],
+        out_shape=[
+            jax.ShapeDtypeStruct((Z, micro, rows, packed), bf16),
+            jax.ShapeDtypeStruct((Z, micro, rows, width), bf16),
+        ],
+        compiler_params=pltpu.CompilerParams(dimension_semantics=("arbitrary",), vmem_limit_bytes=VMEM_BYTES),
+        name="projection_gradients",
+        cost_estimate=pl.CostEstimate(flops=1_000_000_000, bytes_accessed=8_000_000, transcendentals=0),
+    )(arrived, slope, front)
+
+
+def finish_kernel(layout, all_ref, q_ref, k_ref, v_ref, dq_ref, dk_ref, dv_ref, dr_ref, dot_ref):
+    local = layout["local"]
+    flat = layout["flat"]
+    Z = all_ref.shape[0]
+    own = dq_ref.shape[0]
+    dot = jnp.zeros((own, 1), f32)
+    rate = jnp.zeros((own, dr_ref.shape[1]), f32)
+    lanes = lax.broadcasted_iota(jnp.int32, rate.shape, 1)
+    for index, (weight, out) in enumerate(((q_ref, dq_ref), (k_ref, dk_ref), (v_ref, dv_ref))):
+        for z in range(Z):
+            for g in range(local):
+                start = (flat.index(g) * 3 + index) * 64
+                value = all_ref[z, :, start : start + 64].astype(f32)
+                place = (z * local + g) * 64
+                out[:, place : place + 64] = value
+        dot = dot + jnp.sum(out[...] * weight[...].astype(f32), 1, keepdims=True)
+    for z in range(Z):
+        for g in range(local):
+            n = local * 192 + g
+            rate = jnp.where(lanes == z * local + g, all_ref[z, :, n : n + 1].astype(f32), rate)
+    dr_ref[...] = rate
+    dot_ref[...] = dot
+
+
+def finish_call(gathered, q_w, k_w, v_w, layout):
+    own, width = q_w.shape
+    Z = gathered.shape[0]
+    shapes = [(own, width)] * 3 + [(own, Z * layout["local"]), (own, 1)]
+    return pl.pallas_call(
+        functools.partial(finish_kernel, layout),
+        out_shape=[jax.ShapeDtypeStruct(s, f32) for s in shapes],
+        compiler_params=pltpu.CompilerParams(vmem_limit_bytes=VMEM_BYTES),
+        name="weight_gradients",
+        cost_estimate=pl.CostEstimate(flops=10_000_000, bytes_accessed=2_000_000, transcendentals=0),
+    )(gathered, q_w, k_w, v_w)
 
 
 def shards(
@@ -402,6 +544,8 @@
     projected = nn(normed, front)
     rate_sig = jax.nn.sigmoid(projected[:, extra : extra + local])
     rate_rows = (RATE * rate_sig).astype(bf16).reshape(Z, micro, rows, local)
+    rate_slope = pad_to(RATE * rate_sig * (1.0 - rate_sig), 128, 1).reshape(Z, micro, rows, 128)
+    layout = dict(groups=groups, slots=slots, local=local, micro=micro, order=order, flat=flat)
     low = projected.astype(bf16).reshape(Z, micro, rows, packed_width)
     rate_tiles = slots * piece // 128
 
@@ -422,18 +566,6 @@
     send_low = jnp.stack(low_parts).transpose(0, 2, 1, 3, 4).reshape(S, piece, tiles * 128)
     send_rate = jnp.stack(rate_parts).transpose(0, 2, 4, 1, 3).reshape(S, slots, piece)
     arrived = swap(pack_tiles(send_low, send_rate), "fsdp")
-    body = arrived[:, : tiles * piece].reshape(S, tiles, piece, 128)
-
-    def chain_rows(index):
-        out = []
-        for j in range(slots):
-            lane = j * span + index * head
-            out.append(body[:, lane // 128, :, lane % 128 : lane % 128 + head].reshape(length, head))
-        return jnp.stack(out)
-
-    q, k, v = chain_rows(0), chain_rows(1), chain_rows(2)
-    e = arrived[:, tiles * piece : tiles * piece + rate_tiles].reshape(S, slots, piece)
-    e = e.transpose(1, 0, 2).reshape(slots, length, 1).astype(f32)
 
     half = d // micro
     heads_here = [jnp.minimum(half + j * groups, local - 1) for j in range(slots)]
@@ -449,7 +581,8 @@
     b2 = b2 - jnp.mean(b2, -1, keepdims=True)
     gain = of_slots(inner_gain)[:, None]
     shift = of_slots(inner_shift)[:, None]
-    mix, w1s, w2s, z1, h, q1, n, g_, nq = fwd_call(q, k, v, e, w1, b1, w2, b2, gain, shift, unroll=2)
+    mix, q, k, v, e, *saved = fwd_call(arrived, w1, b1, w2, b2, gain, shift, piece, tiles)
+    w1s, w2s, z1, h, q1, n, g_, nq = saved
 
     out_in, gate_in, fgate_in, fup_in, down_in = rear_in
     rear = gather(jnp.concatenate([out_in, gate_in, fgate_in, fup_in], 1))
@@ -460,8 +593,7 @@
     down_full = gather(down_in)
 
     def to_tokens(chains):
-        send = chains.reshape(slots, S, Z, rows, head).transpose(1, 2, 3, 0, 4)
-        got = swap(send.reshape(S * Z, rows, slots * head), ("fsdp", "sp"))
+        got = swap(chains.reshape(S * Z, rows, slots * head), ("fsdp", "sp"))
         got = got.reshape(groups, micro, Z, rows, slots, head).transpose(1, 3, 2, 4, 0, 5)
         return got.reshape(total, Z, slots * groups, head)[:, :, :local].reshape(total, width)
 
@@ -469,7 +601,7 @@
         send = pad_to(block.reshape(micro, rows, Z, local, head), slots * groups, 3)
         send = send.reshape(micro, rows, Z, slots, groups, head).transpose(4, 0, 2, 1, 3, 5)
         got = swap(send.reshape(S * Z, rows, slots * head), ("fsdp", "sp"))
-        return got.reshape(length, slots, head).transpose(1, 0, 2)
+        return got.reshape(length, slots * head)
 
     mixed_rows = to_tokens(mix).astype(f32)
     own_tokens = tokens.reshape(total, width).astype(f32)
@@ -515,12 +647,10 @@
     rear_part = lax.psum_scatter(rear_grad, "fsdp", scatter_dimension=0, tiled=True)
     grad_normed_gate = nt(grad_gate_logit, gate_full)
 
-    dq, dk, dv, de, dw1, db1, dw2, db2, dgn, dsh = bwd_call(
-        q, k, v, e, d_mix, n, g_, nq, w1s, w2s, z1, h, q1, gain, shift
+    packed_back, dw1, db1, dw2, db2, dgn, dsh = bwd_call(
+        q, k, v, e, d_mix, n, g_, nq, w1s, w2s, z1, h, q1, gain, shift, piece, tiles
     )
-    (dq, dk, dv, de, dw1, db1, dw2, db2), rear_part = lax.optimization_barrier(
-        ((dq, dk, dv, de, dw1, db1, dw2, db2), rear_part)
-    )
+    packed_back, rear_part = lax.optimization_barrier((packed_back, rear_part))
     rear_sum = lax.psum(rear_part, "sp")
     dw2 = dw2 - jnp.mean(dw2, 1, keepdims=True)
     db2 = db2 - jnp.mean(db2, -1, keepdims=True)
@@ -530,42 +660,17 @@
     inner_send = inner_rows.astype(bf16).reshape(slots, S, share, 2, 128).transpose(1, 0, 3, 2, 4)
     inner_send = inner_send.reshape(S, slots * 2 * share, 128)
 
-    grads = jnp.stack([dq, dk, dv], 2).transpose(1, 0, 2, 3).reshape(S, piece, slots * span)
-    rates_back = de[..., 0].astype(bf16).reshape(slots, S, piece).transpose(1, 0, 2)
-    packed_back = pack_tiles(pad_to(grads, tiles * 128, 2), rates_back)
-    used = packed_back.shape[1]
-    extent = -(-inner_send.shape[1] // 16) * 16
-    arrived = swap(jnp.concatenate([packed_back, pad_to(inner_send, extent, 1)], 1), "fsdp")
-    inner_part = arrived[:, used : used + inner_send.shape[1]].astype(f32)
-    inner_part = jnp.sum(inner_part.reshape(groups, micro, slots, 2, share, 128), 1)
-    inner_part = inner_part.transpose(1, 0, 3, 2, 4).reshape(slots * groups, share, 2 * 128)[:local]
-    inner_sum = lax.all_gather(inner_part.astype(bf16), "fsdp", axis=1, tiled=True).astype(f32)
-    body = arrived[:, : tiles * piece].reshape(groups, micro, tiles, Z, rows, 128)
-    body = body.transpose(3, 1, 4, 0, 2, 5).reshape(Z * total, groups, tiles * 128)
-    back = arrived[:, tiles * piece : tiles * piece + rate_tiles].reshape(groups, micro, slots, Z, rows)
-    back = back.transpose(3, 1, 4, 2, 0).reshape(Z * total, slots * groups)[:, :local].astype(f32)
-    grad_rate_logit = (back * RATE * rate_sig * (1.0 - rate_sig)).astype(bf16)
-    grad_packed = pad_to(
-        jnp.concatenate(
-            [body[:, i, : len(part) * span] for i, part in enumerate(order) if part] + [grad_rate_logit], 1
-        ),
-        packed_width,
-        1,
-    )
-    weight_parts = tn(normed, grad_packed).astype(bf16).reshape(S, own, packed_width)
-    weight_grad = jnp.sum(swap(weight_parts, "fsdp").astype(f32), 0)
-    rear_sum, weight_grad = lax.optimization_barrier((rear_sum, weight_grad))
+    arrived = swap(packed_back, "fsdp")
+    grad_packed, normed_parts = back_call(arrived, rate_slope, front, layout, piece, tiles)
+    weight_parts = tn(normed, grad_packed.reshape(Z * total, packed_width)).astype(bf16)
+    weight_parts = weight_parts.reshape(S, own, packed_width)
+    extent = -(-inner_send.shape[1] * 128 // packed_width)
+    inner_send = pad_to(inner_send.reshape(S, -1), extent * packed_width, 1).reshape(S, extent, packed_width)
+    got = swap(jnp.concatenate([weight_parts, inner_send], 1), "fsdp")
+    got, normed_parts, rear_sum = lax.optimization_barrier((got, normed_parts, rear_sum))
+    normed_parts = swap(normed_parts.reshape(Z, total, width), "sp")
+    got_sum = jnp.sum(got[:, :own].astype(f32), 0).astype(bf16)
     rear_sum = rear_sum.astype(f32)
-    weight_all = lax.all_gather(weight_grad.astype(bf16), "sp", axis=1).astype(f32)
-    pieces = weight_all[..., :extra].reshape(own, Z, local, 3, head)
-    pieces = jnp.stack([pieces[:, :, flat.index(g)] for g in range(local)], 2)
-    query_grad, key_grad, value_grad = (pieces[:, :, :, i].reshape(own, width) for i in range(3))
-    rate_grad = weight_all[..., extra : extra + local].reshape(own, Z * local)
-    normed_parts = nt(grad_packed, front).astype(bf16).reshape(Z, total, width)
-    grad_normed = jnp.sum(swap(normed_parts, "sp").astype(f32), 0) + grad_normed_gate
-    own_scale = lax.dynamic_slice_in_dim(scale_one, z * total, total, 0)
-    tokens_grad = (grad_middle + rms_back(grad_normed * pre_full, own_tokens, own_scale)).astype(bf16)
-
     out_grad = rear_sum[:, :width]
     gate_grad = rear_sum[:, width : 2 * width]
     fgate_grad = rear_sum[:, 2 * width : 2 * width + ff]
@@ -575,14 +680,29 @@
     def row_dot(grad, weight):
         return jnp.sum(grad * weight.astype(f32), -1)
 
+    post_grad = (row_dot(fgate_grad, ffn_gate) + row_dot(fup_grad, ffn_up)) / post_gain.astype(f32)
+    gate_dot = row_dot(gate_grad, gate_weight)
+    inner_part = got[:, own:].reshape(S, -1)[:, : slots * 2 * share * 128].astype(f32)
+    inner_part = jnp.sum(inner_part.reshape(groups, micro, slots, 2, share, 128), 1)
+    inner_part = inner_part.transpose(1, 0, 3, 2, 4).reshape(slots * groups, share, 2 * 128)[:local]
+    rear_done = (out_grad, gate_grad, fgate_grad, fup_grad, down_grad, post_grad, gate_dot)
+    rear_done, got_sum, inner_part = lax.optimization_barrier((rear_done, got_sum, inner_part.astype(bf16)))
+    out_grad, gate_grad, fgate_grad, fup_grad, down_grad, post_grad, gate_dot = rear_done
+    inner_sum = lax.all_gather(inner_part, "fsdp", axis=1, tiled=True)
+    weight_all = lax.all_gather(got_sum, "sp", axis=0)
+    inner_sum = inner_sum.astype(f32)
+    query_grad, key_grad, value_grad, rate_grad, front_dot = finish_call(
+        weight_all, query_weight, key_weight, value_weight, layout
+    )
+    grad_normed = jnp.sum(normed_parts.astype(f32), 0) + grad_normed_gate
+    own_scale = lax.dynamic_slice_in_dim(scale_one, z * total, total, 0)
+    tokens_grad = (grad_middle + rms_back(grad_normed * pre_full, own_tokens, own_scale)).astype(bf16)
+
     pre_grad = (
-        row_dot(query_grad, query_weight)
-        + row_dot(key_grad, key_weight)
-        + row_dot(value_grad, value_weight)
-        + row_dot(gate_grad, gate_weight)
+        front_dot[:, 0]
+        + gate_dot
         + row_dot(rate_grad, rate_weight)
     ) / pre_gain.astype(f32)
-    post_grad = (row_dot(fgate_grad, ffn_gate) + row_dot(fup_grad, ffn_up)) / post_gain.astype(f32)
 
     tail = inner_sum[:, 2 * head : 2 * head + 2].reshape(local, 2 * inner)
     return (

time: 519 us -> 482 us (0.929); the launches traced: 510 us -> 480 us
  local copies, waits for them, and re-layouts: 70.9 us -> 48 us
  waiting for transfers between devices: 94.6 us -> 114 us
  blocking collectives: 62.6 us -> 43.7 us
  other arithmetic: 41.7 us -> 24.5 us
  Pallas kernels: 155 us -> 171 us
    psum x1, waiting for transfers between devices: 2.71 us -> 29.1 us  [shards(): rear_sum = lax.psum(rear_part, 'sp')]
    all_gather x2, blocking collectives: 50.2 us -> 31.4 us  [the longest x1 22.1 us: shards(): weight_all = lax.all_gather(got_sum, 'sp', axis=0)]
    pallas_call x2 -> x4, Pallas kernels: 155 us -> 171 us  [the longest x1 88 us: bwd_call(): pl.pallas_call(functools.partial(bwd_kernel, slots, count, unroll, piece,...]
    reshape x12 -> x2, local copies, waits for them, and re-layouts: 12.4 us -> 1.68 us  [the longest x1 1.66 us: shards(): inner_part.reshape(groups, micro, slots, 2, share, 128)]
    another operation x10 -> x6, other arithmetic: 8.43 us -> 0.11 us
    unnamed x136 -> x147, local copies, waits for them, and re-layouts: 16.5 us -> 10.2 us
    dot_general x6 -> x5, matrix products: 13.8 us -> 9.78 us  [nt(): lax.dot_general(x.astype(bf16), y.astype(bf16), (((1,), (1,)), ((), ())),...]
  transfers between devices with their start and end apart: 11 -> 11, of which waited for: 7 -> 6; matrix products, arithmetic and copies ran while one was open for 22% -> 18% of each run, Pallas kernels for 30% -> 36%
where the time goes in v3:
time: 482 us; the launch traced here: 480 us
  Pallas kernels  171 us (35%)
  waiting for transfers between devices  114 us (24%)
  local copies, waits for them, and re-layouts  48 us (10%)
  blocking collectives  43.7 us (9%)
  matrix products  40.7 us (8%)
  other arithmetic  24.5 us (5%)
  starting transfers between devices  23.2 us (5%)
  between operations  15 us (3%)
    pallas_call x1, Pallas kernels, bwd_call(): pl.pallas_call(functools.partial(bwd_kernel, slots, count, unroll, piece,...  88 us
    pallas_call x1, Pallas kernels, fwd_call(): pl.pallas_call(functools.partial(fwd_kernel, slots, count, unroll, piece,...  74.6 us
    all_to_all x6, waiting for transfers between devices, swap(): return lax.all_to_all(block, axes, split_axis=0, concat_axis=0, tiled=True)  59.2 us
    psum x1, waiting for transfers between devices, shards(): rear_sum = lax.psum(rear_part, 'sp')  29.1 us
    all_gather x1, waiting for transfers between devices, shards(): all_tokens = lax.all_gather(tokens[:, 0], 'sp', axis=0)  23.2 us
    all_to_all x6, starting transfers between devices, swap(): return lax.all_to_all(block, axes, split_axis=0, concat_axis=0, tiled=True)  22.8 us
    all_gather x1, blocking collectives, shards(): weight_all = lax.all_gather(got_sum, 'sp', axis=0)  22.1 us
    dot_general x6, matrix products, nn(): lax.dot_general(x.astype(bf16), y.astype(bf16), (((1,), (0,)), ((), ())),...  16.8 us
  transfers between devices with their start and end apart: 11, of which 6 were waited for; matrix products, arithmetic and copies ran while one was open for 18% of the time, Pallas kernels for 36%

profile of v3, /device:TPU:0, one launch (start us, length us, event | category | flops | bytes accessed | tf_op | source)
XLA Modules:
  0.0 479.9 jit_solution(6574881210790420453)
XLA Ops:
  14.0 12.3 %all_gather.21.front_ref = bf16[768,640]{1,0:T(8,128)(2,1)S(1)} all-gather(bf16[96,640]{1,0:T(8,128)(2,1)S(1)} %pad.30), channel_id=1, replica_groups=mesh['sp'=4,'fsdp'=8] {'fsdp'}, dimensions={0}, use_global_device_ids=true | all-gather | bytes 1105920 | tf_op jit(solution)/shard_map/all_gather | solution.py:361
  26.3 23.2 %all-gather.10.cloned.1.call-done = bf16[16,1,64,768]{3,2,1,0:T(8,128)(2,1)} async-done(((bf16[4,1,64,768]{3,2,1,0:T(8,128)(2,1)}), bf16[16,1,64,768]{3,2,1,0:T(8,128)(2,1)}) %all-gather.10.cloned.1.call-update) | async-done | bytes 1572880 | tf_op jit(solution)/shard_map/all_gather | solution.py:536
  53.9 2.6 fusion.58
  59.5 3.9 reshape_reshape.9
  65.1 3.8 all-to-all-start
  72.8 25.9 %all-to-all-done.x_ref = bf16[8,784,128]{2,1,0:T(8,128)(2,1)S(1)} async-done(((bf16[8,784,128]{2,1,0:T(8,128)(2,1)}), bf16[8,784,128]{2,1,0:T(8,128)(2,1)S(1)}, u32[]{:S(2)}, u32[]{:S(2)}) %all-to-all-start) | async-done | bytes 1605664 | tf_op jit(solution)/shard_map/all_to_all | solution.py:365
  99.9 74.6 %inner_forward.1 = (bf16[2048,128]{1,0:T(8,128)(2,1)}, bf16[2,2048,64]{2,1,0:T(8,128)(2,1)}, bf16[2,2048,64]{2,1,0:T(8,128)(2,1)}, bf16[2,2048,64]{2,1,0:T(8,128...) custom-call(bf16[8,784,128]{2,1,0:T(8,128)(2,1)} %copy-done.18, ...), custom_call_target="tpu_custom_call" | custom-call | flops 89999998976 | bytes 40000000 | tf_op jit(solution)/shard_map/inner_forward/pallas_call | solution.py:168
  174.4 2.8 all-to-all-start.1
  177.6 13.8 %all-to-all-done.1 = bf16[32,64,128]{2,1,0:T(8,128)(2,1)S(1)} async-done(((bf16[32,64,128]{2,1,0:T(8,128)(2,1)}), bf16[32,64,128]{2,1,0:T(8,128)(2,1)S(1)}, u32[]{:S(2)}, u32[]{:S(2)}) %all-to-all-start.1) | async-done | bytes 524320 | tf_op jit(solution)/shard_map/all_to_all | solution.py:365
  194.0 4.2 fusion.59
  198.2 2.1 multiply_convert_fusion.8
  200.3 2.6 multiply_reduce_fusion.4
  203.1 3.2 fusion.7
  206.3 2.7 multiply_convert_fusion.2
  217.1 4.2 all-to-all-start.2
  226.5 2.4 convolution_convert_fusion
  230.0 4.5 reshape.318
  234.4 4.1 fusion.1
  238.5 2.8 fusion
  241.3 2.2 constant_dynamic-update-slice_fusion
  243.5 88.0 %inner_backward.1 = (bf16[8,784,128]{2,1,0:T(8,128)(2,1)}, f32[2,64,256]{2,1,0:T(8,128)}, f32[2,1,256]{2,1,0:T(1,128)}, f32[2,64,256]{2,1,0:T(8,128)}, f32[2,1,6...) custom-call(bf16[2,2048,64]{2,1,0:T(8,128)(2,1)} %get-tuple-element.77.q_ref, ...), custom_call_target="tpu_custom_call" | custom-call | flops 109999996928 | bytes 40000000 | tf_op jit(solution)/shard_map/inner_backward/pallas_call | solution.py:342
  333.0 3.7 all-to-all-start.3
  338.5 19.5 %all-to-all-done.3.a_ref = bf16[8,784,128]{2,1,0:T(8,128)(2,1)S(1)} async-done(((bf16[8,784,128]{2,1,0:T(8,128)(2,1)}), bf16[8,784,128]{2,1,0:T(8,128)(2,1)S(1)}, u32[]{:S(2)}, u32[]{:S(2)}) %all-to-all-start.3) | async-done | bytes 1605664 | tf_op jit(solution)/shard_map/all_to_all | solution.py:365
  359.3 6.0 %projection_gradients.1 = (bf16[4,4,64,640]{3,2,1,0:T(8,128)(2,1)}, bf16[4,4,64,768]{3,2,1,0:T(8,128)(2,1)}) custom-call(bf16[8,784,128]{2,1,0:T(8,128)(2,1)} %copy-done.17, f32[4,4,64,128]{3,2,1,0:T(8,128)} %bitcast.150, bf16[768,640]{1,0:T(8,128)(2,1)} %copy-done.16), custom_call_target="tpu_custom_call" | custom-call | flops 1000000000 | bytes 8000000 | tf_op jit(solution)/shard_map/projection_gradients/pallas_call | solution.py:428
  365.3 2.9 bitcast_convert_fusion
  369.4 3.6 all-to-all-start.4
  374.3 3.6 fusion.25
  377.9 29.1 %all-reduce.10.cloned.1.call-done = bf16[96,7680]{1,0:T(8,128)(2,1)} async-done(((bf16[96,7680]{1,0:T(8,128)(2,1)}), bf16[96,7680]{1,0:T(8,128)(2,1)}) %all-reduce.10.cloned.1.call-update) | async-done | bytes 1474576 | tf_op jit(solution)/shard_map/psum | solution.py:654
  407.1 4.8 all-to-all-start.5
  428.0 9.3 %all_gather.27 = bf16[3,136,256]{2,0,1:T(4,128)(2,1)S(1)} all-gather(bf16[3,17,256]{2,0,1:T(4,128)(2,1)S(1)} %bitcast.156), channel_id=1, replica_groups=mesh['sp'=4,'fsdp'=8] {'fsdp'}, dimensions={1}, use_global_device_ids=true | all-gather | bytes 235008 | tf_op jit(solution)/shard_map/all_gather | solution.py:691
  437.5 22.1 %all-gather.1 = bf16[384,640]{1,0:T(8,128)(2,1)} all-gather(bf16[96,640]{1,0:T(8,128)(2,1)S(1)} %slice_reduce_fusion), channel_id=3, replica_groups=mesh['sp'=4,'fsdp'=8] {'sp'}, dimensions={0}, use_global_device_ids=true | all-gather | bytes 614400 | tf_op jit(solution)/shard_map/all_gather | solution.py:692
  459.6 2.4 weight_gradients.1
  (285 shorter events, 72.3 us)
Async XLA Ops:
  7.2 42.3 %copy-start.27 = (bf16[96,768]{1,0:T(8,128)(2,1)S(1)}, bf16[96,768]{1,0:T(8,128)(2,1)}, u32[]{:S(2)}) copy-start(bf16[96,768]{1,0:T(8,128)(2,1)} %param.27) | copy-start | bytes 442372
  7.2 42.3 %copy-start.24 = (bf16[96,2048]{1,0:T(8,128)(2,1)S(1)}, bf16[96,2048]{1,0:T(8,128)(2,1)}, u32[]{:S(2)}) copy-start(bf16[96,2048]{1,0:T(8,128)(2,1)} %param.31) | copy-start | bytes 1179652
  7.2 42.3 %copy-start.22 = (bf16[96,2048]{1,0:T(8,128)(2,1)S(1)}, bf16[96,2048]{1,0:T(8,128)(2,1)}, u32[]{:S(2)}) copy-start(bf16[96,2048]{1,0:T(8,128)(2,1)} %param.32) | copy-start | bytes 1179652
  7.2 42.2 %all-gather.10.cloned.1.call-start = ((), (), s32[]{:S(2)}) async-start(), calls=%async_computation.11 | async-start | bytes 1966080 | tf_op jit(solution)/shard_map/all_gather | solution.py:536
  8.0 186.0 %all-gather.8.cloned.1.call-start = ((), (), s32[]{:S(2)}) async-start(), calls=%async_computation.8 | async-start | bytes 3538944 | tf_op jit(solution)/shard_map/all_gather | solution.py:361
  26.3 27.6 %copy-start.16 = (bf16[768,640]{1,0:T(8,128)(2,1)}, bf16[768,640]{1,0:T(8,128)(2,1)S(1)}, u32[]{:S(2)}) copy-start(bf16[768,640]{1,0:T(8,128)(2,1)S(1)} %all_gather.21.front_ref) | copy-start | bytes 2949124
  26.3 25.4 %copy-start.50 = (f32[3,256]{1,0:T(4,128)S(1)}, f32[3,256]{1,0:T(4,128)}, u32[]{:S(2)}) copy-start(f32[3,256]{1,0:T(4,128)} %param.35) | copy-start | bytes 9220
  26.3 25.5 %copy-start.53 = (f32[3,64]{1,0:T(4,128)S(1)}, f32[3,64]{1,0:T(4,128)}, u32[]{:S(2)}) copy-start(f32[3,64]{1,0:T(4,128)} %param.39) | copy-start | bytes 2308
  26.3 25.5 %copy-start.54 = (f32[3,64]{1,0:T(4,128)S(1)}, f32[3,64]{1,0:T(4,128)}, u32[]{:S(2)}) copy-start(f32[3,64]{1,0:T(4,128)} %param.38) | copy-start | bytes 2308
  49.5 148.7 %all-gather.6.cloned.1.call-start = ((), (), s32[]{:S(2)}) async-start(), calls=%async_computation.7 | async-start | bytes 9732096 | tf_op jit(solution)/shard_map/all_gather | solution.py:361
  65.1 33.5 %all-to-all-start = ((bf16[8,784,128]{2,1,0:T(8,128)(2,1)}), bf16[8,784,128]{2,1,0:T(8,128)(2,1)S(1)}, u32[]{:S(2)}, u32[]{:S(2)}) async-start(bf16[8,784,128]{2,1,0:T(8,128)(2,1)} %fusion.14), calls=%async_computation | async-start | bytes 3211264 | tf_op jit(solution)/shard_map/all_to_all | solution.py:365
  99.9 77.4 %copy-start.56 = (s32[4]{0:T(128)S(1)}, s32[4]{0:T(128)}, u32[]{:S(2)}) copy-start(s32[4]{0:T(128)} %param.21) | copy-start | bytes 52
  99.9 77.6 %copy-start.21 = (bf16[4,1,64,768]{3,2,1,0:T(8,128)(2,1)S(1)}, bf16[4,1,64,768]{3,2,1,0:T(8,128)(2,1)}, u32[]{:S(2)}) copy-start(bf16[4,1,64,768]{3,2,1,0:T(8,128)(2,1)} %param.22) | copy-start | bytes 1179652
  174.4 17.0 %all-to-all-start.1 = ((bf16[32,64,128]{2,1,0:T(8,128)(2,1)}), bf16[32,64,128]{2,1,0:T(8,128)(2,1)S(1)}, u32[]{:S(2)}, u32[]{:S(2)}) async-start(bf16[32,64,128]{2,1,0:T(8,128)(2,1)} %bitcast.149), calls=%async_computation.1 | async-start | bytes 1048576 | tf_op jit(solution)/shard_map/all_to_all | solution.py:365
  177.6 16.4 %copy-start.8 = (bf16[256,768]{1,0:T(8,128)(2,1)}, bf16[256,768]{1,0:T(8,128)(2,1)S(1)}, u32[]{:S(2)}) copy-start(bf16[256,768]{1,0:T(8,128)(2,1)S(1)} %fusion.40) | copy-start | bytes 1179652
  202.9 8.6 %copy-start.12 = (f32[256,768]{1,0:T(8,128)}, f32[256,768]{1,0:T(8,128)S(1)}, u32[]{:S(2)}) copy-start(f32[256,768]{1,0:T(8,128)S(1)} %get-tuple-element.243) | copy-start | bytes 2359300
  217.1 26.3 %all-to-all-start.2 = ((bf16[32,64,128]{2,1,0:T(8,128)(2,1)}), bf16[32,64,128]{2,1,0:T(8,128)(2,1)}, u32[]{:S(2)}, u32[]{:S(2)}) async-start(bf16[32,64,128]{2,1,0:T(8,128)(2,1)} %reshape.316), calls=%async_computation.2 | async-start | bytes 1048576 | tf_op jit(solution)/shard_map/all_to_all | solution.py:365
  221.3 111.7 %reduce-scatter.2.cloned.1.call-start = ((), (), s32[]{:S(2)}) async-start(), calls=%async_computation.9 | async-start | bytes 13271040 | tf_op jit(solution)/shard_map/reduce_scatter | solution.py:647
  333.0 25.0 %all-to-all-start.3 = ((bf16[8,784,128]{2,1,0:T(8,128)(2,1)}), bf16[8,784,128]{2,1,0:T(8,128)(2,1)S(1)}, u32[]{:S(2)}, u32[]{:S(2)}) async-start(bf16[8,784,128]{2,1,0:T(8,128)(2,1)} %get-tuple-element.92), calls=%async_computation.4 | async-start | bytes 3211264 | tf_op jit(solution)/shard_map/all_to_all | solution.py:365
  336.8 70.3 %all-reduce.10.cloned.1.call-start = ((), (), s32[]{:S(2)}) async-start(), calls=%async_computation.10 | async-start | bytes 2949120 | tf_op jit(solution)/shard_map/psum | solution.py:654
  338.5 26.7 %copy-start.5 = (bf16[16,1,64,768]{3,2,1,0:T(8,128)(2,1)S(1)}, bf16[16,1,64,768]{3,2,1,0:T(8,128)(2,1)}, u32[]{:S(2)}) copy-start(bf16[16,1,64,768]{3,2,1,0:T(8,128)(2,1)} %all-gather.10.cloned.1.call-done) | copy-start | bytes 4718596
  338.5 26.7 %copy-start.38 = (f32[4,4,64]{2,1,0:T(4,128)S(1)}, f32[4,4,64]{2,1,0:T(4,128)}, u32[]{:S(2)}) copy-start(f32[4,4,64]{2,1,0:T(4,128)} %copy-done.37) | copy-start | bytes 12292
  338.5 26.7 %copy-start.41 = (f32[768]{0:T(1024)S(1)}, f32[768]{0:T(1024)}, u32[]{:S(2)}) copy-start(f32[768]{0:T(1024)} %copy-done.40) | copy-start | bytes 9220
  369.4 37.7 %all-to-all-start.4 = ((bf16[8,110,640]{2,1,0:T(8,128)(2,1)}), bf16[8,110,640]{2,1,0:T(8,128)(2,1)S(1)}, u32[]{:S(2)}, u32[]{:S(2)}) async-start(bf16[8,110,640]{2,1,0:T(8,128)(2,1)} %pad_maximum_fusion), calls=%async_computation.5 | async-start | bytes 2293760 | tf_op jit(solution)/shard_map/all_to_all | solution.py:365
  407.1 61.6 %all-to-all-start.5 = ((bf16[4,256,768]{2,1,0:T(8,128)(2,1)}), bf16[4,256,768]{2,1,0:T(8,128)(2,1)}, u32[]{:S(2)}, u32[]{:S(2)}) async-start(bf16[4,256,768]{2,1,0:T(8,128)(2,1)} %bitcast.142), calls=%async_computation.6 | async-start | bytes 3145728 | tf_op jit(solution)/shard_map/all_to_all | solution.py:365
  416.2 8.8 %copy-start.23 = (bf16[96,2048]{1,0:T(8,128)(2,1)S(1)}, bf16[96,2048]{1,0:T(8,128)(2,1)}, u32[]{:S(2)}) copy-start(bf16[96,2048]{1,0:T(8,128)(2,1)} %param.32) | copy-start | bytes 1179652
  416.2 8.8 %copy-start.25 = (bf16[96,2048]{1,0:T(8,128)(2,1)S(1)}, bf16[96,2048]{1,0:T(8,128)(2,1)}, u32[]{:S(2)}) copy-start(bf16[96,2048]{1,0:T(8,128)(2,1)} %param.31) | copy-start | bytes 1179652
  437.4 29.1 %copy-start.32 = (f32[96,12]{1,0:T(8,128)S(1)}, f32[96,12]{1,0:T(8,128)}, u32[]{:S(2)}) copy-start(f32[96,12]{1,0:T(8,128)} %copy.177) | copy-start | bytes 13828
  437.4 30.1 %copy-start.46 = (bf16[96]{0:T(256)(128)(2,1)S(1)}, bf16[96]{0:T(256)(128)(2,1)}, u32[]{:S(2)}) copy-start(bf16[96]{0:T(256)(128)(2,1)} %param.23) | copy-start | bytes 580
  437.4 30.0 %copy-start.49 = (f32[96]{0:T(128)S(1)}, f32[96]{0:T(128)}, u32[]{:S(2)}) copy-start(f32[96]{0:T(128)} %multiply_reduce_fusion.5) | copy-start | bytes 1156
  462.0 8.4 %copy-start.20 = (bf16[256,768]{1,0:T(8,128)(2,1)S(1)}, bf16[256,768]{1,0:T(8,128)(2,1)}, u32[]{:S(2)}) copy-start(bf16[256,768]{1,0:T(8,128)(2,1)} %get-tuple-element.202) | copy-start | bytes 1179652
  462.0 8.4 %copy-start.42 = (f32[768]{0:T(1024)S(1)}, f32[768]{0:T(1024)}, u32[]{:S(2)}) copy-start(f32[768]{0:T(1024)} %copy-done.40) | copy-start | bytes 9220
  (39 other events, 149.0 us)
Sparse Core Ops, SparseCore 0:
  9.6 39.7 all-gather.9
  51.3 43.6 all-gather.7
  96.9 57.8 all-gather.5
  243.6 89.3 reduce-scatter.1
  339.8 67.2 all-reduce.9

commit v4 on v3

--- a/solution.py
+++ b/solution.py
@@ -12,7 +12,7 @@
 RATE = 1.0 / 1024.0
 GELU_C = 0.7978845608028654
 GELU_K = 0.044715
-VMEM_BYTES = 56 * 1024 * 1024
+VMEM_BYTES = 58 * 1024 * 1024
 f32 = jnp.float32
 bf16 = jnp.bfloat16
 
@@ -440,7 +440,7 @@
     )(arrived, slope, front)
 
 
-def finish_kernel(layout, all_ref, q_ref, k_ref, v_ref, dq_ref, dk_ref, dv_ref, dr_ref, dot_ref):
+def finish_kernel(layout, all_ref, q_ref, k_ref, v_ref, r_ref, gate_ref, pre_ref, dq_ref, dk_ref, dv_ref, dr_ref, dot_ref):
     local = layout["local"]
     flat = layout["flat"]
     Z = all_ref.shape[0]
@@ -461,10 +461,11 @@
             n = local * 192 + g
             rate = jnp.where(lanes == z * local + g, all_ref[z, :, n : n + 1].astype(f32), rate)
     dr_ref[...] = rate
-    dot_ref[...] = dot
-
-
-def finish_call(gathered, q_w, k_w, v_w, layout):
+    dot = dot + jnp.sum(rate * r_ref[...].astype(f32), 1, keepdims=True) + gate_ref[...]
+    dot_ref[...] = dot / pre_ref[...].astype(f32)
+
+
+def finish_call(gathered, q_w, k_w, v_w, r_w, gate_dot, pre, layout):
     own, width = q_w.shape
     Z = gathered.shape[0]
     shapes = [(own, width)] * 3 + [(own, Z * layout["local"]), (own, 1)]
@@ -474,7 +475,198 @@
         compiler_params=pltpu.CompilerParams(vmem_limit_bytes=VMEM_BYTES),
         name="weight_gradients",
         cost_estimate=pl.CostEstimate(flops=10_000_000, bytes_accessed=2_000_000, transcendentals=0),
-    )(gathered, q_w, k_w, v_w)
+    )(gathered, q_w, k_w, v_w, r_w, gate_dot, pre)
+
+
+def rear_kernel(layout, got_ref, act_ref, slope_ref, tok_ref, w_ref, post_ref, gh_ref, go_ref,
+                send_ref, lhs_ref, rhs_ref, hid_ref, gm_ref, mid_ref):
+    groups, slots, local, micro = layout["groups"], layout["slots"], layout["local"], layout["micro"]
+    Z, rows = got_ref.shape[1], got_ref.shape[2]
+    total, width = act_ref.shape
+    ff = hid_ref.shape[1]
+    blocks = []
+    for m in range(micro):
+        pieces = []
+        for z in range(Z):
+            for g in range(local):
+                h, j = g % groups, g // groups
+                pieces.append(got_ref[h * micro + m, z, :, 64 * j : 64 * j + 64])
+        blocks.append(jnp.concatenate(pieces, 1))
+    mixed = cat(*blocks).astype(f32)
+    gated = (act_ref[...] * mixed).astype(bf16)
+    lhs_ref[0] = gated.T
+    middle = tok_ref[...].astype(f32) + nn(gated, w_ref[:, :width])
+    mid_ref[...] = middle
+    scale = lax.rsqrt(jnp.mean(middle * middle, -1, keepdims=True) + EPS)
+    post = post_ref[...]
+    low = (middle * scale * post).astype(bf16)
+    lhs_ref[1] = low.T
+    gm_ref[...] = jnp.zeros((total, width), f32)
+    step = 256
+
+    @pl.loop(0, ff // step)
+    def _(c):
+        here = pl.ds(pl.multiple_of(c * step, step), step)
+        gate_at = pl.ds(pl.multiple_of(2 * width + c * step, step), step)
+        up_at = pl.ds(pl.multiple_of(2 * width + ff + c * step, step), step)
+        gate_w, up_w = w_ref[:, gate_at], w_ref[:, up_at]
+        gate_pre, up_pre = nn(low, gate_w), nn(low, up_w)
+        sig = 0.5 + 0.5 * jnp.tanh(0.5 * gate_pre)
+        silu = gate_pre * sig
+        hid_ref[:, here] = (silu * up_pre).astype(bf16)
+        grad = gh_ref[:, here]
+        g_gate = (grad * up_pre * sig * (1.0 + gate_pre * (1.0 - sig))).astype(bf16)
+        g_up = (grad * silu).astype(bf16)
+        rhs_ref[:, gate_at] = g_gate
+        rhs_ref[:, up_at] = g_up
+        gm_ref[...] += nt(g_gate, gate_w) + nt(g_up, up_w)
+
+    middle = mid_ref[...]
+    grad_middle = go_ref[...].astype(f32) + rms_back(gm_ref[...] * post, middle, scale)
+    gm_ref[...] = grad_middle
+    branch = grad_middle.astype(bf16)
+    rhs_ref[:, :width] = branch
+    grad_gated = nt(branch, w_ref[:, :width])
+    grad_mixed = (grad_gated * act_ref[...]).astype(bf16)
+    rhs_ref[:, width : 2 * width] = (grad_gated * mixed * slope_ref[...]).astype(bf16)
+    for m in range(micro):
+        for z in range(Z):
+            for h in range(groups):
+                for j in range(slots):
+                    g = h + j * groups
+                    if g < local:
+                        lane = (z * local + g) * 64
+                        value = grad_mixed[m * rows : m * rows + rows, lane : lane + 64]
+                    else:
+                        value = jnp.zeros((rows, 64), bf16)
+                    send_ref[h * micro + m, z, :, 64 * j : 64 * j + 64] = value
+
+
+def rear_call(layout, got, act, slope, tok, weights, post, grad_hidden, grad_low):
+    total, width = act.shape
+    ff = grad_hidden.shape[1]
+    S_ = jax.ShapeDtypeStruct
+    return pl.pallas_call(
+        functools.partial(rear_kernel, layout),
+        out_shape=[
+            S_(got.shape, bf16), S_((2, width, total), bf16), S_((total, weights.shape[1]), bf16),
+            S_((total, ff), bf16), S_((total, width), f32), S_((total, width), f32),
+        ],
+        compiler_params=pltpu.CompilerParams(vmem_limit_bytes=VMEM_BYTES),
+        name="rear",
+        cost_estimate=pl.CostEstimate(flops=5_000_000_000, bytes_accessed=16_000_000, transcendentals=0),
+    )(got, act, slope, tok, weights, post, grad_hidden, grad_low)
+
+
+def rear_grad_kernel(starts, per_step, lhs_ref, normed_ref, low_ref, rhs_ref, hid_ref, out_ref):
+    S = out_ref.shape[0]
+    own = out_ref.shape[1] // per_step
+    gate_at, ffn_at, down_at = starts
+
+    def block(n, top):
+        here = pl.ds(top * own, own)
+
+        def write(left):
+            right = rhs_ref[:, pl.ds(pl.multiple_of(n * 256, 256), 256)]
+            out_ref[:, here] = nn(left, right).astype(bf16).reshape(S, own, 256)
+
+        @pl.when(n < gate_at)
+        def _():
+            write(lhs_ref[0])
+
+        @pl.when((n >= gate_at) & (n < ffn_at))
+        def _():
+            write(normed_ref[...])
+
+        @pl.when((n >= ffn_at) & (n < down_at))
+        def _():
+            write(lhs_ref[1])
+
+        @pl.when(n >= down_at)
+        def _():
+            i = n - down_at
+            part = hid_ref.shape[1] // S
+            k = 256 // part
+            gap = low_ref.shape[0] // k
+            left = [low_ref[pl.ds(pl.multiple_of(c * gap + i * own, 8), own)] for c in range(k)]
+            product = nn(cat(*left), hid_ref[...]).astype(bf16)
+            for d in range(S):
+                parts = [product[c * own : c * own + own, part * d : part * d + part] for c in range(k)]
+                out_ref[d, here] = parts[0] if k == 1 else jnp.concatenate(parts, 1)
+
+    for u in range(per_step):
+        block(pl.program_id(0) * per_step + u, u)
+
+
+def rear_grad_call(lhs, normed_t, low_t, rhs, hidden, S):
+    _, width, total = lhs.shape
+    own = width // S
+    starts = (width // 256, 2 * width // 256, rhs.shape[1] // 256)
+    blocks = starts[2] + width * hidden.shape[1] // S // 256 // own
+    per_step = 2 - blocks % 2
+    full = lambda a: pl.BlockSpec(a.shape, lambda n: (0,) * a.ndim, pipeline_mode=pl.Buffered(1))
+    return pl.pallas_call(
+        functools.partial(rear_grad_kernel, starts, per_step),
+        grid=(blocks // per_step,),
+        in_specs=[full(a) for a in (lhs, normed_t, low_t, rhs, hidden)],
+        out_specs=pl.BlockSpec((S, per_step * own, 256), lambda n: (0, n, 0)),
+        out_shape=jax.ShapeDtypeStruct((S, blocks * own, 256), bf16),
+        compiler_params=pltpu.CompilerParams(dimension_semantics=("arbitrary",), vmem_limit_bytes=VMEM_BYTES),
+        name="rear_gradients",
+        cost_estimate=pl.CostEstimate(flops=4_000_000_000, bytes_accessed=16_000_000, transcendentals=0),
+    )(lhs, normed_t, low_t, rhs, hidden)
+
+
+def unpack_kernel(down_at, part, sum_ref, gate_w, fgate_w, fup_w, post_ref,
+                  out_ref, gate_ref, fgate_ref, fup_ref, down_ref, dot_ref, post_grad_ref):
+    own = out_ref.shape[0]
+    n = 0
+    for ref in (out_ref, gate_ref, fgate_ref, fup_ref):
+        for c in range(ref.shape[1] // 256):
+            ref[:, c * 256 : c * 256 + 256] = sum_ref[n * own : n * own + own].astype(f32)
+            n += 1
+    gap = down_ref.shape[1] * part // 256
+    for c in range(256 // part):
+        block = sum_ref[down_at * own : down_at * own + gap, c * part : c * part + part].astype(f32)
+        down_ref[:, c * gap : c * gap + gap] = block.T
+
+    def row_dot(grad, weight):
+        return jnp.sum(grad[...] * weight[...].astype(f32), 1, keepdims=True)
+
+    dot_ref[...] = row_dot(gate_ref, gate_w)
+    post_grad_ref[...] = (row_dot(fgate_ref, fgate_w) + row_dot(fup_ref, fup_w)) / post_ref[...].astype(f32)
+
+
+def unpack_call(packed, gate_w, fgate_w, fup_w, post, ff_own):
+    own, width = gate_w.shape
+    ff = fgate_w.shape[1]
+    shapes = [(own, width), (own, width), (own, ff), (own, ff), (ff_own, width), (own, 1), (own, 1)]
+    return pl.pallas_call(
+        functools.partial(unpack_kernel, (2 * width + 2 * ff) // 256, ff_own),
+        out_shape=[jax.ShapeDtypeStruct(s, f32) for s in shapes],
+        compiler_params=pltpu.CompilerParams(vmem_limit_bytes=VMEM_BYTES),
+        name="rear_unpack",
+        cost_estimate=pl.CostEstimate(flops=1_000_000, bytes_accessed=1_000_000, transcendentals=0),
+    )(packed, gate_w, fgate_w, fup_w, post)
+
+
+def token_kernel(parts_ref, gate_ref, tok_ref, gain_ref, middle_ref, out_ref):
+    grad = gate_ref[...]
+    for z in range(parts_ref.shape[0]):
+        grad = grad + parts_ref[z].astype(f32)
+    tok = tok_ref[...].astype(f32)
+    scale = lax.rsqrt(jnp.mean(tok * tok, -1, keepdims=True) + EPS)
+    out_ref[...] = (middle_ref[...] + rms_back(grad * gain_ref[...], tok, scale)).astype(bf16)
+
+
+def token_call(parts, gate, tok, gain, middle):
+    return pl.pallas_call(
+        token_kernel,
+        out_shape=jax.ShapeDtypeStruct(tok.shape, bf16),
+        compiler_params=pltpu.CompilerParams(vmem_limit_bytes=VMEM_BYTES),
+        name="token_gradients",
+        cost_estimate=pl.CostEstimate(flops=10_000_000, bytes_accessed=4_000_000, transcendentals=0),
+    )(parts, gate, tok, gain, middle)
 
 
 def shards(
@@ -592,60 +784,28 @@
     fup_full = rear[:, 2 * width + ff :]
     down_full = gather(down_in)
 
-    def to_tokens(chains):
-        got = swap(chains.reshape(S * Z, rows, slots * head), ("fsdp", "sp"))
-        got = got.reshape(groups, micro, Z, rows, slots, head).transpose(1, 3, 2, 4, 0, 5)
-        return got.reshape(total, Z, slots * groups, head)[:, :, :local].reshape(total, width)
-
-    def to_chains(block):
-        send = pad_to(block.reshape(micro, rows, Z, local, head), slots * groups, 3)
-        send = send.reshape(micro, rows, Z, slots, groups, head).transpose(4, 0, 2, 1, 3, 5)
-        got = swap(send.reshape(S * Z, rows, slots * head), ("fsdp", "sp"))
-        return got.reshape(length, slots * head)
-
-    mixed_rows = to_tokens(mix).astype(f32)
-    own_tokens = tokens.reshape(total, width).astype(f32)
+    got = swap(mix.reshape(S * Z, rows, slots * head), ("fsdp", "sp"))
+    own_tokens = tokens.reshape(total, width)
     own_normed = lax.dynamic_slice_in_dim(normed, z * total, total, 0)
-    gate_logit = nn(own_normed, gate_full)
-    gate_act, gate_slope = gelu2(gate_logit)
-    gated = (gate_act * mixed_rows).astype(bf16)
-    middle = own_tokens + nn(gated, out_full)
-    scale_two = lax.rsqrt(jnp.mean(middle * middle, -1, keepdims=True) + EPS)
-    normed_two = (middle * scale_two * post_full).astype(bf16)
-    gate_pre = nn(normed_two, fgate_full)
-    up_pre = nn(normed_two, fup_full)
-    gate_sig = jax.nn.sigmoid(gate_pre)
-    silu_act = gate_pre * gate_sig
-    hidden = (silu_act * up_pre).astype(bf16)
-    output = (middle + nn(hidden, down_full)).astype(bf16)
-
+    gate_act, gate_slope = gelu2(nn(own_normed, gate_full))
     position = d * piece + z * rows + lax.broadcasted_iota(jnp.int32, (micro, rows), 1)
     live = (position < lengths[:, None]).astype(f32).reshape(total, 1)
-    grad_out = cotangent.reshape(total, width).astype(f32) * live
-    grad_low = grad_out.astype(bf16)
+    grad_low = (cotangent.reshape(total, width).astype(f32) * live).astype(bf16)
     grad_hidden = nt(grad_low, down_full)
-    grad_gate_pre = (grad_hidden * up_pre * gate_sig * (1.0 + gate_pre * (1.0 - gate_sig))).astype(bf16)
-    grad_up_pre = (grad_hidden * silu_act).astype(bf16)
-    grad_normed_two = nt(grad_gate_pre, fgate_full) + nt(grad_up_pre, fup_full)
-    grad_middle = grad_out + rms_back(grad_normed_two * post_full, middle, scale_two)
-    grad_branch = grad_middle.astype(bf16)
-    grad_gated = nt(grad_branch, out_full)
-    grad_mixed = (grad_gated * gate_act).astype(bf16)
-    grad_gate_logit = (grad_gated * mixed_rows * gate_slope).astype(bf16)
-    d_mix = to_chains(grad_mixed)
-    rear_grad = jnp.concatenate(
-        [
-            tn(gated, grad_branch).astype(bf16),
-            tn(own_normed, grad_gate_logit).astype(bf16),
-            tn(normed_two, grad_gate_pre).astype(bf16),
-            tn(normed_two, grad_up_pre).astype(bf16),
-            tn(hidden, grad_low).astype(bf16).reshape(width, ff),
-        ],
-        1,
+    got, gate_act, gate_slope, grad_hidden, normed_t, low_t = lax.optimization_barrier(
+        (got, gate_act, gate_slope, grad_hidden, own_normed.T, grad_low.T)
     )
+    sent, lhs, rhs, hidden, grad_middle, middle = rear_call(
+        layout, got.reshape(S, Z, rows, slots * head), gate_act, gate_slope, own_tokens, rear, post_full,
+        grad_hidden, grad_low,
+    )
+    d_mix = swap(sent.reshape(S * Z, rows, slots * head), ("fsdp", "sp")).reshape(length, slots * head)
+    rear_grad = rear_grad_call(lhs, normed_t, low_t, rhs, hidden, S)
     d_mix, rear_grad = lax.optimization_barrier((d_mix, rear_grad))
-    rear_part = lax.psum_scatter(rear_grad, "fsdp", scatter_dimension=0, tiled=True)
-    grad_normed_gate = nt(grad_gate_logit, gate_full)
+    packed_rows = rear_grad.shape[1]
+    rear_part = lax.psum_scatter(rear_grad.reshape(S * packed_rows, 256), "fsdp", scatter_dimension=0, tiled=True)
+    output = (middle + nn(hidden, down_full)).astype(bf16)
+    grad_normed_gate = nt(rhs[:, width : 2 * width], gate_full)
 
     packed_back, dw1, db1, dw2, db2, dgn, dsh = bwd_call(
         q, k, v, e, d_mix, n, g_, nq, w1s, w2s, z1, h, q1, gain, shift, piece, tiles
@@ -670,18 +830,10 @@
     got, normed_parts, rear_sum = lax.optimization_barrier((got, normed_parts, rear_sum))
     normed_parts = swap(normed_parts.reshape(Z, total, width), "sp")
     got_sum = jnp.sum(got[:, :own].astype(f32), 0).astype(bf16)
-    rear_sum = rear_sum.astype(f32)
-    out_grad = rear_sum[:, :width]
-    gate_grad = rear_sum[:, width : 2 * width]
-    fgate_grad = rear_sum[:, 2 * width : 2 * width + ff]
-    fup_grad = rear_sum[:, 2 * width + ff : 2 * width + 2 * ff]
-    down_grad = rear_sum[:, 2 * width + 2 * ff :].reshape(-1, width)
-
-    def row_dot(grad, weight):
-        return jnp.sum(grad * weight.astype(f32), -1)
-
-    post_grad = (row_dot(fgate_grad, ffn_gate) + row_dot(fup_grad, ffn_up)) / post_gain.astype(f32)
-    gate_dot = row_dot(gate_grad, gate_weight)
+    out_grad, gate_grad, fgate_grad, fup_grad, down_grad, gate_dot, post_grad = unpack_call(
+        rear_sum, gate_weight, ffn_gate, ffn_up, post_gain[:, None], ff // S
+    )
+    post_grad = post_grad[:, 0]
     inner_part = got[:, own:].reshape(S, -1)[:, : slots * 2 * share * 128].astype(f32)
     inner_part = jnp.sum(inner_part.reshape(groups, micro, slots, 2, share, 128), 1)
     inner_part = inner_part.transpose(1, 0, 3, 2, 4).reshape(slots * groups, share, 2 * 128)[:local]
@@ -691,19 +843,11 @@
     inner_sum = lax.all_gather(inner_part, "fsdp", axis=1, tiled=True)
     weight_all = lax.all_gather(got_sum, "sp", axis=0)
     inner_sum = inner_sum.astype(f32)
-    query_grad, key_grad, value_grad, rate_grad, front_dot = finish_call(
-        weight_all, query_weight, key_weight, value_weight, layout
+    query_grad, key_grad, value_grad, rate_grad, pre_grad = finish_call(
+        weight_all, query_weight, key_weight, value_weight, rate_weight, gate_dot, pre_gain[:, None], layout
     )
-    grad_normed = jnp.sum(normed_parts.astype(f32), 0) + grad_normed_gate
-    own_scale = lax.dynamic_slice_in_dim(scale_one, z * total, total, 0)
-    tokens_grad = (grad_middle + rms_back(grad_normed * pre_full, own_tokens, own_scale)).astype(bf16)
-
-    pre_grad = (
-        front_dot[:, 0]
-        + gate_dot
-        + row_dot(rate_grad, rate_weight)
-    ) / pre_gain.astype(f32)
-
+    pre_grad = pre_grad[:, 0]
+    tokens_grad = token_call(normed_parts, grad_normed_gate, own_tokens, pre_full, grad_middle)
     tail = inner_sum[:, 2 * head : 2 * head + 2].reshape(local, 2 * inner)
     return (
         output.reshape(tokens.shape),

time: 482 us -> 459 us (0.952)
  Pallas kernels: 171 us -> 206 us
  matrix products: 40.7 us -> 18.3 us
  local copies, waits for them, and re-layouts: 48 us -> 30.6 us
  waiting for transfers between devices: 114 us -> 104 us
  other arithmetic: 24.5 us -> 15.3 us
    pallas_call x0 -> x4, Pallas kernels: none -> 34.7 us  [the longest x1 14.3 us: rear_grad_call(): pl.pallas_call(functools.partial(rear_grad_kernel, starts, per_step), gri...]
    all_to_all x6, waiting for transfers between devices: 59.2 us -> 46.2 us  [swap(): return lax.all_to_all(block, axes, split_axis=0, concat_axis=0, tiled=True)]
    dot_general x6 -> x1, matrix products: 14.2 us -> 2.91 us  [tn(): lax.dot_general(x.astype(bf16), y.astype(bf16), (((0,), (0,)), ((), ())),...]
    reshape x7 -> x0, local copies, waits for them, and re-layouts: 9.2 us -> none  [the longest x1 4.46 us: shards(): tn(hidden, grad_low).astype(bf16).reshape(width, ff)]
    dot_general x6 -> x3, matrix products: 16.8 us -> 8.29 us  [nn(): lax.dot_general(x.astype(bf16), y.astype(bf16), (((1,), (0,)), ((), ())),...]
    reduce_sum x4 -> x0, other arithmetic: 5.9 us -> none  [the longest x3 4.18 us: row_dot(): return jnp.sum(grad * weight.astype(f32), -1)]
    psum x1, waiting for transfers between devices: 29.1 us -> 34.1 us  [shards(): rear_sum = lax.psum(rear_part, 'sp')]
    dot_general x5 -> x2, matrix products: 9.78 us -> 7.09 us  [nt(): lax.dot_general(x.astype(bf16), y.astype(bf16), (((1,), (1,)), ((), ())),...]
  transfers between devices with their start and end apart: 11 -> 11, of which waited for: 6 -> 6; matrix products, arithmetic and copies ran while one was open for 18% -> 13% of each run, Pallas kernels for 36% -> 41%
where the time goes in v4:
time: 459 us; the launch traced here: 458 us
  Pallas kernels  206 us (45%)
  waiting for transfers between devices  104 us (23%)
  blocking collectives  46.1 us (10%)
  local copies, waits for them, and re-layouts  30.6 us (7%)
  starting transfers between devices  23 us (5%)
  matrix products  18.3 us (4%)
  other arithmetic  15.3 us (3%)
  between operations  14.7 us (3%)
    pallas_call x1, Pallas kernels, bwd_call(): pl.pallas_call(functools.partial(bwd_kernel, slots, count, unroll, piece,...  88 us
    pallas_call x1, Pallas kernels, fwd_call(): pl.pallas_call(functools.partial(fwd_kernel, slots, count, unroll, piece,...  74.6 us
    all_to_all x6, waiting for transfers between devices, swap(): return lax.all_to_all(block, axes, split_axis=0, concat_axis=0, tiled=True)  46.2 us
    psum x1, waiting for transfers between devices, shards(): rear_sum = lax.psum(rear_part, 'sp')  34.1 us
    all_gather x1, blocking collectives, shards(): weight_all = lax.all_gather(got_sum, 'sp', axis=0)  23.5 us
    all_to_all x6, starting transfers between devices, swap(): return lax.all_to_all(block, axes, split_axis=0, concat_axis=0, tiled=True)  22.8 us
    all_gather x1, waiting for transfers between devices, shards(): all_tokens = lax.all_gather(tokens[:, 0], 'sp', axis=0)  22 us
    pallas_call x1, Pallas kernels, rear_grad_call(): pl.pallas_call(functools.partial(rear_grad_kernel, starts, per_step), gri...  14.3 us
  transfers between devices with their start and end apart: 11, of which 6 were waited for; matrix products, arithmetic and copies ran while one was open for 13% of the time, Pallas kernels for 41%

profile of v4, /device:TPU:0, one launch (start us, length us, event | category | flops | bytes accessed | tf_op | source)
XLA Modules:
  0.0 457.8 jit_solution(6116548193428279567)
XLA Ops:
  14.1 13.4 %all_gather.21.front_ref = bf16[768,640]{1,0:T(8,128)(2,1)} all-gather(bf16[96,640]{1,0:T(8,128)(2,1)S(1)} %pad.26), channel_id=1, replica_groups=mesh['sp'=4,'fsdp'=8] {'fsdp'}, dimensions={0}, use_global_device_ids=true | all-gather | bytes 1105920 | tf_op jit(solution)/shard_map/all_gather | solution.py:361
  27.4 22.0 %all-gather.10.cloned.1.call-done = bf16[16,1,64,768]{3,2,1,0:T(8,128)(2,1)} async-done(((bf16[4,1,64,768]{3,2,1,0:T(8,128)(2,1)}), bf16[16,1,64,768]{3,2,1,0:T(8,128)(2,1)}) %all-gather.10.cloned.1.call-update) | async-done | bytes 1572880 | tf_op jit(solution)/shard_map/all_gather | solution.py:728
  53.7 1.7 copy.153
  58.1 1.5 fusion.22
  62.5 3.9 reshape_reshape.9
  68.1 3.8 all-to-all-start
  76.8 22.2 %all-to-all-done.x_ref = bf16[8,784,128]{2,1,0:T(8,128)(2,1)S(1)} async-done(((bf16[8,784,128]{2,1,0:T(8,128)(2,1)}), bf16[8,784,128]{2,1,0:T(8,128)(2,1)S(1)}, u32[]{:S(2)}, u32[]{:S(2)}) %all-to-all-start) | async-done | bytes 1605664 | tf_op jit(solution)/shard_map/all_to_all | solution.py:365
  100.2 74.6 %inner_forward.1 = (bf16[2048,128]{1,0:T(8,128)(2,1)}, bf16[2,2048,64]{2,1,0:T(8,128)(2,1)}, bf16[2,2048,64]{2,1,0:T(8,128)(2,1)}, bf16[2,2048,64]{2,1,0:T(8,128...) custom-call(bf16[8,784,128]{2,1,0:T(8,128)(2,1)} %copy-done.9, ...), custom_call_target="tpu_custom_call" | custom-call | flops 89999998976 | bytes 40000000 | tf_op jit(solution)/shard_map/inner_forward/pallas_call | solution.py:168
  174.8 3.9 all-to-all-start.1
  181.0 4.3 fusion.23.gh_ref
  185.3 3.2 multiply_add_fusion
  188.5 4.5 all-to-all-done.1
  193.7 13.6 %rear.1 = (bf16[8,4,64,128]{3,2,1,0:T(8,128)(2,1)}, bf16[2,768,256]{2,1,0:T(8,128)(2,1)}, bf16[256,5632]{1,0:T(8,128)(2,1)}, bf16[256,2048]{1,0:T(8,128)(2,1)}, f32[256,768]{1,0:T(8,128)}, /*index=5*/f32[256,768]{1,0:T(8,128)}) custom-call(bf16[8,4,64,128]{3,2,1,0:T(8,128)(2,1)} %bitcast.126, f32[256,768]{1,0:T(8,128)} %get-tuple-element.97.act_ref, ...), custom_call_target="tpu_custom_call" | custom-call | flops 5000000000 | bytes 16000000 | tf_op jit(solution)/shard_map/rear/pallas_call | solution.py:549
  207.3 4.1 all-to-all-start.2
  211.4 14.3 %rear_gradients.1 = bf16[8,2880,256]{2,1,0:T(8,128)(2,1)} custom-call(bf16[2,768,256]{2,1,0:T(8,128)(2,1)} %get-tuple-element.107.lhs_ref, bf16[768,256]{1,0:T(8,128)(2,1)} %dynamic-slice_bitcast_fusion.normed_ref, bf16[768,256]{1,0:T(8,128)(2,1)} %fusion.31.low_ref, bf16[256,5632]{1,0:T(8,128)(2,1)} %get-tuple-element.110.rhs_ref, ...), custom_call_target="tpu_custom_call" | custom-call | flops 4000000000 | bytes 16000000 | tf_op jit(solution)/shard_map/rear_gradients/pallas_call | solution.py:608
  226.5 88.0 %inner_backward.1 = (bf16[8,784,128]{2,1,0:T(8,128)(2,1)}, f32[2,64,256]{2,1,0:T(8,128)}, f32[2,1,256]{2,1,0:T(1,128)}, f32[2,64,256]{2,1,0:T(8,128)}, f32[2,1,6...) custom-call(bf16[2,2048,64]{2,1,0:T(8,128)(2,1)} %get-tuple-element.102.q_ref, ...), custom_call_target="tpu_custom_call" | custom-call | flops 109999996928 | bytes 40000000 | tf_op jit(solution)/shard_map/inner_backward/pallas_call | solution.py:342
  315.4 3.7 all-to-all-start.3
  320.9 19.5 %all-to-all-done.3.a_ref = bf16[8,784,128]{2,1,0:T(8,128)(2,1)S(1)} async-done(((bf16[8,784,128]{2,1,0:T(8,128)(2,1)}), bf16[8,784,128]{2,1,0:T(8,128)(2,1)S(1)}, u32[]{:S(2)}, u32[]{:S(2)}) %all-to-all-start.3) | async-done | bytes 1605664 | tf_op jit(solution)/shard_map/all_to_all | solution.py:365
  341.6 6.1 %projection_gradients.1 = (bf16[4,4,64,640]{3,2,1,0:T(8,128)(2,1)}, bf16[4,4,64,768]{3,2,1,0:T(8,128)(2,1)}) custom-call(bf16[8,784,128]{2,1,0:T(8,128)(2,1)} %copy-done.8, f32[4,4,64,128]{3,2,1,0:T(8,128)} %bitcast.128, bf16[768,640]{1,0:T(8,128)(2,1)} %all_gather.21.front_ref), custom_call_target="tpu_custom_call" | custom-call | flops 1000000000 | bytes 8000000 | tf_op jit(solution)/shard_map/projection_gradients/pallas_call | solution.py:428
  347.7 2.9 bitcast_convert_fusion
  351.7 3.6 all-to-all-start.4
  355.3 34.1 %all-reduce.9.cloned.1.call-done.sum_ref = bf16[2880,256]{1,0:T(8,128)(2,1)} async-done(((bf16[2880,256]{1,0:T(8,128)(2,1)}), bf16[2880,256]{1,0:T(8,128)(2,1)}) %all-reduce.9.cloned.1.call-update) | async-done | bytes 1474576 | tf_op jit(solution)/shard_map/psum | solution.py:814
  389.4 3.8 all-to-all-start.5
  393.8 2.8 fusion.6.gate_ref
  396.6 3.6 fusion.5
  400.7 3.5 rear_unpack.1
  404.2 1.4 reduce.9
  405.8 9.3 %all_gather.27 = bf16[3,136,256]{2,0,1:T(4,128)(2,1)S(1)} all-gather(bf16[3,17,256]{2,0,1:T(4,128)(2,1)S(1)} %bitcast.134), channel_id=1, replica_groups=mesh['sp'=4,'fsdp'=8] {'fsdp'}, dimensions={1}, use_global_device_ids=true | all-gather | bytes 235008 | tf_op jit(solution)/shard_map/all_gather | solution.py:843
  417.3 23.5 %all-gather.1 = bf16[384,640]{1,0:T(8,128)(2,1)} all-gather(bf16[96,640]{1,0:T(8,128)(2,1)S(1)} %slice_reduce_fusion), channel_id=3, replica_groups=mesh['sp'=4,'fsdp'=8] {'sp'}, dimensions={0}, use_global_device_ids=true | all-gather | bytes 614400 | tf_op jit(solution)/shard_map/all_gather | solution.py:844
  440.8 2.5 weight_gradients.1
  444.7 1.5 copy.178
  448.0 3.2 token_gradients.1
  (223 shorter events, 39.3 us)
Async XLA Ops:
  7.2 42.2 %all-gather.10.cloned.1.call-start = ((), (), s32[]{:S(2)}) async-start(), calls=%async_computation.11 | async-start | bytes 1966080 | tf_op jit(solution)/shard_map/all_gather | solution.py:728
  7.9 173.1 %all-gather.8.cloned.1.call-start = ((), (), s32[]{:S(2)}) async-start(), calls=%async_computation.8 | async-start | bytes 3538944 | tf_op jit(solution)/shard_map/all_gather | solution.py:361
  8.7 40.7 %copy-start.21 = (bf16[96,1]{1,0:T(8,128)(2,1)}, bf16[96,1]{1,0:T(8,128)(2,1)S(1)}, u32[]{:S(2)}) copy-start(bf16[96,1]{1,0:T(8,128)(2,1)S(1)} %copy.151.pre_ref) | copy-start | bytes 580
  9.6 4.3 copy-start.22
  10.4 39.1 %copy-start.20 = (bf16[96,1]{1,0:T(8,128)(2,1)}, bf16[96,1]{1,0:T(8,128)(2,1)S(1)}, u32[]{:S(2)}) copy-start(bf16[96,1]{1,0:T(8,128)(2,1)S(1)} %copy.152.post_ref) | copy-start | bytes 580
  11.5 38.1 %copy-start.10 = (bf16[96,2048]{1,0:T(8,128)(2,1)S(1)}, bf16[96,2048]{1,0:T(8,128)(2,1)}, u32[]{:S(2)}) copy-start(bf16[96,2048]{1,0:T(8,128)(2,1)} %fup_w.1) | copy-start | bytes 1179652
  11.5 38.1 %copy-start.11 = (bf16[96,2048]{1,0:T(8,128)(2,1)S(1)}, bf16[96,2048]{1,0:T(8,128)(2,1)}, u32[]{:S(2)}) copy-start(bf16[96,2048]{1,0:T(8,128)(2,1)} %fgate_w.1) | copy-start | bytes 1179652
  11.5 38.1 %copy-start.13 = (bf16[96,768]{1,0:T(8,128)(2,1)S(1)}, bf16[96,768]{1,0:T(8,128)(2,1)}, u32[]{:S(2)}) copy-start(bf16[96,768]{1,0:T(8,128)(2,1)} %gate_w.1) | copy-start | bytes 442372
  11.5 38.0 %copy-start.23 = (bf16[96,768]{1,0:T(8,128)(2,1)S(1)}, bf16[96,768]{1,0:T(8,128)(2,1)}, u32[]{:S(2)}) copy-start(bf16[96,768]{1,0:T(8,128)(2,1)} %param.29) | copy-start | bytes 442372
  49.5 135.8 %all-gather.6.cloned.1.call-start = ((), (), s32[]{:S(2)}) async-start(), calls=%async_computation.7 | async-start | bytes 9732096 | tf_op jit(solution)/shard_map/all_gather | solution.py:361
  68.1 5.5 %copy-start.14 = (f32[1,256,64]{1,2,0:T(8,128)S(1)}, f32[1,256,64]{1,2,0:T(8,128)}, u32[]{:S(2)}) copy-start(f32[1,256,64]{1,2,0:T(8,128)} %get-tuple-element.237) | copy-start | bytes 196612
  68.1 5.5 %copy-start.15 = (f32[1,256,64]{1,2,0:T(8,128)S(1)}, f32[1,256,64]{1,2,0:T(8,128)}, u32[]{:S(2)}) copy-start(f32[1,256,64]{1,2,0:T(8,128)} %get-tuple-element.238) | copy-start | bytes 196612
  68.1 5.5 %copy-start.36 = (f32[1,64]{1,0:T(1,128)S(1)}, f32[1,64]{1,0:T(1,128)}, u32[]{:S(2)}) copy-start(f32[1,64]{1,0:T(1,128)} %get-tuple-element.260) | copy-start | bytes 772
  68.1 5.5 %copy-start.37 = (f32[1,64]{1,0:T(1,128)S(1)}, f32[1,64]{1,0:T(1,128)}, u32[]{:S(2)}) copy-start(f32[1,64]{1,0:T(1,128)} %get-tuple-element.261) | copy-start | bytes 772
  68.1 6.1 %copy-start.34 = (f32[1,64]{1,0:T(1,128)S(1)}, f32[1,64]{1,0:T(1,128)}, u32[]{:S(2)}) copy-start(f32[1,64]{1,0:T(1,128)} %get-tuple-element.270) | copy-start | bytes 772
  68.1 6.1 %copy-start.35 = (f32[1,64]{1,0:T(1,128)S(1)}, f32[1,64]{1,0:T(1,128)}, u32[]{:S(2)}) copy-start(f32[1,64]{1,0:T(1,128)} %get-tuple-element.271) | copy-start | bytes 772
  68.1 6.6 %copy-start.26 = (f32[3,64,256]{2,1,0:T(8,128)S(1)}, f32[3,64,256]{2,1,0:T(8,128)}, u32[]{:S(2)}) copy-start(f32[3,64,256]{2,1,0:T(8,128)} %param.34) | copy-start | bytes 589828
  68.1 30.8 %all-to-all-start = ((bf16[8,784,128]{2,1,0:T(8,128)(2,1)}), bf16[8,784,128]{2,1,0:T(8,128)(2,1)S(1)}, u32[]{:S(2)}, u32[]{:S(2)}) async-start(bf16[8,784,128]{2,1,0:T(8,128)(2,1)} %fusion.1), calls=%async_computation | async-start | bytes 3211264 | tf_op jit(solution)/shard_map/all_to_all | solution.py:365
  100.2 78.6 %copy-start.1 = (f32[256,768]{0,1:T(8,128)S(1)}, f32[256,768]{0,1:T(8,128)}, u32[]{:S(2)}) copy-start(f32[256,768]{0,1:T(8,128)} %copy-done) | copy-start | bytes 2359300
  174.8 5.4 %copy-start.6 = (bf16[1024,768]{0,1:T(8,128)(2,1)S(1)}, bf16[1024,768]{0,1:T(8,128)(2,1)}, u32[]{:S(2)}) copy-start(bf16[1024,768]{0,1:T(8,128)(2,1)} %copy-done.5) | copy-start | bytes 4718596
  174.8 18.1 %all-to-all-start.1 = ((bf16[32,64,128]{2,1,0:T(8,128)(2,1)}), bf16[32,64,128]{2,1,0:T(8,128)(2,1)S(1)}, u32[]{:S(2)}, u32[]{:S(2)}) async-start(bf16[32,64,128]{2,1,0:T(8,128)(2,1)} %bitcast.125), calls=%async_computation.1 | async-start | bytes 1048576 | tf_op jit(solution)/shard_map/all_to_all | solution.py:365
  207.3 18.5 %all-to-all-start.2 = ((bf16[32,64,128]{2,1,0:T(8,128)(2,1)}), bf16[32,64,128]{2,1,0:T(8,128)(2,1)S(1)}, u32[]{:S(2)}, u32[]{:S(2)}) async-start(bf16[32,64,128]{2,1,0:T(8,128)(2,1)} %bitcast.127), calls=%async_computation.2 | async-start | bytes 1048576 | tf_op jit(solution)/shard_map/all_to_all | solution.py:365
  211.4 104.0 %reduce-scatter.2.cloned.1.call-start = ((), (), s32[]{:S(2)}) async-start(), calls=%async_computation.9 | async-start | bytes 13271040 | tf_op jit(solution)/shard_map/reduce_scatter | solution.py:806
  315.4 4.9 %copy-start.32 = (f32[2,1,64]{2,1,0:T(1,128)S(1)}, f32[2,1,64]{2,1,0:T(1,128)}, u32[]{:S(2)}) copy-start(f32[2,1,64]{2,1,0:T(1,128)} %get-tuple-element.127) | copy-start | bytes 1540
  315.4 5.1 %copy-start.40 = (f32[2,1,64]{2,1,0:T(1,128)S(1)}, f32[2,1,64]{2,1,0:T(1,128)}, u32[]{:S(2)}) copy-start(f32[2,1,64]{2,1,0:T(1,128)} %get-tuple-element.128) | copy-start | bytes 1540
  315.4 25.0 %all-to-all-start.3 = ((bf16[8,784,128]{2,1,0:T(8,128)(2,1)}), bf16[8,784,128]{2,1,0:T(8,128)(2,1)S(1)}, u32[]{:S(2)}, u32[]{:S(2)}) async-start(bf16[8,784,128]{2,1,0:T(8,128)(2,1)} %get-tuple-element.122), calls=%async_computation.4 | async-start | bytes 3211264 | tf_op jit(solution)/shard_map/all_to_all | solution.py:365
  319.1 70.3 %all-reduce.9.cloned.1.call-start = ((), (), s32[]{:S(2)}) async-start(), calls=%async_computation.10 | async-start | bytes 2949120 | tf_op jit(solution)/shard_map/psum | solution.py:814
  341.6 6.1 %copy-start.3 = (bf16[16,1,64,768]{3,2,1,0:T(8,128)(2,1)S(1)}, bf16[16,1,64,768]{3,2,1,0:T(8,128)(2,1)}, u32[]{:S(2)}) copy-start(bf16[16,1,64,768]{3,2,1,0:T(8,128)(2,1)} %all-gather.10.cloned.1.call-done) | copy-start | bytes 4718596
  341.6 6.1 %copy-start.29 = (f32[768]{0:T(1024)S(1)}, f32[768]{0:T(1024)}, u32[]{:S(2)}) copy-start(f32[768]{0:T(1024)} %copy-done.28) | copy-start | bytes 9220
  341.6 6.1 %copy-start.31 = (f32[4,4,64]{2,1,0:T(4,128)S(1)}, f32[4,4,64]{2,1,0:T(4,128)}, u32[]{:S(2)}) copy-start(f32[4,4,64]{2,1,0:T(4,128)} %copy-done.30) | copy-start | bytes 12292
  351.7 37.6 %all-to-all-start.4 = ((bf16[8,110,640]{2,1,0:T(8,128)(2,1)}), bf16[8,110,640]{2,1,0:T(8,128)(2,1)S(1)}, u32[]{:S(2)}, u32[]{:S(2)}) async-start(bf16[8,110,640]{2,1,0:T(8,128)(2,1)} %pad_maximum_fusion), calls=%async_computation.5 | async-start | bytes 2293760 | tf_op jit(solution)/shard_map/all_to_all | solution.py:365
  389.4 57.4 %all-to-all-start.5 = ((bf16[4,256,768]{2,1,0:T(8,128)(2,1)}), bf16[4,256,768]{2,1,0:T(8,128)(2,1)S(1)}, u32[]{:S(2)}, u32[]{:S(2)}) async-start(bf16[4,256,768]{2,1,0:T(8,128)(2,1)} %bitcast.115), calls=%async_computation.6 | async-start | bytes 3145728 | tf_op jit(solution)/shard_map/all_to_all | solution.py:365
  (25 other events, 39.3 us)
Sparse Core Ops, SparseCore 0:
  9.6 39.7 all-gather.9
  51.3 41.2 all-gather.7
  94.5 62.4 all-gather.5
  225.9 89.4 reduce-scatter.1
  322.2 67.1 all-reduce.8

commit v5 on v4

--- a/solution.py
+++ b/solution.py
@@ -74,7 +74,7 @@
                 for i in range(piece//128):
                     n=j*(piece//128)+i
                     column=jnp.sum(jnp.where(eye,rates[n:n+1],0.0),1,keepdims=True)
-                    e_ref[j,pl.ds(base+i*128,128)]=column
+                    e_ref[j,pl.ds(base+i*128,128)]=jnp.broadcast_to(column,(128,128))
         for j in range(slots):
             W1[j]=w1_ref[j]; B1[j]=b1_ref[j]; W2[j]=w2_ref[j]; B2[j]=b2_ref[j]
             Z[j]=nn(k_ref[j,:MINI],w1_ref[j])+b1_ref[j]
@@ -105,7 +105,7 @@
         L=cat(KK[:MINI].astype(bf16),(lower*KK[MINI:]).astype(bf16),K.T)
         base=nn(KQ,w1b)+b1
         U=gain*(shift-v_ref[j,rows].astype(f32)+K.astype(f32)); mU=rs(U)
-        e=e_ref[j,rows]
+        e=e_ref[j,rows]; e64=e[:,:64]; e256=jnp.concatenate([e,e],1)
         yield
         Q2=qb+nn(P2,Ep)
         yield
@@ -119,14 +119,14 @@
         Gb=G.astype(bf16)
         yield
         H=nn(Gb,w2b)
-        E2=e*G; E2b=E2.astype(bf16)
+        E2=e64*G; E2b=E2.astype(bf16)
         n_ref[j,rows]=(z-mz).astype(bf16); g_ref[j,rows]=Gb
         EP[j]=E2b; AP[j]=Ab
         yield
         W2[j]=w2-tn(E2b,Ab)
         B2[j]=b2-jnp.sum(E2,0,keepdims=True)
         yield
-        E1=(e*Ad)*H; E1b=E1.astype(bf16)
+        E1=(e256*Ad)*H; E1b=E1.astype(bf16)
         X=nn(L,E1b)
         Z[j]=base[:MINI]-X[:MINI]
         Q1=base[MINI:]-X[MINI:2*MINI]
@@ -162,14 +162,14 @@
     count=block//MINI; nb=length//block; steps=length//MINI
     row=lambda w: pl.BlockSpec((slots,block,w),lambda i:(0,i,0))
     full=lambda s: pl.BlockSpec(s,lambda i:(0,)*len(s),pipeline_mode=pl.Buffered(1))
-    r64=full((slots,length,64)); r1=full((slots,length,1)); rm_=full((length,64*slots))
+    r64=full((slots,length,64)); r1=full((slots,length,128)); rm_=full((length,64*slots))
     st=pl.BlockSpec((slots,count,64,256),lambda i:(0,i,0,0))
     S=jax.ShapeDtypeStruct
     return pl.pallas_call(functools.partial(fwd_kernel,slots,count,unroll,piece,tiles),
         grid=(nb,),
         in_specs=[full(a.shape) for a in (x,w1,b1,w2,b2,gain,shift)],
         out_specs=[rm_,r64,r64,r64,r1,st,st,row(256),row(256),row(256),r64,r64,r64],
-        out_shape=[S((length,64*slots),bf16)]+[S((slots,length,64),bf16)]*3+[S((slots,length,1),f32)]+[S((slots,steps,64,256),bf16)]*2+[S((slots,length,256),bf16)]*3+[S((slots,length,64),bf16)]*3,
+        out_shape=[S((length,64*slots),bf16)]+[S((slots,length,64),bf16)]*3+[S((slots,length,128),f32)]+[S((slots,steps,64,256),bf16)]*2+[S((slots,length,256),bf16)]*3+[S((slots,length,64),bf16)]*3,
         scratch_shapes=[pltpu.VMEM((slots,64,256),f32),pltpu.VMEM((slots,1,256),f32),pltpu.VMEM((slots,64,256),f32),pltpu.VMEM((slots,1,64),f32),pltpu.VMEM((slots,MINI,256),f32),pltpu.VMEM((slots,MINI,256),f32),pltpu.VMEM((slots,MINI,256),bf16),pltpu.VMEM((slots,MINI,64),bf16)],
         compiler_params=pltpu.CompilerParams(dimension_semantics=("arbitrary",),vmem_limit_bytes=VMEM_BYTES),
         name="inner_forward",cost_estimate=pl.CostEstimate(flops=90_000_000_000,bytes_accessed=40_000_000,transcendentals=0),**kw)(x,w1,b1,w2,b2,gain,shift)
@@ -204,7 +204,7 @@
         rows=pl.ds(pl.multiple_of(jnp.minimum(t,steps-1)*MINI,MINI),MINI)
         prow=pl.ds(pl.multiple_of(jnp.maximum(t-1,0)*MINI,MINI),MINI)
         gain=gain_ref[j]; shift=shift_ref[j]; g2=gain*gain; mg=rs(g2)
-        e=e_ref[j,rows]
+        e=e_ref[j,rows]; e64=e[:,:64]; e=jnp.concatenate([e,e],1)
         nE1=sR1[p,j]+KD[j]
         dgZ1=(-e)*nE1
         dH=dgZ1*sAd[p,j]
@@ -234,7 +234,7 @@
         L2=cat((nt(Kp,cat(Q,K))+1.0).astype(bf16),cat(Q,K).T)
         yield
         nE2=sR2[p,j]+a1+DB2[j]
-        y=yP-e*nE2
+        y=yP-e64*nE2
         yg=y*g2; yn=y*N
         ym=rs(y); yN=rs(yn); yG=rs(y*G); ygm=rs(yg); ygN=rs(yg*N)
         mdy=s*ym; mdyN=s*yN
@@ -280,10 +280,10 @@
         dQ2b=dQ2.astype(bf16)
         A,Ad,Add=gelu3(z1_ref[j,brow].astype(f32))
         AQ,AQd=gelu2(q1_ref[j,brow].astype(f32))
-        H=h_ref[j,brow].astype(f32); e=e_ref[j,rows]
+        H=h_ref[j,brow].astype(f32); e=e_ref[j,rows]; e64=e[:,:64]; e=jnp.concatenate([e,e],1)
         Ab=A.astype(bf16); AQb=AQ.astype(bf16)
         gZ1=H*Ad
-        E1b=(e*gZ1).astype(bf16); E2b=(e*g_ref[j,rows].astype(f32)).astype(bf16)
+        E1b=(e*gZ1).astype(bf16); E2b=(e64*g_ref[j,rows].astype(f32)).astype(bf16)
         w1b=w1s_ref[j,i]; w2b=w2s_ref[j,i]
         yield
         sA[p,j]=Ab; sAd[p,j]=Ad; sHA[p,j]=H*Add; sGZ[p,j]=gZ1; sE1[p,j]=E1b; sE2[p,j]=E2b; sW1[p,j]=w1b; sW2[p,j]=w2b; sAQ[p,j]=AQb
@@ -334,7 +334,7 @@
     count=block//MINI; nb=length//block; steps=length//MINI
     row=lambda w: pl.BlockSpec((slots,block,w),lambda i:(0,nb-1-i,0))
     full=lambda s: pl.BlockSpec(s,lambda i:(0,)*len(s),pipeline_mode=pl.Buffered(1))
-    r64=full((slots,length,64)); r1=full((slots,length,1))
+    r64=full((slots,length,64)); r1=full((slots,length,128))
     st=pl.BlockSpec((slots,count,64,256),lambda i:(0,nb-1-i,0,0))
     S=jax.ShapeDtypeStruct
     outs=[((length//piece,tiles*piece+16,128),bf16),((slots,64,256),f32),((slots,1,256),f32),((slots,64,256),f32),((slots,1,64),f32),((slots,1,64),f32),((slots,1,64),f32)]
@@ -669,6 +669,79 @@
     )(parts, gate, tok, gain, middle)
 
 
+def front_kernel(layout, piece, tiles, tok_ref, w_ref, normed_ref, slope_ref, send_ref, gains_ref):
+    local, order = layout["local"], layout["order"]
+    width, packed = w_ref.shape
+    extra = local * 192
+    eye = lax.broadcasted_iota(jnp.int32, (128, 128), 0) == lax.broadcasted_iota(jnp.int32, (128, 128), 1)
+
+    def to_row(column):
+        return jnp.sum(jnp.where(eye, column, 0.0), 0, keepdims=True)
+
+    @pl.when(pl.program_id(0) == 0)
+    def _():
+        for n in range(2):
+            lane = extra + local + n
+            for c in range(width // 128):
+                column = w_ref[c * 128 : c * 128 + 128, lane : lane + 1].astype(f32)
+                gains_ref[n : n + 1, c * 128 : c * 128 + 128] = to_row(column)
+
+    tok = tok_ref[:, 0].reshape(piece, width).astype(f32)
+    scale = lax.rsqrt(jnp.mean(tok * tok, -1, keepdims=True) + EPS)
+    normed = (tok * scale * gains_ref[0:1]).astype(bf16)
+    normed_ref[:, 0] = normed.reshape(normed_ref.shape[0], -1, width)
+    projected = nn(normed, w_ref[...])
+    sig = 0.5 + 0.5 * jnp.tanh(0.5 * projected[:, extra : extra + local])
+    slope = jnp.concatenate([RATE * sig * (1.0 - sig), jnp.zeros((piece, 128 - local), f32)], 1)
+    slope_ref[:, 0] = slope.reshape(slope_ref.shape[0], -1, 128)
+    rates = (RATE * sig).astype(bf16).astype(f32)
+    low = projected.astype(bf16)
+    start = 0
+    for h, part in enumerate(order):
+        for t in range(tiles):
+            first, stop = start + t * 128, min(start + t * 128 + 128, packed)
+            if first >= packed:
+                value = jnp.zeros((piece, 128), bf16)
+            else:
+                value = low[:, first:stop]
+                if stop - first < 128:
+                    value = jnp.concatenate([value, jnp.zeros((piece, 128 - stop + first), bf16)], 1)
+            send_ref[h, 0, t * piece : t * piece + piece] = value
+        start += len(part) * 192
+        rows = []
+        for j in range(layout["slots"]):
+            for i in range(piece // 128):
+                if j < len(part):
+                    g = part[j]
+                    rows.append(to_row(rates[i * 128 : i * 128 + 128, g : g + 1]))
+                else:
+                    rows.append(jnp.zeros((1, 128), f32))
+        rows.append(jnp.zeros((16 - len(rows), 128), f32))
+        send_ref[h, 0, tiles * piece : tiles * piece + 16] = cat(*rows).astype(bf16)
+
+
+def front_call(tokens, weights, layout, piece, tiles):
+    Z, micro, rows, width = tokens.shape
+    groups = layout["groups"]
+    extent = tiles * piece + 16
+    step = lambda w: pl.BlockSpec((Z, 1, rows, w), lambda m: (0, m, 0, 0))
+    full = lambda s: pl.BlockSpec(s, lambda m: (0,) * len(s), pipeline_mode=pl.Buffered(1))
+    S_ = jax.ShapeDtypeStruct
+    return pl.pallas_call(
+        functools.partial(front_kernel, layout, piece, tiles),
+        grid=(micro,),
+        in_specs=[step(width), full(weights.shape)],
+        out_specs=[step(width), step(128), pl.BlockSpec((groups, 1, extent, 128), lambda m: (0, m, 0, 0)), full((2, width))],
+        out_shape=[
+            S_((Z, micro, rows, width), bf16), S_((Z, micro, rows, 128), f32),
+            S_((groups, micro, extent, 128), bf16), S_((2, width), f32),
+        ],
+        compiler_params=pltpu.CompilerParams(dimension_semantics=("arbitrary",), vmem_limit_bytes=VMEM_BYTES),
+        name="front",
+        cost_estimate=pl.CostEstimate(flops=1_000_000_000, bytes_accessed=7_000_000, transcendentals=0),
+    )(tokens, weights)
+
+
 def shards(
     tokens,
     lengths,
@@ -728,36 +801,11 @@
     all_tokens = lax.all_gather(tokens[:, 0], "sp", axis=0)
     rear_in = (out_weight, gate_weight, ffn_gate, ffn_up, ffn_down)
     rear_in, front, all_tokens = lax.optimization_barrier((rear_in, front, all_tokens))
-    pre_full = front[:, extra + local].astype(f32)[None]
-    post_full = front[:, extra + local + 1].astype(f32)[None]
-    token_rows = all_tokens.reshape(Z * total, width).astype(f32)
-    scale_one = lax.rsqrt(jnp.mean(token_rows * token_rows, -1, keepdims=True) + EPS)
-    normed = (token_rows * scale_one * pre_full).astype(bf16)
-    projected = nn(normed, front)
-    rate_sig = jax.nn.sigmoid(projected[:, extra : extra + local])
-    rate_rows = (RATE * rate_sig).astype(bf16).reshape(Z, micro, rows, local)
-    rate_slope = pad_to(RATE * rate_sig * (1.0 - rate_sig), 128, 1).reshape(Z, micro, rows, 128)
     layout = dict(groups=groups, slots=slots, local=local, micro=micro, order=order, flat=flat)
-    low = projected.astype(bf16).reshape(Z, micro, rows, packed_width)
-    rate_tiles = slots * piece // 128
-
-    def pack_tiles(pieces, rates):
-        body = pieces.reshape(S, piece, tiles, 128).transpose(0, 2, 1, 3)
-        tail = pad_to(rates.reshape(S, rate_tiles, 128), 16 * (-(-rate_tiles // 16)), 1)
-        return jnp.concatenate([body.reshape(S, tiles * piece, 128), tail], 1)
-
-    low_parts = []
-    rate_parts = []
-    start = 0
-    for part in order:
-        stop = min(start + tiles * 128, packed_width)
-        low_parts.append(pad_to(low[..., start:stop], tiles * 128, 3))
-        start += len(part) * span
-        here = [rate_rows[..., g : g + 1] for g in part] + [jnp.zeros_like(rate_rows[..., :1])] * (slots - len(part))
-        rate_parts.append(jnp.concatenate(here, 3))
-    send_low = jnp.stack(low_parts).transpose(0, 2, 1, 3, 4).reshape(S, piece, tiles * 128)
-    send_rate = jnp.stack(rate_parts).transpose(0, 2, 4, 1, 3).reshape(S, slots, piece)
-    arrived = swap(pack_tiles(send_low, send_rate), "fsdp")
+    normed, rate_slope, send, gains = front_call(all_tokens, front, layout, piece, tiles)
+    normed = normed.reshape(Z * total, width)
+    pre_full, post_full = gains[:1], gains[1:]
+    arrived = swap(send.reshape(S, tiles * piece + 16, 128), "fsdp")
 
     half = d // micro
     heads_here = [jnp.minimum(half + j * groups, local - 1) for j in range(slots)]

time: 459 us -> 445 us (0.969)
  local copies, waits for them, and re-layouts: 30.6 us -> 20.6 us
  other arithmetic: 15.3 us -> 9.89 us
    pallas_call x0 -> x1, Pallas kernels: none -> 6.13 us  [front_call(): pl.pallas_call(functools.partial(front_kernel, layout, piece, tiles), gri...]
    unnamed x117 -> x82, local copies, waits for them, and re-layouts: 12.3 us -> 12.3 us
  transfers between devices with their start and end apart: 11 -> 11, of which waited for: 6 -> 6; matrix products, arithmetic and copies ran while one was open for 13% -> 9% of each run, Pallas kernels for 41% -> 43%
where the time goes in v5:
time: 445 us; the launch traced here: 444 us
  Pallas kernels  210 us (47%)
  waiting for transfers between devices  104 us (23%)
  blocking collectives  46.6 us (10%)
  starting transfers between devices  21.6 us (5%)
  local copies, waits for them, and re-layouts  20.6 us (5%)
  matrix products  16.7 us (4%)
  between operations  14.5 us (3%)
  other arithmetic  9.89 us (2%)
    pallas_call x1, Pallas kernels, bwd_call(): pl.pallas_call(functools.partial(bwd_kernel, slots, count, unroll, piece,...  87 us
    pallas_call x1, Pallas kernels, fwd_call(): pl.pallas_call(functools.partial(fwd_kernel, slots, count, unroll, piece,...  73.6 us
    all_to_all x6, waiting for transfers between devices, swap(): return lax.all_to_all(block, axes, split_axis=0, concat_axis=0, tiled=True)  45.5 us
    psum x1, waiting for transfers between devices, shards(): rear_sum = lax.psum(rear_part, 'sp')  34.3 us
    all_gather x1, blocking collectives, shards(): weight_all = lax.all_gather(got_sum, 'sp', axis=0)  23.9 us
    all_gather x1, waiting for transfers between devices, shards(): all_tokens = lax.all_gather(tokens[:, 0], 'sp', axis=0)  22 us
    all_to_all x6, starting transfers between devices, swap(): return lax.all_to_all(block, axes, split_axis=0, concat_axis=0, tiled=True)  21.2 us
    pallas_call x1, Pallas kernels, rear_grad_call(): pl.pallas_call(functools.partial(rear_grad_kernel, starts, per_step), gri...  14.3 us
  transfers between devices with their start and end apart: 11, of which 6 were waited for; matrix products, arithmetic and copies ran while one was open for 9% of the time, Pallas kernels for 43%

profile of v5, /device:TPU:0, one launch (start us, length us, event | category | flops | bytes accessed | tf_op | source)
XLA Modules:
  0.0 444.1 jit_solution(10299970862583011830)
XLA Ops:
  14.1 13.3 %all_gather.21.w_ref.front_ref = bf16[768,640]{1,0:T(8,128)(2,1)} all-gather(bf16[96,640]{1,0:T(8,128)(2,1)S(1)} %pad.13), channel_id=1, replica_groups=mesh['sp'=4,'fsdp'=8] {'fsdp'}, dimensions={0}, use_global_device_ids=true | all-gather | bytes 1105920 | tf_op jit(solution)/shard_map/all_gather | solution.py:361
  27.4 22.0 %all-gather.10.cloned.1.call-done = bf16[16,1,64,768]{3,2,1,0:T(8,128)(2,1)} async-done(((bf16[4,1,64,768]{3,2,1,0:T(8,128)(2,1)}), bf16[16,1,64,768]{3,2,1,0:T(8,128)(2,1)}) %all-gather.10.cloned.1.call-update) | async-done | bytes 1572880 | tf_op jit(solution)/shard_map/all_gather | solution.py:801
  52.1 6.1 %front.1 = (bf16[4,4,64,768]{3,2,1,0:T(8,128)(2,1)}, f32[4,4,64,128]{3,2,1,0:T(8,128)}, bf16[2,4,784,128]{3,2,1,0:T(8,128)(2,1)}, f32[2,768]{1,0:T(2,128)}) custom-call(bf16[4,4,64,768]{3,2,1,0:T(8,128)(2,1)} %bitcast.132, bf16[768,640]{1,0:T(8,128)(2,1)} %all_gather.21.w_ref.front_ref), custom_call_target="tpu_custom_call" | custom-call | flops 1000000000 | bytes 7000000 | tf_op jit(solution)/shard_map/front/pallas_call | solution.py:730
  58.2 3.8 all-to-all-start
  67.1 20.5 %all-to-all-done.x_ref = bf16[8,784,128]{2,1,0:T(8,128)(2,1)S(1)} async-done(((bf16[8,784,128]{2,1,0:T(8,128)(2,1)}), bf16[8,784,128]{2,1,0:T(8,128)(2,1)S(1)}, u32[]{:S(2)}, u32[]{:S(2)}) %all-to-all-start) | async-done | bytes 1605664 | tf_op jit(solution)/shard_map/all_to_all | solution.py:365
  88.8 73.6 %inner_forward.1 = (bf16[2048,128]{1,0:T(8,128)(2,1)}, bf16[2,2048,64]{2,1,0:T(8,128)(2,1)}, bf16[2,2048,64]{2,1,0:T(8,128)(2,1)}, bf16[2,2048,64]{2,1,0:T(8,128...) custom-call(bf16[8,784,128]{2,1,0:T(8,128)(2,1)} %copy-done.2, ...), custom_call_target="tpu_custom_call" | custom-call | flops 89999998976 | bytes 40000000 | tf_op jit(solution)/shard_map/inner_forward/pallas_call | solution.py:168
  162.5 2.6 all-to-all-start.1
  167.6 4.3 fusion.15.gh_ref
  171.9 3.1 multiply_add_fusion
  175.0 4.4 all-to-all-done.1
  180.2 13.5 %rear.1 = (bf16[8,4,64,128]{3,2,1,0:T(8,128)(2,1)}, bf16[2,768,256]{2,1,0:T(8,128)(2,1)}, bf16[256,5632]{1,0:T(8,128)(2,1)}, bf16[256,2048]{1,0:T(8,128)(2,1)}, f32[256,768]{1,0:T(8,128)}, /*index=5*/f32[256,768]{1,0:T(8,128)}) custom-call(bf16[8,4,64,128]{3,2,1,0:T(8,128)(2,1)} %bitcast.100, f32[256,768]{1,0:T(8,128)} %get-tuple-element.103.act_ref, ...), custom_call_target="tpu_custom_call" | custom-call | flops 5000000000 | bytes 16000000 | tf_op jit(solution)/shard_map/rear/pallas_call | solution.py:549
  193.8 4.1 all-to-all-start.2
  198.1 14.3 %rear_gradients.1 = bf16[8,2880,256]{2,1,0:T(8,128)(2,1)} custom-call(bf16[2,768,256]{2,1,0:T(8,128)(2,1)} %get-tuple-element.114.lhs_ref, bf16[768,256]{1,0:T(8,128)(2,1)} %bitcast.93, bf16[768,256]{1,0:T(8,128)(2,1)} %fusion.23.low_ref, bf16[256,5632]{1,0:T(8,128)(2,1)} %get-tuple-element.117.rhs_ref, bf16[256,2048]{1,0:T(8,128)(2,1)} %get-tuple-element.108.hid_ref), custom_call_target="tpu_custom_call" | custom-call | flops 4000000000 | bytes 16000000 | tf_op jit(solution)/shard_map/rear_gradients/pallas_call | solution.py:608
  213.2 87.0 %inner_backward.1 = (bf16[8,784,128]{2,1,0:T(8,128)(2,1)}, f32[2,64,256]{2,1,0:T(8,128)}, f32[2,1,256]{2,1,0:T(1,128)}, f32[2,64,256]{2,1,0:T(8,128)}, f32[2,1,6...) custom-call(bf16[2,2048,64]{2,1,0:T(8,128)(2,1)} %get-tuple-element.109.q_ref, ...), custom_call_target="tpu_custom_call" | custom-call | flops 109999996928 | bytes 40000000 | tf_op jit(solution)/shard_map/inner_backward/pallas_call | solution.py:342
  300.3 1.8 reduce-scatter.2.cloned.1.call-done
  302.1 3.6 all-to-all-start.3
  306.4 20.6 %all-to-all-done.3.a_ref = bf16[8,784,128]{2,1,0:T(8,128)(2,1)S(1)} async-done(((bf16[8,784,128]{2,1,0:T(8,128)(2,1)}), bf16[8,784,128]{2,1,0:T(8,128)(2,1)S(1)}, u32[]{:S(2)}, u32[]{:S(2)}) %all-to-all-start.3) | async-done | bytes 1605664 | tf_op jit(solution)/shard_map/all_to_all | solution.py:365
  328.1 6.0 %projection_gradients.1 = (bf16[4,4,64,640]{3,2,1,0:T(8,128)(2,1)}, bf16[4,4,64,768]{3,2,1,0:T(8,128)(2,1)}) custom-call(bf16[8,784,128]{2,1,0:T(8,128)(2,1)} %copy-done.1, f32[4,4,64,128]{3,2,1,0:T(8,128)} %get-tuple-element.130.slope_ref, bf16[768,640]{1,0:T(8,128)(2,1)} %all_gather.21.w_ref.front_ref), custom_call_target="tpu_custom_call" | custom-call | flops 1000000000 | bytes 8000000 | tf_op jit(solution)/shard_map/projection_gradients/pallas_call | solution.py:428
  334.2 2.7 bitcast_convert_fusion
  338.1 3.6 all-to-all-start.4
  341.6 34.3 %all-reduce.5.cloned.1.call-done.sum_ref = bf16[2880,256]{1,0:T(8,128)(2,1)} async-done(((bf16[2880,256]{1,0:T(8,128)(2,1)}), bf16[2880,256]{1,0:T(8,128)(2,1)}) %all-reduce.5.cloned.1.call-update) | async-done | bytes 1474576 | tf_op jit(solution)/shard_map/psum | solution.py:862
  375.9 3.6 all-to-all-start.5
  379.5 2.9 fusion.1.gate_ref
  382.5 3.6 fusion
  386.6 3.5 rear_unpack.1
  390.1 1.4 reduce.5
  391.6 9.3 %all_gather.27 = bf16[3,136,256]{2,0,1:T(4,128)(2,1)S(1)} all-gather(bf16[3,17,256]{2,0,1:T(4,128)(2,1)S(1)} %bitcast.107), channel_id=1, replica_groups=mesh['sp'=4,'fsdp'=8] {'fsdp'}, dimensions={1}, use_global_device_ids=true | all-gather | bytes 235008 | tf_op jit(solution)/shard_map/all_gather | solution.py:891
  403.2 23.9 %all-gather.1 = bf16[384,640]{1,0:T(8,128)(2,1)} all-gather(bf16[96,640]{1,0:T(8,128)(2,1)S(1)} %slice_reduce_fusion), channel_id=3, replica_groups=mesh['sp'=4,'fsdp'=8] {'sp'}, dimensions={0}, use_global_device_ids=true | all-gather | bytes 614400 | tf_op jit(solution)/shard_map/all_gather | solution.py:892
  427.0 2.5 weight_gradients.1
  429.6 1.4 reduce.6
  431.0 1.5 copy.120
  434.3 3.2 token_gradients.1
  (165 shorter events, 27.3 us)
Async XLA Ops:
  7.2 42.3 %copy-start.3 = (bf16[96,2048]{1,0:T(8,128)(2,1)S(1)}, bf16[96,2048]{1,0:T(8,128)(2,1)}, u32[]{:S(2)}) copy-start(bf16[96,2048]{1,0:T(8,128)(2,1)} %fup_w.1) | copy-start | bytes 1179652
  7.2 42.3 %copy-start.4 = (bf16[96,2048]{1,0:T(8,128)(2,1)S(1)}, bf16[96,2048]{1,0:T(8,128)(2,1)}, u32[]{:S(2)}) copy-start(bf16[96,2048]{1,0:T(8,128)(2,1)} %fgate_w.1) | copy-start | bytes 1179652
  7.2 42.3 %copy-start.6 = (bf16[96,768]{1,0:T(8,128)(2,1)S(1)}, bf16[96,768]{1,0:T(8,128)(2,1)}, u32[]{:S(2)}) copy-start(bf16[96,768]{1,0:T(8,128)(2,1)} %gate_w.1) | copy-start | bytes 442372
  7.2 42.3 %copy-start.14 = (bf16[96,768]{1,0:T(8,128)(2,1)S(1)}, bf16[96,768]{1,0:T(8,128)(2,1)}, u32[]{:S(2)}) copy-start(bf16[96,768]{1,0:T(8,128)(2,1)} %param.29) | copy-start | bytes 442372
  7.2 42.2 %all-gather.10.cloned.1.call-start = ((), (), s32[]{:S(2)}) async-start(), calls=%async_computation.11 | async-start | bytes 1966080 | tf_op jit(solution)/shard_map/all_gather | solution.py:801
  8.0 159.7 %all-gather.8.cloned.1.call-start = ((), (), s32[]{:S(2)}) async-start(), calls=%async_computation.8 | async-start | bytes 3538944 | tf_op jit(solution)/shard_map/all_gather | solution.py:361
  8.8 41.9 %copy-start.12 = (bf16[96,1]{1,0:T(8,128)(2,1)}, bf16[96,1]{1,0:T(8,128)(2,1)S(1)}, u32[]{:S(2)}) copy-start(bf16[96,1]{1,0:T(8,128)(2,1)S(1)} %copy.101.pre_ref) | copy-start | bytes 580
  9.6 4.3 copy-start.13
  10.4 40.3 %copy-start.11 = (bf16[96,1]{1,0:T(8,128)(2,1)}, bf16[96,1]{1,0:T(8,128)(2,1)S(1)}, u32[]{:S(2)}) copy-start(bf16[96,1]{1,0:T(8,128)(2,1)S(1)} %copy.102.post_ref) | copy-start | bytes 580
  27.4 23.3 %copy-start.28 = (s32[4]{0:T(128)S(1)}, s32[4]{0:T(128)}, u32[]{:S(2)}) copy-start(s32[4]{0:T(128)} %param.21) | copy-start | bytes 52
  27.4 23.5 %copy-start.10 = (bf16[4,1,64,768]{3,2,1,0:T(8,128)(2,1)S(1)}, bf16[4,1,64,768]{3,2,1,0:T(8,128)(2,1)}, u32[]{:S(2)}) copy-start(bf16[4,1,64,768]{3,2,1,0:T(8,128)(2,1)} %param.22) | copy-start | bytes 1179652
  49.5 122.4 %all-gather.6.cloned.1.call-start = ((), (), s32[]{:S(2)}) async-start(), calls=%async_computation.7 | async-start | bytes 9732096 | tf_op jit(solution)/shard_map/all_gather | solution.py:361
  50.7 1.3 copy-start.17
  58.2 6.0 %copy-start.18 = (f32[3,64,256]{2,1,0:T(8,128)S(1)}, f32[3,64,256]{2,1,0:T(8,128)}, u32[]{:S(2)}) copy-start(f32[3,64,256]{2,1,0:T(8,128)} %param.34) | copy-start | bytes 589828
  58.2 29.4 %all-to-all-start = ((bf16[8,784,128]{2,1,0:T(8,128)(2,1)}), bf16[8,784,128]{2,1,0:T(8,128)(2,1)S(1)}, u32[]{:S(2)}, u32[]{:S(2)}) async-start(bf16[8,784,128]{2,1,0:T(8,128)(2,1)} %bitcast.89), calls=%async_computation | async-start | bytes 3211264 | tf_op jit(solution)/shard_map/all_to_all | solution.py:365
  162.4 4.6 %copy-start.19 = (f32[2,768]{1,0:T(2,128)S(1)}, f32[2,768]{1,0:T(2,128)}, u32[]{:S(2)}) copy-start(f32[2,768]{1,0:T(2,128)} %get-tuple-element.105) | copy-start | bytes 18436
  162.5 17.0 %all-to-all-start.1 = ((bf16[32,64,128]{2,1,0:T(8,128)(2,1)}), bf16[32,64,128]{2,1,0:T(8,128)(2,1)S(1)}, u32[]{:S(2)}, u32[]{:S(2)}) async-start(bf16[32,64,128]{2,1,0:T(8,128)(2,1)} %bitcast.99), calls=%async_computation.1 | async-start | bytes 1048576 | tf_op jit(solution)/shard_map/all_to_all | solution.py:365
  193.8 18.6 %all-to-all-start.2 = ((bf16[32,64,128]{2,1,0:T(8,128)(2,1)}), bf16[32,64,128]{2,1,0:T(8,128)(2,1)S(1)}, u32[]{:S(2)}, u32[]{:S(2)}) async-start(bf16[32,64,128]{2,1,0:T(8,128)(2,1)} %bitcast.101), calls=%async_computation.2 | async-start | bytes 1048576 | tf_op jit(solution)/shard_map/all_to_all | solution.py:365
  197.8 104.2 %reduce-scatter.2.cloned.1.call-start = ((), (), s32[]{:S(2)}) async-start(), calls=%async_computation.9 | async-start | bytes 13271040 | tf_op jit(solution)/shard_map/reduce_scatter | solution.py:854
  300.2 5.5 %copy-start.20 = (f32[2,1,64]{2,1,0:T(1,128)S(1)}, f32[2,1,64]{2,1,0:T(1,128)}, u32[]{:S(2)}) copy-start(f32[2,1,64]{2,1,0:T(1,128)} %get-tuple-element.135) | copy-start | bytes 1540
  300.2 5.7 %copy-start.24 = (f32[2,1,64]{2,1,0:T(1,128)S(1)}, f32[2,1,64]{2,1,0:T(1,128)}, u32[]{:S(2)}) copy-start(f32[2,1,64]{2,1,0:T(1,128)} %get-tuple-element.136) | copy-start | bytes 1540
  300.2 5.7 %copy-start.23 = (f32[2,1,64]{2,1,0:T(1,128)S(1)}, f32[2,1,64]{2,1,0:T(1,128)}, u32[]{:S(2)}) copy-start(f32[2,1,64]{2,1,0:T(1,128)} %get-tuple-element.137) | copy-start | bytes 1540
  300.2 5.7 %copy-start.21 = (f32[2,1,256]{2,1,0:T(1,128)S(1)}, f32[2,1,256]{2,1,0:T(1,128)}, u32[]{:S(2)}) copy-start(f32[2,1,256]{2,1,0:T(1,128)} %get-tuple-element.134) | copy-start | bytes 6148
  300.3 5.8 %copy-start.9 = (f32[2,64,256]{2,1,0:T(8,128)S(1)}, f32[2,64,256]{2,1,0:T(8,128)}, u32[]{:S(2)}) copy-start(f32[2,64,256]{2,1,0:T(8,128)} %get-tuple-element.133) | copy-start | bytes 393220
  300.3 5.9 %copy-start.15 = (f32[2,64,256]{2,1,0:T(8,128)S(1)}, f32[2,64,256]{2,1,0:T(8,128)}, u32[]{:S(2)}) copy-start(f32[2,64,256]{2,1,0:T(8,128)} %get-tuple-element.132) | copy-start | bytes 393220
  302.1 24.9 %all-to-all-start.3 = ((bf16[8,784,128]{2,1,0:T(8,128)(2,1)}), bf16[8,784,128]{2,1,0:T(8,128)(2,1)S(1)}, u32[]{:S(2)}, u32[]{:S(2)}) async-start(bf16[8,784,128]{2,1,0:T(8,128)(2,1)} %get-tuple-element.129), calls=%async_computation.4 | async-start | bytes 3211264 | tf_op jit(solution)/shard_map/all_to_all | solution.py:365
  305.6 70.3 %all-reduce.5.cloned.1.call-start = ((), (), s32[]{:S(2)}) async-start(), calls=%async_computation.10 | async-start | bytes 2949120 | tf_op jit(solution)/shard_map/psum | solution.py:862
  306.4 27.8 %copy-start.16 = (bf16[4,4,64,768]{3,2,1,0:T(8,128)(2,1)S(1)}, bf16[4,4,64,768]{3,2,1,0:T(8,128)(2,1)}, u32[]{:S(2)}) copy-start(bf16[4,4,64,768]{3,2,1,0:T(8,128)(2,1)} %get-tuple-element.96) | copy-start | bytes 4718596
  338.1 37.9 %all-to-all-start.4 = ((bf16[8,110,640]{2,1,0:T(8,128)(2,1)}), bf16[8,110,640]{2,1,0:T(8,128)(2,1)S(1)}, u32[]{:S(2)}, u32[]{:S(2)}) async-start(bf16[8,110,640]{2,1,0:T(8,128)(2,1)} %pad_maximum_fusion), calls=%async_computation.5 | async-start | bytes 2293760 | tf_op jit(solution)/shard_map/all_to_all | solution.py:365
  375.9 57.2 %all-to-all-start.5 = ((bf16[4,256,768]{2,1,0:T(8,128)(2,1)}), bf16[4,256,768]{2,1,0:T(8,128)(2,1)S(1)}, u32[]{:S(2)}, u32[]{:S(2)}) async-start(bf16[4,256,768]{2,1,0:T(8,128)(2,1)} %bitcast.90), calls=%async_computation.6 | async-start | bytes 3145728 | tf_op jit(solution)/shard_map/all_to_all | solution.py:365
  379.5 3.0 copy-start.5
  379.5 3.0 copy-start.29
  (9 other events, 8.5 us)
Sparse Core Ops, SparseCore 0:
  9.6 39.7 all-gather.9
  51.3 41.6 all-gather.7
  94.9 54.7 all-gather.5
  212.5 89.4 reduce-scatter.1
  308.7 67.2 all-reduce.4

commit v6 on v5

--- a/solution.py
+++ b/solution.py
@@ -799,7 +799,7 @@
     packed = pad_to(jnp.concatenate(parts, 1), packed_width, 1)
     front = gather(packed)
     all_tokens = lax.all_gather(tokens[:, 0], "sp", axis=0)
-    rear_in = (out_weight, gate_weight, ffn_gate, ffn_up, ffn_down)
+    rear_in = (jnp.concatenate([out_weight, gate_weight, ffn_gate, ffn_up], 1), ffn_down)
     rear_in, front, all_tokens = lax.optimization_barrier((rear_in, front, all_tokens))
     layout = dict(groups=groups, slots=slots, local=local, micro=micro, order=order, flat=flat)
     normed, rate_slope, send, gains = front_call(all_tokens, front, layout, piece, tiles)
@@ -824,8 +824,8 @@
     mix, q, k, v, e, *saved = fwd_call(arrived, w1, b1, w2, b2, gain, shift, piece, tiles)
     w1s, w2s, z1, h, q1, n, g_, nq = saved
 
-    out_in, gate_in, fgate_in, fup_in, down_in = rear_in
-    rear = gather(jnp.concatenate([out_in, gate_in, fgate_in, fup_in], 1))
+    rear_own, down_in = rear_in
+    rear = gather(rear_own)
     out_full = rear[:, :width]
     gate_full = rear[:, width : 2 * width]
     fgate_full = rear[:, 2 * width : 2 * width + ff]
@@ -875,9 +875,11 @@
     extent = -(-inner_send.shape[1] * 128 // packed_width)
     inner_send = pad_to(inner_send.reshape(S, -1), extent * packed_width, 1).reshape(S, extent, packed_width)
     got = swap(jnp.concatenate([weight_parts, inner_send], 1), "fsdp")
-    got, normed_parts, rear_sum = lax.optimization_barrier((got, normed_parts, rear_sum))
+    got, normed_parts = lax.optimization_barrier((got, normed_parts))
+    got_sum = jnp.sum(got[:, :own].astype(f32), 0).astype(bf16)
+    weight_all = lax.all_gather(got_sum, "sp", axis=0)
+    normed_parts, rear_sum, weight_all = lax.optimization_barrier((normed_parts, rear_sum, weight_all))
     normed_parts = swap(normed_parts.reshape(Z, total, width), "sp")
-    got_sum = jnp.sum(got[:, :own].astype(f32), 0).astype(bf16)
     out_grad, gate_grad, fgate_grad, fup_grad, down_grad, gate_dot, post_grad = unpack_call(
         rear_sum, gate_weight, ffn_gate, ffn_up, post_gain[:, None], ff // S
     )
@@ -885,16 +887,14 @@
     inner_part = got[:, own:].reshape(S, -1)[:, : slots * 2 * share * 128].astype(f32)
     inner_part = jnp.sum(inner_part.reshape(groups, micro, slots, 2, share, 128), 1)
     inner_part = inner_part.transpose(1, 0, 3, 2, 4).reshape(slots * groups, share, 2 * 128)[:local]
-    rear_done = (out_grad, gate_grad, fgate_grad, fup_grad, down_grad, post_grad, gate_dot)
-    rear_done, got_sum, inner_part = lax.optimization_barrier((rear_done, got_sum, inner_part.astype(bf16)))
-    out_grad, gate_grad, fgate_grad, fup_grad, down_grad, post_grad, gate_dot = rear_done
-    inner_sum = lax.all_gather(inner_part, "fsdp", axis=1, tiled=True)
-    weight_all = lax.all_gather(got_sum, "sp", axis=0)
-    inner_sum = inner_sum.astype(f32)
     query_grad, key_grad, value_grad, rate_grad, pre_grad = finish_call(
         weight_all, query_weight, key_weight, value_weight, rate_weight, gate_dot, pre_gain[:, None], layout
     )
     pre_grad = pre_grad[:, 0]
+    rear_done = (out_grad, gate_grad, fgate_grad, fup_grad, down_grad, post_grad, pre_grad)
+    rear_done, inner_part = lax.optimization_barrier((rear_done, inner_part.astype(bf16)))
+    out_grad, gate_grad, fgate_grad, fup_grad, down_grad, post_grad, pre_grad = rear_done
+    inner_sum = lax.all_gather(inner_part, "fsdp", axis=1, tiled=True).astype(f32)
     tokens_grad = token_call(normed_parts, grad_normed_gate, own_tokens, pre_full, grad_middle)
     tail = inner_sum[:, 2 * head : 2 * head + 2].reshape(local, 2 * inner)
     return (

time: 445 us -> 435 us (0.978)
  waiting for transfers between devices: 104 us -> 80.9 us
  blocking collectives: 46.6 us -> 63.8 us
    psum x1, waiting for transfers between devices: 34.3 us -> 5.54 us  [shards(): rear_sum = lax.psum(rear_part, 'sp')]
    all_to_all x0 -> x1, blocking collectives: none -> 18.8 us  [swap(): return lax.all_to_all(block, axes, split_axis=0, concat_axis=0, tiled=True)]
    all_to_all x6 -> x5, waiting for transfers between devices: 45.5 us -> 51.4 us  [swap(): return lax.all_to_all(block, axes, split_axis=0, concat_axis=0, tiled=True)]
    all_to_all x6 -> x5, starting transfers between devices: 21.2 us -> 18.3 us  [swap(): return lax.all_to_all(block, axes, split_axis=0, concat_axis=0, tiled=True)]
  transfers between devices with their start and end apart: 11 -> 10, of which waited for: 6 -> 7; matrix products, arithmetic and copies ran while one was open for 9% -> 9% of each run, Pallas kernels for 43% -> 45%
where the time goes in v6:
time: 435 us; the launch traced here: 434 us
  Pallas kernels  210 us (48%)
  waiting for transfers between devices  80.9 us (19%)
  blocking collectives  63.8 us (15%)
  local copies, waits for them, and re-layouts  20.5 us (5%)
  starting transfers between devices  18.7 us (4%)
  matrix products  16.7 us (4%)
  between operations  14.5 us (3%)
  other arithmetic  8.86 us (2%)
    pallas_call x1, Pallas kernels, bwd_call(): pl.pallas_call(functools.partial(bwd_kernel, slots, count, unroll, piece,...  87 us
    pallas_call x1, Pallas kernels, fwd_call(): pl.pallas_call(functools.partial(fwd_kernel, slots, count, unroll, piece,...  73.7 us
    all_to_all x5, waiting for transfers between devices, swap(): return lax.all_to_all(block, axes, split_axis=0, concat_axis=0, tiled=True)  51.4 us
    all_gather x1, blocking collectives, shards(): weight_all = lax.all_gather(got_sum, 'sp', axis=0)  22.3 us
    all_gather x1, waiting for transfers between devices, shards(): all_tokens = lax.all_gather(tokens[:, 0], 'sp', axis=0)  20.9 us
    all_to_all x1, blocking collectives, swap(): return lax.all_to_all(block, axes, split_axis=0, concat_axis=0, tiled=True)  18.8 us
    all_to_all x5, starting transfers between devices, swap(): return lax.all_to_all(block, axes, split_axis=0, concat_axis=0, tiled=True)  18.3 us
    pallas_call x1, Pallas kernels, rear_grad_call(): pl.pallas_call(functools.partial(rear_grad_kernel, starts, per_step), gri...  14.5 us
  transfers between devices with their start and end apart: 10, of which 7 were waited for; matrix products, arithmetic and copies ran while one was open for 9% of the time, Pallas kernels for 45%

profile of v6, /device:TPU:0, one launch (start us, length us, event | category | flops | bytes accessed | tf_op | source)
XLA Modules:
  0.0 434.0 jit_solution(17024300403589438589)
XLA Ops:
  14.1 13.3 %all_gather.21.w_ref.front_ref = bf16[768,640]{1,0:T(8,128)(2,1)} all-gather(bf16[96,640]{1,0:T(8,128)(2,1)S(1)} %pad.13), channel_id=1, replica_groups=mesh['sp'=4,'fsdp'=8] {'fsdp'}, dimensions={0}, use_global_device_ids=true | all-gather | bytes 1105920 | tf_op jit(solution)/shard_map/all_gather | solution.py:361
  28.6 20.9 %all-gather.10.cloned.1.call-done = bf16[16,1,64,768]{3,2,1,0:T(8,128)(2,1)} async-done(((bf16[4,1,64,768]{3,2,1,0:T(8,128)(2,1)}), bf16[16,1,64,768]{3,2,1,0:T(8,128)(2,1)}) %all-gather.10.cloned.1.call-update) | async-done | bytes 1572880 | tf_op jit(solution)/shard_map/all_gather | solution.py:801
  51.6 6.1 %front.1 = (bf16[4,4,64,768]{3,2,1,0:T(8,128)(2,1)}, f32[4,4,64,128]{3,2,1,0:T(8,128)}, bf16[2,4,784,128]{3,2,1,0:T(8,128)(2,1)}, f32[2,768]{1,0:T(2,128)}) custom-call(bf16[4,4,64,768]{3,2,1,0:T(8,128)(2,1)} %bitcast.132, bf16[768,640]{1,0:T(8,128)(2,1)} %all_gather.21.w_ref.front_ref), custom_call_target="tpu_custom_call" | custom-call | flops 1000000000 | bytes 7000000 | tf_op jit(solution)/shard_map/front/pallas_call | solution.py:730
  57.8 3.8 all-to-all-start
  66.6 19.6 %all-to-all-done.x_ref = bf16[8,784,128]{2,1,0:T(8,128)(2,1)S(1)} async-done(((bf16[8,784,128]{2,1,0:T(8,128)(2,1)}), bf16[8,784,128]{2,1,0:T(8,128)(2,1)S(1)}, u32[]{:S(2)}, u32[]{:S(2)}) %all-to-all-start) | async-done | bytes 1605664 | tf_op jit(solution)/shard_map/all_to_all | solution.py:365
  87.5 73.7 %inner_forward.1 = (bf16[2048,128]{1,0:T(8,128)(2,1)}, bf16[2,2048,64]{2,1,0:T(8,128)(2,1)}, bf16[2,2048,64]{2,1,0:T(8,128)(2,1)}, bf16[2,2048,64]{2,1,0:T(8,128...) custom-call(bf16[8,784,128]{2,1,0:T(8,128)(2,1)} %copy-done.2, ...), custom_call_target="tpu_custom_call" | custom-call | flops 89999998976 | bytes 40000000 | tf_op jit(solution)/shard_map/inner_forward/pallas_call | solution.py:168
  161.1 3.3 all-to-all-start.1
  167.0 4.3 fusion.15.gh_ref
  171.3 3.1 multiply_add_fusion
  174.4 4.4 %all-to-all-done.1 = bf16[32,64,128]{2,1,0:T(8,128)(2,1)S(1)} async-done(((bf16[32,64,128]{2,1,0:T(8,128)(2,1)}), bf16[32,64,128]{2,1,0:T(8,128)(2,1)S(1)}, u32[]{:S(2)}, u32[]{:S(2)}) %all-to-all-start.1) | async-done | bytes 524320 | tf_op jit(solution)/shard_map/all_to_all | solution.py:365
  179.6 13.5 %rear.1 = (bf16[8,4,64,128]{3,2,1,0:T(8,128)(2,1)}, bf16[2,768,256]{2,1,0:T(8,128)(2,1)}, bf16[256,5632]{1,0:T(8,128)(2,1)}, bf16[256,2048]{1,0:T(8,128)(2,1)}, f32[256,768]{1,0:T(8,128)}, /*index=5*/f32[256,768]{1,0:T(8,128)}) custom-call(bf16[8,4,64,128]{3,2,1,0:T(8,128)(2,1)} %bitcast.100, f32[256,768]{1,0:T(8,128)} %get-tuple-element.98.act_ref, ...), custom_call_target="tpu_custom_call" | custom-call | flops 5000000000 | bytes 16000000 | tf_op jit(solution)/shard_map/rear/pallas_call | solution.py:549
  193.1 4.1 all-to-all-start.2
  197.4 14.5 %rear_gradients.1 = bf16[8,2880,256]{2,1,0:T(8,128)(2,1)} custom-call(bf16[2,768,256]{2,1,0:T(8,128)(2,1)} %get-tuple-element.109.lhs_ref, bf16[768,256]{1,0:T(8,128)(2,1)} %bitcast.93, bf16[768,256]{1,0:T(8,128)(2,1)} %fusion.23.low_ref, bf16[256,5632]{1,0:T(8,128)(2,1)} %get-tuple-element.112.rhs_ref, bf16[256,2048]{1,0:T(8,128)(2,1)} %get-tuple-element.103.hid_ref), custom_call_target="tpu_custom_call" | custom-call | flops 4000000000 | bytes 16000000 | tf_op jit(solution)/shard_map/rear_gradients/pallas_call | solution.py:608
  212.7 87.0 %inner_backward.1 = (bf16[8,784,128]{2,1,0:T(8,128)(2,1)}, f32[2,64,256]{2,1,0:T(8,128)}, f32[2,1,256]{2,1,0:T(1,128)}, f32[2,64,256]{2,1,0:T(8,128)}, f32[2,1,6...) custom-call(bf16[2,2048,64]{2,1,0:T(8,128)(2,1)} %get-tuple-element.104.q_ref, ...), custom_call_target="tpu_custom_call" | custom-call | flops 109999996928 | bytes 40000000 | tf_op jit(solution)/shard_map/inner_backward/pallas_call | solution.py:342
  299.8 1.7 reduce-scatter.2.cloned.1.call-done
  301.5 3.6 all-to-all-start.3
  305.8 20.6 %all-to-all-done.3.a_ref = bf16[8,784,128]{2,1,0:T(8,128)(2,1)S(1)} async-done(((bf16[8,784,128]{2,1,0:T(8,128)(2,1)}), bf16[8,784,128]{2,1,0:T(8,128)(2,1)S(1)}, u32[]{:S(2)}, u32[]{:S(2)}) %all-to-all-start.3) | async-done | bytes 1605664 | tf_op jit(solution)/shard_map/all_to_all | solution.py:365
  327.6 6.0 %projection_gradients.1 = (bf16[4,4,64,640]{3,2,1,0:T(8,128)(2,1)}, bf16[4,4,64,768]{3,2,1,0:T(8,128)(2,1)}) custom-call(bf16[8,784,128]{2,1,0:T(8,128)(2,1)} %copy-done.1, f32[4,4,64,128]{3,2,1,0:T(8,128)} %get-tuple-element.125.slope_ref, bf16[768,640]{1,0:T(8,128)(2,1)} %all_gather.21.w_ref.front_ref), custom_call_target="tpu_custom_call" | custom-call | flops 1000000000 | bytes 8000000 | tf_op jit(solution)/shard_map/projection_gradients/pallas_call | solution.py:428
  333.6 2.7 bitcast_convert_fusion
  336.5 18.8 %all_to_all.30 = bf16[8,110,640]{2,1,0:T(8,128)(2,1)S(1)} all-to-all(bf16[8,110,640]{2,1,0:T(8,128)(2,1)S(1)} %pad_maximum_fusion), channel_id=1, replica_groups=mesh['sp'=4,'fsdp'=8] {'fsdp'}, dimensions={0} | all-to-all | bytes 2252800 | tf_op jit(solution)/shard_map/all_to_all | solution.py:365
  355.4 22.3 %all-gather.1 = bf16[384,640]{1,0:T(8,128)(2,1)} all-gather(bf16[96,640]{1,0:T(8,128)(2,1)S(1)} %slice_reduce_fusion), channel_id=3, replica_groups=mesh['sp'=4,'fsdp'=8] {'sp'}, dimensions={0}, use_global_device_ids=true | all-gather | bytes 614400 | tf_op jit(solution)/shard_map/all_gather | solution.py:880
  377.7 5.5 %all-reduce.5.cloned.1.call-done.sum_ref = bf16[2880,256]{1,0:T(8,128)(2,1)} async-done(((bf16[2880,256]{1,0:T(8,128)(2,1)}), bf16[2880,256]{1,0:T(8,128)(2,1)}) %all-reduce.5.cloned.1.call-update) | async-done | bytes 1474576 | tf_op jit(solution)/shard_map/psum | solution.py:862
  383.2 3.6 all-to-all-start.5
  386.8 2.9 fusion.1.gate_ref
  389.8 3.6 fusion
  393.9 3.5 rear_unpack.1
  397.4 1.4 reduce.5
  398.8 2.5 weight_gradients.1
  402.7 9.3 %all_gather.27 = bf16[3,136,256]{2,0,1:T(4,128)(2,1)S(1)} all-gather(bf16[3,17,256]{2,0,1:T(4,128)(2,1)S(1)} %bitcast.107), channel_id=1, replica_groups=mesh['sp'=4,'fsdp'=8] {'fsdp'}, dimensions={1}, use_global_device_ids=true | all-gather | bytes 235008 | tf_op jit(solution)/shard_map/all_gather | solution.py:897
  412.2 1.5 copy.120
  416.4 6.7 %all-to-all-done.5.parts_ref = bf16[4,256,768]{2,1,0:T(8,128)(2,1)S(1)} async-done(((bf16[4,256,768]{2,1,0:T(8,128)(2,1)}), bf16[4,256,768]{2,1,0:T(8,128)(2,1)S(1)}, u32[]{:S(2)}, u32[]{:S(2)}) %all-to-all-start.5) | async-done | bytes 1572896 | tf_op jit(solution)/shard_map/all_to_all | solution.py:365
  424.3 3.2 token_gradients.1
  (164 shorter events, 28.3 us)
Async XLA Ops:
  7.2 20.2 %copy-start.3 = (bf16[96,2048]{1,0:T(8,128)(2,1)S(1)}, bf16[96,2048]{1,0:T(8,128)(2,1)}, u32[]{:S(2)}) copy-start(bf16[96,2048]{1,0:T(8,128)(2,1)} %fup_w.1) | copy-start | bytes 1179652
  7.2 20.2 %copy-start.4 = (bf16[96,2048]{1,0:T(8,128)(2,1)S(1)}, bf16[96,2048]{1,0:T(8,128)(2,1)}, u32[]{:S(2)}) copy-start(bf16[96,2048]{1,0:T(8,128)(2,1)} %fgate_w.1) | copy-start | bytes 1179652
  7.2 20.2 %copy-start.6 = (bf16[96,768]{1,0:T(8,128)(2,1)S(1)}, bf16[96,768]{1,0:T(8,128)(2,1)}, u32[]{:S(2)}) copy-start(bf16[96,768]{1,0:T(8,128)(2,1)} %gate_w.1) | copy-start | bytes 442372
  7.2 20.2 %copy-start.14 = (bf16[96,768]{1,0:T(8,128)(2,1)S(1)}, bf16[96,768]{1,0:T(8,128)(2,1)}, u32[]{:S(2)}) copy-start(bf16[96,768]{1,0:T(8,128)(2,1)} %param.29) | copy-start | bytes 442372
  7.2 42.2 %all-gather.10.cloned.1.call-start = ((), (), s32[]{:S(2)}) async-start(), calls=%async_computation.11 | async-start | bytes 1966080 | tf_op jit(solution)/shard_map/all_gather | solution.py:801
  8.0 159.0 %all-gather.8.cloned.1.call-start = ((), (), s32[]{:S(2)}) async-start(), calls=%async_computation.8 | async-start | bytes 3538944 | tf_op jit(solution)/shard_map/all_gather | solution.py:361
  8.8 19.8 %copy-start.12 = (bf16[96,1]{1,0:T(8,128)(2,1)}, bf16[96,1]{1,0:T(8,128)(2,1)S(1)}, u32[]{:S(2)}) copy-start(bf16[96,1]{1,0:T(8,128)(2,1)S(1)} %copy.101.pre_ref) | copy-start | bytes 580
  9.6 4.3 copy-start.13
  10.4 18.2 %copy-start.11 = (bf16[96,1]{1,0:T(8,128)(2,1)}, bf16[96,1]{1,0:T(8,128)(2,1)S(1)}, u32[]{:S(2)}) copy-start(bf16[96,1]{1,0:T(8,128)(2,1)S(1)} %copy.102.post_ref) | copy-start | bytes 580
  27.4 22.9 %copy-start.28 = (s32[4]{0:T(128)S(1)}, s32[4]{0:T(128)}, u32[]{:S(2)}) copy-start(s32[4]{0:T(128)} %param.21) | copy-start | bytes 52
  27.5 23.0 %copy-start.10 = (bf16[4,1,64,768]{3,2,1,0:T(8,128)(2,1)S(1)}, bf16[4,1,64,768]{3,2,1,0:T(8,128)(2,1)}, u32[]{:S(2)}) copy-start(bf16[4,1,64,768]{3,2,1,0:T(8,128)(2,1)} %param.22) | copy-start | bytes 1179652
  49.5 2.0 copy-start.22
  49.5 2.0 copy-start.17
  49.6 121.7 %all-gather.6.cloned.1.call-start = ((), (), s32[]{:S(2)}) async-start(), calls=%async_computation.7 | async-start | bytes 9732096 | tf_op jit(solution)/shard_map/all_gather | solution.py:361
  57.8 6.0 %copy-start.18 = (f32[3,64,256]{2,1,0:T(8,128)S(1)}, f32[3,64,256]{2,1,0:T(8,128)}, u32[]{:S(2)}) copy-start(f32[3,64,256]{2,1,0:T(8,128)} %param.34) | copy-start | bytes 589828
  57.8 28.5 %all-to-all-start = ((bf16[8,784,128]{2,1,0:T(8,128)(2,1)}), bf16[8,784,128]{2,1,0:T(8,128)(2,1)S(1)}, u32[]{:S(2)}, u32[]{:S(2)}) async-start(bf16[8,784,128]{2,1,0:T(8,128)(2,1)} %bitcast.89), calls=%async_computation | async-start | bytes 3211264 | tf_op jit(solution)/shard_map/all_to_all | solution.py:365
  161.1 5.3 %copy-start.19 = (f32[2,768]{1,0:T(2,128)S(1)}, f32[2,768]{1,0:T(2,128)}, u32[]{:S(2)}) copy-start(f32[2,768]{1,0:T(2,128)} %get-tuple-element.100) | copy-start | bytes 18436
  161.1 17.7 %all-to-all-start.1 = ((bf16[32,64,128]{2,1,0:T(8,128)(2,1)}), bf16[32,64,128]{2,1,0:T(8,128)(2,1)S(1)}, u32[]{:S(2)}, u32[]{:S(2)}) async-start(bf16[32,64,128]{2,1,0:T(8,128)(2,1)} %bitcast.99), calls=%async_computation.1 | async-start | bytes 1048576 | tf_op jit(solution)/shard_map/all_to_all | solution.py:365
  193.1 18.8 %all-to-all-start.2 = ((bf16[32,64,128]{2,1,0:T(8,128)(2,1)}), bf16[32,64,128]{2,1,0:T(8,128)(2,1)S(1)}, u32[]{:S(2)}, u32[]{:S(2)}) async-start(bf16[32,64,128]{2,1,0:T(8,128)(2,1)} %bitcast.101), calls=%async_computation.2 | async-start | bytes 1048576 | tf_op jit(solution)/shard_map/all_to_all | solution.py:365
  197.2 104.3 %reduce-scatter.2.cloned.1.call-start = ((), (), s32[]{:S(2)}) async-start(), calls=%async_computation.9 | async-start | bytes 13271040 | tf_op jit(solution)/shard_map/reduce_scatter | solution.py:854
  299.7 5.4 %copy-start.20 = (f32[2,1,64]{2,1,0:T(1,128)S(1)}, f32[2,1,64]{2,1,0:T(1,128)}, u32[]{:S(2)}) copy-start(f32[2,1,64]{2,1,0:T(1,128)} %get-tuple-element.130) | copy-start | bytes 1540
  299.7 5.6 %copy-start.24 = (f32[2,1,64]{2,1,0:T(1,128)S(1)}, f32[2,1,64]{2,1,0:T(1,128)}, u32[]{:S(2)}) copy-start(f32[2,1,64]{2,1,0:T(1,128)} %get-tuple-element.131) | copy-start | bytes 1540
  299.7 5.6 %copy-start.23 = (f32[2,1,64]{2,1,0:T(1,128)S(1)}, f32[2,1,64]{2,1,0:T(1,128)}, u32[]{:S(2)}) copy-start(f32[2,1,64]{2,1,0:T(1,128)} %get-tuple-element.132) | copy-start | bytes 1540
  299.8 5.6 %copy-start.21 = (f32[2,1,256]{2,1,0:T(1,128)S(1)}, f32[2,1,256]{2,1,0:T(1,128)}, u32[]{:S(2)}) copy-start(f32[2,1,256]{2,1,0:T(1,128)} %get-tuple-element.129) | copy-start | bytes 6148
  299.8 5.8 %copy-start.9 = (f32[2,64,256]{2,1,0:T(8,128)S(1)}, f32[2,64,256]{2,1,0:T(8,128)}, u32[]{:S(2)}) copy-start(f32[2,64,256]{2,1,0:T(8,128)} %get-tuple-element.128) | copy-start | bytes 393220
  299.8 5.8 %copy-start.15 = (f32[2,64,256]{2,1,0:T(8,128)S(1)}, f32[2,64,256]{2,1,0:T(8,128)}, u32[]{:S(2)}) copy-start(f32[2,64,256]{2,1,0:T(8,128)} %get-tuple-element.127) | copy-start | bytes 393220
  301.5 24.9 %all-to-all-start.3 = ((bf16[8,784,128]{2,1,0:T(8,128)(2,1)}), bf16[8,784,128]{2,1,0:T(8,128)(2,1)S(1)}, u32[]{:S(2)}, u32[]{:S(2)}) async-start(bf16[8,784,128]{2,1,0:T(8,128)(2,1)} %get-tuple-element.124), calls=%async_computation.4 | async-start | bytes 3211264 | tf_op jit(solution)/shard_map/all_to_all | solution.py:365
  305.1 78.1 %all-reduce.5.cloned.1.call-start = ((), (), s32[]{:S(2)}) async-start(), calls=%async_computation.10 | async-start | bytes 2949120 | tf_op jit(solution)/shard_map/psum | solution.py:862
  305.8 27.8 %copy-start.16 = (bf16[4,4,64,768]{3,2,1,0:T(8,128)(2,1)S(1)}, bf16[4,4,64,768]{3,2,1,0:T(8,128)(2,1)}, u32[]{:S(2)}) copy-start(bf16[4,4,64,768]{3,2,1,0:T(8,128)(2,1)} %get-tuple-element.94) | copy-start | bytes 4718596
  383.2 39.9 %all-to-all-start.5 = ((bf16[4,256,768]{2,1,0:T(8,128)(2,1)}), bf16[4,256,768]{2,1,0:T(8,128)(2,1)S(1)}, u32[]{:S(2)}, u32[]{:S(2)}) async-start(bf16[4,256,768]{2,1,0:T(8,128)(2,1)} %bitcast.90), calls=%async_computation.6 | async-start | bytes 3145728 | tf_op jit(solution)/shard_map/all_to_all | solution.py:365
  386.8 3.0 copy-start.5
  386.8 3.0 copy-start.29
  (8 other events, 9.3 us)
Sparse Core Ops, SparseCore 0:
  9.6 39.7 all-gather.9
  51.3 41.6 all-gather.7
  95.0 54.6 all-gather.5
  212.0 89.4 reduce-scatter.1
  308.1 75.0 all-reduce.4

commit v7 on v6

--- a/solution.py
+++ b/solution.py
@@ -52,29 +52,32 @@
     lower=lax.broadcasted_iota(jnp.int32,(MINI,MINI),0)>=lax.broadcasted_iota(jnp.int32,(MINI,MINI),1)
     return lower.astype(f32), jnp.where(lower,0.0,1.0)
 
+def split_rows(slots,piece,tiles,x_ref,q_ref,k_ref,v_ref,e_ref):
+    eye=lax.broadcasted_iota(jnp.int32,(128,128),0)==lax.broadcasted_iota(jnp.int32,(128,128),1)
+    @pl.loop(0,x_ref.shape[0])
+    def _(src):
+        base=pl.multiple_of(src*piece,piece)
+        for j in range(slots):
+            for index,ref in enumerate((q_ref,k_ref,v_ref)):
+                lane=(3*j+index)*64
+                top=lane//128*piece
+                ref[j,pl.ds(base,piece)]=x_ref[src,top:top+piece,lane%128:lane%128+64]
+        rates=x_ref[src,tiles*piece:tiles*piece+16].astype(f32)
+        for j in range(slots):
+            for i in range(piece//128):
+                n=j*(piece//128)+i
+                column=jnp.sum(jnp.where(eye,rates[n:n+1],0.0),1,keepdims=True)
+                e_ref[j,pl.ds(base+i*128,128)]=jnp.broadcast_to(column,(128,128))
+
 def fwd_kernel(slots,count,unroll,piece,tiles,x_ref,w1_ref,b1_ref,w2_ref,b2_ref,gain_ref,shift_ref,
-    mix_ref,q_ref,k_ref,v_ref,e_ref,w1s_ref,w2s_ref,z1_ref,h_ref,q1_ref,n_ref,g_ref,nq_ref,
-    W1,B1,W2,B2,Z,ZQ,AP,EP):
+    mix_ref,w1s_ref,w2s_ref,z1_ref,h_ref,q1_ref,n_ref,g_ref,nq_ref,
+    q_ref,k_ref,v_ref,e_ref,W1,B1,W2,B2,Z,ZQ,AP,EP):
     lower,upper=masks()
     steps=q_ref.shape[1]//MINI
     pid=pl.program_id(0)
     @pl.when(pid==0)
     def _():
-        eye=lax.broadcasted_iota(jnp.int32,(128,128),0)==lax.broadcasted_iota(jnp.int32,(128,128),1)
-        @pl.loop(0,x_ref.shape[0])
-        def _(src):
-            base=pl.multiple_of(src*piece,piece)
-            for j in range(slots):
-                for index,ref in enumerate((q_ref,k_ref,v_ref)):
-                    lane=(3*j+index)*64
-                    top=lane//128*piece
-                    ref[j,pl.ds(base,piece)]=x_ref[src,top:top+piece,lane%128:lane%128+64]
-            rates=x_ref[src,tiles*piece:tiles*piece+16].astype(f32)
-            for j in range(slots):
-                for i in range(piece//128):
-                    n=j*(piece//128)+i
-                    column=jnp.sum(jnp.where(eye,rates[n:n+1],0.0),1,keepdims=True)
-                    e_ref[j,pl.ds(base+i*128,128)]=jnp.broadcast_to(column,(128,128))
+        split_rows(slots,piece,tiles,x_ref,q_ref,k_ref,v_ref,e_ref)
         for j in range(slots):
             W1[j]=w1_ref[j]; B1[j]=b1_ref[j]; W2[j]=w2_ref[j]; B2[j]=b2_ref[j]
             Z[j]=nn(k_ref[j,:MINI],w1_ref[j])+b1_ref[j]
@@ -120,7 +123,7 @@
         yield
         H=nn(Gb,w2b)
         E2=e64*G; E2b=E2.astype(bf16)
-        n_ref[j,rows]=(z-mz).astype(bf16); g_ref[j,rows]=Gb
+        n_ref[j,brow]=(z-mz).astype(bf16); g_ref[j,brow]=Gb
         EP[j]=E2b; AP[j]=Ab
         yield
         W2[j]=w2-tn(E2b,Ab)
@@ -168,22 +171,23 @@
     return pl.pallas_call(functools.partial(fwd_kernel,slots,count,unroll,piece,tiles),
         grid=(nb,),
         in_specs=[full(a.shape) for a in (x,w1,b1,w2,b2,gain,shift)],
-        out_specs=[rm_,r64,r64,r64,r1,st,st,row(256),row(256),row(256),r64,r64,r64],
-        out_shape=[S((length,64*slots),bf16)]+[S((slots,length,64),bf16)]*3+[S((slots,length,128),f32)]+[S((slots,steps,64,256),bf16)]*2+[S((slots,length,256),bf16)]*3+[S((slots,length,64),bf16)]*3,
-        scratch_shapes=[pltpu.VMEM((slots,64,256),f32),pltpu.VMEM((slots,1,256),f32),pltpu.VMEM((slots,64,256),f32),pltpu.VMEM((slots,1,64),f32),pltpu.VMEM((slots,MINI,256),f32),pltpu.VMEM((slots,MINI,256),f32),pltpu.VMEM((slots,MINI,256),bf16),pltpu.VMEM((slots,MINI,64),bf16)],
+        out_specs=[rm_,st,st,row(256),row(256),row(256),row(64),row(64),r64],
+        out_shape=[S((length,64*slots),bf16)]+[S((slots,steps,64,256),bf16)]*2+[S((slots,length,256),bf16)]*3+[S((slots,length,64),bf16)]*3,
+        scratch_shapes=[pltpu.VMEM((slots,length,64),bf16)]*3+[pltpu.VMEM((slots,length,128),f32)]+[pltpu.VMEM((slots,64,256),f32),pltpu.VMEM((slots,1,256),f32),pltpu.VMEM((slots,64,256),f32),pltpu.VMEM((slots,1,64),f32),pltpu.VMEM((slots,MINI,256),f32),pltpu.VMEM((slots,MINI,256),f32),pltpu.VMEM((slots,MINI,256),bf16),pltpu.VMEM((slots,MINI,64),bf16)],
         compiler_params=pltpu.CompilerParams(dimension_semantics=("arbitrary",),vmem_limit_bytes=VMEM_BYTES),
         name="inner_forward",cost_estimate=pl.CostEstimate(flops=90_000_000_000,bytes_accessed=40_000_000,transcendentals=0),**kw)(x,w1,b1,w2,b2,gain,shift)
 
 
-def bwd_kernel(slots,count,unroll,piece,tiles,q_ref,k_ref,v_ref,e_ref,dx_ref,n_ref,g_ref,nq_ref,w1s_ref,w2s_ref,z1_ref,h_ref,q1_ref,gain_ref,shift_ref,
+def bwd_kernel(slots,count,unroll,piece,tiles,x_ref,dx_ref,n_ref,g_ref,nq_ref,w1s_ref,w2s_ref,z1_ref,h_ref,q1_ref,gain_ref,shift_ref,
     out_ref,dw1_ref,db1_ref,dw2_ref,db2_ref,dgn_ref,dsh_ref,
-    do_ref,de_ref,    DW1,DB1,G2,DB2,KD,DGN,DSH,DGQ,DSQ,
+    q_ref,k_ref,v_ref,e_ref,do_ref,de_ref,    DW1,DB1,G2,DB2,KD,DGN,DSH,DGQ,DSQ,
     sA,sAd,sHA,sGZ,sE1,sE2,sW1,sW2,sR1,sR2,sDA,sQ1,sQ2,sAQ,sb1,sb2):
     lower,_=masks()
     steps=q_ref.shape[1]//MINI
     pid=pl.program_id(0); nb=pl.num_programs(0)
     @pl.when(pid==0)
     def _():
+        split_rows(slots,piece,tiles,x_ref,q_ref,k_ref,v_ref,e_ref)
         @pl.loop(0,out_ref.shape[0])
         def _(src):
             rows=pl.ds(pl.multiple_of(src*piece,piece),piece)
@@ -329,8 +333,8 @@
             dw1_ref[j]=DW1[j]; db1_ref[j]=DB1[j]; dw2_ref[j]=G2[j]; db2_ref[j]=DB2[j]
             dgn_ref[j]=jnp.sum(DGN[j]+DGQ[j],0,keepdims=True); dsh_ref[j]=jnp.sum(DSH[j]+DSQ[j],0,keepdims=True)
 
-def bwd_call(q,k,v,e,dO,n,g,nq,w1s,w2s,z1,h,q1,gain,shift,piece,tiles,block=256,unroll=2,**kw):
-    slots,length,_=q.shape
+def bwd_call(x,dO,n,g,nq,w1s,w2s,z1,h,q1,gain,shift,piece,tiles,block=256,unroll=2,**kw):
+    slots,length,_=n.shape
     count=block//MINI; nb=length//block; steps=length//MINI
     row=lambda w: pl.BlockSpec((slots,block,w),lambda i:(0,nb-1-i,0))
     full=lambda s: pl.BlockSpec(s,lambda i:(0,)*len(s),pipeline_mode=pl.Buffered(1))
@@ -341,14 +345,14 @@
     V=lambda *s,d=f32: pltpu.VMEM(s,d)
     return pl.pallas_call(functools.partial(bwd_kernel,slots,count,unroll,piece,tiles),
         grid=(nb,),
-        in_specs=[r64]*3+[r1,full(dO.shape)]+[r64]*3+[st,st]+[row(256)]*3+[full(gain.shape)]*2,
+        in_specs=[full(x.shape),full(dO.shape)]+[r64]*3+[st,st]+[row(256)]*3+[full(gain.shape)]*2,
         out_specs=[full(o[0]) for o in outs],
         out_shape=[S(*o) for o in outs],
-        scratch_shapes=[V(slots,length,64,d=bf16),V(slots,length,1),V(slots,64,256),V(slots,1,256),V(slots,64,256),V(slots,1,64),V(slots,MINI,256),V(slots,MINI,64),V(slots,MINI,64),V(slots,MINI,64),V(slots,MINI,64),
+        scratch_shapes=[V(slots,length,64,d=bf16)]*3+[V(slots,length,128)]+[V(slots,length,64,d=bf16),V(slots,length,1),V(slots,64,256),V(slots,1,256),V(slots,64,256),V(slots,1,64),V(slots,MINI,256),V(slots,MINI,64),V(slots,MINI,64),V(slots,MINI,64),V(slots,MINI,64),
           V(2,slots,MINI,256,d=bf16),V(2,slots,MINI,256),V(2,slots,MINI,256),V(2,slots,MINI,256),V(2,slots,MINI,256,d=bf16),V(2,slots,MINI,64,d=bf16),
           V(2,slots,64,256,d=bf16),V(2,slots,64,256,d=bf16),V(2,slots,MINI,256),V(2,slots,MINI,64),V(2,slots,MINI,256),V(2,slots,MINI,256,d=bf16),V(2,slots,MINI,64,d=bf16),V(2,slots,MINI,256,d=bf16),V(2,slots,1,256),V(2,slots,1,64)],
         compiler_params=pltpu.CompilerParams(dimension_semantics=("arbitrary",),vmem_limit_bytes=VMEM_BYTES),
-        name="inner_backward",cost_estimate=pl.CostEstimate(flops=110_000_000_000,bytes_accessed=40_000_000,transcendentals=0),**kw)(q,k,v,e,dO,n,g,nq,w1s,w2s,z1,h,q1,gain,shift)
+        name="inner_backward",cost_estimate=pl.CostEstimate(flops=110_000_000_000,bytes_accessed=40_000_000,transcendentals=0),**kw)(x,dO,n,g,nq,w1s,w2s,z1,h,q1,gain,shift)
 
 
 def rms_back(grad_scaled, inputs, scale):
@@ -478,12 +482,23 @@
     )(gathered, q_w, k_w, v_w, r_w, gate_dot, pre)
 
 
-def rear_kernel(layout, got_ref, act_ref, slope_ref, tok_ref, w_ref, post_ref, gh_ref, go_ref,
-                send_ref, lhs_ref, rhs_ref, hid_ref, gm_ref, mid_ref):
+def rear_kernel(layout, got_ref, act_ref, slope_ref, tok_ref, w_hbm, post_ref, gh_ref, go_ref,
+                send_ref, lhs_ref, rhs_ref, hid_ref, gm_ref, mid_ref, w_all, sems):
     groups, slots, local, micro = layout["groups"], layout["slots"], layout["local"], layout["micro"]
     Z, rows = got_ref.shape[1], got_ref.shape[2]
     total, width = act_ref.shape
     ff = hid_ref.shape[1]
+    w_ref = w_all
+    part = 512
+    regions = [(0, width)]
+    for c in range(ff // part):
+        regions += [(2 * width + c * part, part), (2 * width + ff + c * part, part)]
+    copies = [
+        pltpu.make_async_copy(w_hbm.at[:, pl.ds(first, size)], w_all.at[:, pl.ds(first, size)], sems.at[n])
+        for n, (first, size) in enumerate(regions)
+    ]
+    for copy in copies:
+        copy.start()
     blocks = []
     for m in range(micro):
         pieces = []
@@ -493,6 +508,7 @@
                 pieces.append(got_ref[h * micro + m, z, :, 64 * j : 64 * j + 64])
         blocks.append(jnp.concatenate(pieces, 1))
     mixed = cat(*blocks).astype(f32)
+    copies[0].wait()
     gated = (act_ref[...] * mixed).astype(bf16)
     lhs_ref[0] = gated.T
     middle = tok_ref[...].astype(f32) + nn(gated, w_ref[:, :width])
@@ -504,8 +520,7 @@
     gm_ref[...] = jnp.zeros((total, width), f32)
     step = 256
 
-    @pl.loop(0, ff // step)
-    def _(c):
+    def chunk(c):
         here = pl.ds(pl.multiple_of(c * step, step), step)
         gate_at = pl.ds(pl.multiple_of(2 * width + c * step, step), step)
         up_at = pl.ds(pl.multiple_of(2 * width + ff + c * step, step), step)
@@ -520,6 +535,11 @@
         rhs_ref[:, gate_at] = g_gate
         rhs_ref[:, up_at] = g_up
         gm_ref[...] += nt(g_gate, gate_w) + nt(g_up, up_w)
+
+    for n in range(ff // part):
+        copies[1 + 2 * n].wait()
+        copies[2 + 2 * n].wait()
+        pl.loop(n * (part // step), (n + 1) * (part // step))(chunk)
 
     middle = mid_ref[...]
     grad_middle = go_ref[...].astype(f32) + rms_back(gm_ref[...] * post, middle, scale)
@@ -546,8 +566,12 @@
     total, width = act.shape
     ff = grad_hidden.shape[1]
     S_ = jax.ShapeDtypeStruct
+    specs = [pl.BlockSpec(memory_space=pltpu.VMEM)] * 8
+    specs[4] = pl.BlockSpec(memory_space=pl.ANY)
     return pl.pallas_call(
         functools.partial(rear_kernel, layout),
+        in_specs=specs,
+        scratch_shapes=[pltpu.VMEM(weights.shape, bf16), pltpu.SemaphoreType.DMA((1 + 2 * (ff // 512),))],
         out_shape=[
             S_(got.shape, bf16), S_((2, width, total), bf16), S_((total, weights.shape[1]), bf16),
             S_((total, ff), bf16), S_((total, width), f32), S_((total, width), f32),
@@ -821,7 +845,7 @@
     b2 = b2 - jnp.mean(b2, -1, keepdims=True)
     gain = of_slots(inner_gain)[:, None]
     shift = of_slots(inner_shift)[:, None]
-    mix, q, k, v, e, *saved = fwd_call(arrived, w1, b1, w2, b2, gain, shift, piece, tiles)
+    mix, *saved = fwd_call(arrived, w1, b1, w2, b2, gain, shift, piece, tiles)
     w1s, w2s, z1, h, q1, n, g_, nq = saved
 
     rear_own, down_in = rear_in
@@ -856,7 +880,7 @@
     grad_normed_gate = nt(rhs[:, width : 2 * width], gate_full)
 
     packed_back, dw1, db1, dw2, db2, dgn, dsh = bwd_call(
-        q, k, v, e, d_mix, n, g_, nq, w1s, w2s, z1, h, q1, gain, shift, piece, tiles
+        arrived, d_mix, n, g_, nq, w1s, w2s, z1, h, q1, gain, shift, piece, tiles, unroll=4
     )
     packed_back, rear_part = lax.optimization_barrier((packed_back, rear_part))
     rear_sum = lax.psum(rear_part, "sp")

time: 435 us -> 432 us (level)
  Pallas kernels: 210 us -> 203 us
  waiting for transfers between devices: 80.9 us -> 85.3 us
    unnamed x82 -> x84, local copies, waits for them, and re-layouts: 12.3 us -> 11.5 us
  transfers between devices with their start and end apart: 10 -> 10, of which waited for: 7 -> 7; matrix products, arithmetic and copies ran while one was open for 9% -> 9% of each run, Pallas kernels for 45% -> 44%
where the time goes in v7:
time: 432 us; the launch traced here: 431 us
  Pallas kernels  203 us (47%)
  waiting for transfers between devices  85.3 us (20%)
  blocking collectives  63.7 us (15%)
  local copies, waits for them, and re-layouts  19.8 us (5%)
  starting transfers between devices  18.8 us (4%)
  matrix products  16.7 us (4%)
  between operations  14.5 us (3%)
  other arithmetic  8.82 us (2%)
    pallas_call x1, Pallas kernels, bwd_call(): pl.pallas_call(functools.partial(bwd_kernel, slots, count, unroll, piece,...  83.5 us
    pallas_call x1, Pallas kernels, fwd_call(): pl.pallas_call(functools.partial(fwd_kernel, slots, count, unroll, piece,...  71.4 us
    all_to_all x5, waiting for transfers between devices, swap(): return lax.all_to_all(block, axes, split_axis=0, concat_axis=0, tiled=True)  52.3 us
    all_gather x1, blocking collectives, shards(): weight_all = lax.all_gather(got_sum, 'sp', axis=0)  22.3 us
    all_gather x1, waiting for transfers between devices, shards(): all_tokens = lax.all_gather(tokens[:, 0], 'sp', axis=0)  20.8 us
    all_to_all x1, blocking collectives, swap(): return lax.all_to_all(block, axes, split_axis=0, concat_axis=0, tiled=True)  18.8 us
    all_to_all x5, starting transfers between devices, swap(): return lax.all_to_all(block, axes, split_axis=0, concat_axis=0, tiled=True)  18.4 us
    pallas_call x1, Pallas kernels, rear_grad_call(): pl.pallas_call(functools.partial(rear_grad_kernel, starts, per_step), gri...  14.3 us
  transfers between devices with their start and end apart: 10, of which 7 were waited for; matrix products, arithmetic and copies ran while one was open for 9% of the time, Pallas kernels for 44%

profile of v7, /device:TPU:0, one launch (start us, length us, event | category | flops | bytes accessed | tf_op | source)
XLA Modules:
  0.0 430.7 jit_solution(2683460134458438528)
XLA Ops:
  14.2 13.3 %all_gather.21.w_ref.front_ref = bf16[768,640]{1,0:T(8,128)(2,1)} all-gather(bf16[96,640]{1,0:T(8,128)(2,1)S(1)} %pad.13), channel_id=1, replica_groups=mesh['sp'=4,'fsdp'=8] {'fsdp'}, dimensions={0}, use_global_device_ids=true | all-gather | bytes 1105920 | tf_op jit(solution)/shard_map/all_gather | solution.py:365
  28.6 20.8 %all-gather.10.cloned.1.call-done = bf16[16,1,64,768]{3,2,1,0:T(8,128)(2,1)} async-done(((bf16[4,1,64,768]{3,2,1,0:T(8,128)(2,1)}), bf16[16,1,64,768]{3,2,1,0:T(8,128)(2,1)}) %all-gather.10.cloned.1.call-update) | async-done | bytes 1572880 | tf_op jit(solution)/shard_map/all_gather | solution.py:825
  51.6 6.2 %front.1 = (bf16[4,4,64,768]{3,2,1,0:T(8,128)(2,1)}, f32[4,4,64,128]{3,2,1,0:T(8,128)}, bf16[2,4,784,128]{3,2,1,0:T(8,128)(2,1)}, f32[2,768]{1,0:T(2,128)}) custom-call(bf16[4,4,64,768]{3,2,1,0:T(8,128)(2,1)} %bitcast.132, bf16[768,640]{1,0:T(8,128)(2,1)} %all_gather.21.w_ref.front_ref), custom_call_target="tpu_custom_call" | custom-call | flops 1000000000 | bytes 7000000 | tf_op jit(solution)/shard_map/front/pallas_call | solution.py:754
  57.8 3.8 all-to-all-start
  66.6 19.8 %all-to-all-done.x_ref = bf16[8,784,128]{2,1,0:T(8,128)(2,1)S(1)} async-done(((bf16[8,784,128]{2,1,0:T(8,128)(2,1)}), bf16[8,784,128]{2,1,0:T(8,128)(2,1)S(1)}, u32[]{:S(2)}, u32[]{:S(2)}) %all-to-all-start) | async-done | bytes 1605664 | tf_op jit(solution)/shard_map/all_to_all | solution.py:369
  87.5 71.4 %inner_forward.1 = (bf16[2048,128]{1,0:T(8,128)(2,1)}, bf16[2,128,64,256]{3,2,1,0:T(8,128)(2,1)}, bf16[2,128,64,256]{3,2,1,0:T(8,128)(2,1)}, bf16[2,2048,256]{2,...) custom-call(bf16[8,784,128]{2,1,0:T(8,128)(2,1)} %copy-done.1, ...), custom_call_target="tpu_custom_call" | custom-call | flops 89999998976 | bytes 40000000 | tf_op jit(solution)/shard_map/inner_forward/pallas_call | solution.py:171
  159.0 3.2 all-to-all-start.1
  164.8 4.3 fusion.15.gh_ref
  169.0 3.1 multiply_add_fusion
  172.1 4.4 %all-to-all-done.1 = bf16[32,64,128]{2,1,0:T(8,128)(2,1)S(1)} async-done(((bf16[32,64,128]{2,1,0:T(8,128)(2,1)}), bf16[32,64,128]{2,1,0:T(8,128)(2,1)S(1)}, u32[]{:S(2)}, u32[]{:S(2)}) %all-to-all-start.1) | async-done | bytes 524320 | tf_op jit(solution)/shard_map/all_to_all | solution.py:369
  177.4 12.4 %rear.1 = (bf16[8,4,64,128]{3,2,1,0:T(8,128)(2,1)}, bf16[2,768,256]{2,1,0:T(8,128)(2,1)}, bf16[256,5632]{1,0:T(8,128)(2,1)}, bf16[256,2048]{1,0:T(8,128)(2,1)}, f32[256,768]{1,0:T(8,128)}, /*index=5*/f32[256,768]{1,0:T(8,128)}) custom-call(bf16[8,4,64,128]{3,2,1,0:T(8,128)(2,1)} %bitcast.100, f32[256,768]{1,0:T(8,128)} %get-tuple-element.94.act_ref, ...), custom_call_target="tpu_custom_call" | custom-call | flops 5000000000 | bytes 16000000 | tf_op jit(solution)/shard_map/rear/pallas_call | solution.py:571
  189.8 4.1 all-to-all-start.2
  194.1 14.3 %rear_gradients.1 = bf16[8,2880,256]{2,1,0:T(8,128)(2,1)} custom-call(bf16[2,768,256]{2,1,0:T(8,128)(2,1)} %get-tuple-element.101.lhs_ref, bf16[768,256]{1,0:T(8,128)(2,1)} %bitcast.93, bf16[768,256]{1,0:T(8,128)(2,1)} %fusion.23.low_ref, bf16[256,5632]{1,0:T(8,128)(2,1)} %get-tuple-element.104.rhs_ref, bf16[256,2048]{1,0:T(8,128)(2,1)} %get-tuple-element.99.hid_ref), custom_call_target="tpu_custom_call" | custom-call | flops 4000000000 | bytes 16000000 | tf_op jit(solution)/shard_map/rear_gradients/pallas_call | solution.py:632
  209.2 83.5 %inner_backward.1 = (bf16[8,784,128]{2,1,0:T(8,128)(2,1)}, f32[2,64,256]{2,1,0:T(8,128)}, f32[2,1,256]{2,1,0:T(1,128)}, f32[2,64,256]{2,1,0:T(8,128)}, f32[2,1,6...) custom-call(bf16[8,784,128]{2,1,0:T(8,128)(2,1)} %copy-done.1, bf16[2048,128]{1,0:T(8,128)(2,1)} %bitcast.98, ...), custom_call_target="tpu_custom_call" | custom-call | flops 109999996928 | bytes 40000000 | tf_op jit(solution)/shard_map/inner_backward/pallas_call | solution.py:346
  292.8 5.3 %reduce-scatter.2.cloned.1.call-done = bf16[2880,256]{1,0:T(8,128)(2,1)} async-done(((bf16[23040,256]{1,0:T(8,128)(2,1)}), bf16[2880,256]{1,0:T(8,128)(2,1)}) %reduce-scatter.2.cloned.1.call-update) | async-done | bytes 1474576 | tf_op jit(solution)/shard_map/reduce_scatter | solution.py:878
  298.0 3.7 all-to-all-start.3
  302.5 20.6 %all-to-all-done.3.a_ref = bf16[8,784,128]{2,1,0:T(8,128)(2,1)S(1)} async-done(((bf16[8,784,128]{2,1,0:T(8,128)(2,1)}), bf16[8,784,128]{2,1,0:T(8,128)(2,1)S(1)}, u32[]{:S(2)}, u32[]{:S(2)}) %all-to-all-start.3) | async-done | bytes 1605664 | tf_op jit(solution)/shard_map/all_to_all | solution.py:369
  324.3 6.1 %projection_gradients.1 = (bf16[4,4,64,640]{3,2,1,0:T(8,128)(2,1)}, bf16[4,4,64,768]{3,2,1,0:T(8,128)(2,1)}) custom-call(bf16[8,784,128]{2,1,0:T(8,128)(2,1)} %copy-done.2, f32[4,4,64,128]{3,2,1,0:T(8,128)} %get-tuple-element.117.slope_ref, bf16[768,640]{1,0:T(8,128)(2,1)} %all_gather.21.w_ref.front_ref), custom_call_target="tpu_custom_call" | custom-call | flops 1000000000 | bytes 8000000 | tf_op jit(solution)/shard_map/projection_gradients/pallas_call | solution.py:432
  330.4 2.7 bitcast_convert_fusion
  333.2 18.8 %all_to_all.30 = bf16[8,110,640]{2,1,0:T(8,128)(2,1)S(1)} all-to-all(bf16[8,110,640]{2,1,0:T(8,128)(2,1)S(1)} %pad_maximum_fusion), channel_id=1, replica_groups=mesh['sp'=4,'fsdp'=8] {'fsdp'}, dimensions={0} | all-to-all | bytes 2252800 | tf_op jit(solution)/shard_map/all_to_all | solution.py:369
  352.2 22.3 %all-gather.1 = bf16[384,640]{1,0:T(8,128)(2,1)} all-gather(bf16[96,640]{1,0:T(8,128)(2,1)S(1)} %slice_reduce_fusion), channel_id=3, replica_groups=mesh['sp'=4,'fsdp'=8] {'sp'}, dimensions={0}, use_global_device_ids=true | all-gather | bytes 614400 | tf_op jit(solution)/shard_map/all_gather | solution.py:904
  374.4 5.5 %all-reduce.5.cloned.1.call-done.sum_ref = bf16[2880,256]{1,0:T(8,128)(2,1)} async-done(((bf16[2880,256]{1,0:T(8,128)(2,1)}), bf16[2880,256]{1,0:T(8,128)(2,1)}) %all-reduce.5.cloned.1.call-update) | async-done | bytes 1474576 | tf_op jit(solution)/shard_map/psum | solution.py:886
  379.9 3.6 all-to-all-start.5
  383.5 2.9 fusion.1.gate_ref
  386.4 3.6 fusion
  390.5 3.5 rear_unpack.1
  394.0 1.4 reduce.5
  395.5 2.5 weight_gradients.1
  398.0 1.4 reduce.6
  399.4 9.3 %all_gather.27 = bf16[3,136,256]{2,0,1:T(4,128)(2,1)S(1)} all-gather(bf16[3,17,256]{2,0,1:T(4,128)(2,1)S(1)} %bitcast.107), channel_id=1, replica_groups=mesh['sp'=4,'fsdp'=8] {'fsdp'}, dimensions={1}, use_global_device_ids=true | all-gather | bytes 235008 | tf_op jit(solution)/shard_map/all_gather | solution.py:921
  412.2 7.5 %all-to-all-done.5.parts_ref = bf16[4,256,768]{2,1,0:T(8,128)(2,1)S(1)} async-done(((bf16[4,256,768]{2,1,0:T(8,128)(2,1)}), bf16[4,256,768]{2,1,0:T(8,128)(2,1)S(1)}, u32[]{:S(2)}, u32[]{:S(2)}) %all-to-all-start.5) | async-done | bytes 1572896 | tf_op jit(solution)/shard_map/all_to_all | solution.py:369
  420.9 3.2 token_gradients.1
  (166 shorter events, 27.5 us)
Async XLA Ops:
  7.2 42.2 %all-gather.10.cloned.1.call-start = ((), (), s32[]{:S(2)}) async-start(), calls=%async_computation.11 | async-start | bytes 1966080 | tf_op jit(solution)/shard_map/all_gather | solution.py:825
  7.9 156.8 %all-gather.8.cloned.1.call-start = ((), (), s32[]{:S(2)}) async-start(), calls=%async_computation.8 | async-start | bytes 3538944 | tf_op jit(solution)/shard_map/all_gather | solution.py:365
  8.0 19.5 %copy-start.3 = (bf16[96,2048]{1,0:T(8,128)(2,1)S(1)}, bf16[96,2048]{1,0:T(8,128)(2,1)}, u32[]{:S(2)}) copy-start(bf16[96,2048]{1,0:T(8,128)(2,1)} %fup_w.1) | copy-start | bytes 1179652
  8.0 19.5 %copy-start.4 = (bf16[96,2048]{1,0:T(8,128)(2,1)S(1)}, bf16[96,2048]{1,0:T(8,128)(2,1)}, u32[]{:S(2)}) copy-start(bf16[96,2048]{1,0:T(8,128)(2,1)} %fgate_w.1) | copy-start | bytes 1179652
  8.0 19.5 %copy-start.6 = (bf16[96,768]{1,0:T(8,128)(2,1)S(1)}, bf16[96,768]{1,0:T(8,128)(2,1)}, u32[]{:S(2)}) copy-start(bf16[96,768]{1,0:T(8,128)(2,1)} %gate_w.1) | copy-start | bytes 442372
  8.0 19.5 %copy-start.14 = (bf16[96,768]{1,0:T(8,128)(2,1)S(1)}, bf16[96,768]{1,0:T(8,128)(2,1)}, u32[]{:S(2)}) copy-start(bf16[96,768]{1,0:T(8,128)(2,1)} %param.29) | copy-start | bytes 442372
  8.9 19.7 %copy-start.12 = (bf16[96,1]{1,0:T(8,128)(2,1)}, bf16[96,1]{1,0:T(8,128)(2,1)S(1)}, u32[]{:S(2)}) copy-start(bf16[96,1]{1,0:T(8,128)(2,1)S(1)} %copy.101.pre_ref) | copy-start | bytes 580
  9.7 4.3 copy-start.13
  10.5 18.1 %copy-start.11 = (bf16[96,1]{1,0:T(8,128)(2,1)}, bf16[96,1]{1,0:T(8,128)(2,1)S(1)}, u32[]{:S(2)}) copy-start(bf16[96,1]{1,0:T(8,128)(2,1)S(1)} %copy.102.post_ref) | copy-start | bytes 580
  27.5 22.8 %copy-start.29 = (s32[4]{0:T(128)S(1)}, s32[4]{0:T(128)}, u32[]{:S(2)}) copy-start(s32[4]{0:T(128)} %param.21) | copy-start | bytes 52
  27.5 22.9 %copy-start.10 = (bf16[4,1,64,768]{3,2,1,0:T(8,128)(2,1)S(1)}, bf16[4,1,64,768]{3,2,1,0:T(8,128)(2,1)}, u32[]{:S(2)}) copy-start(bf16[4,1,64,768]{3,2,1,0:T(8,128)(2,1)} %param.22) | copy-start | bytes 1179652
  49.4 119.6 %all-gather.6.cloned.1.call-start = ((), (), s32[]{:S(2)}) async-start(), calls=%async_computation.7 | async-start | bytes 9732096 | tf_op jit(solution)/shard_map/all_gather | solution.py:365
  50.2 1.3 copy-start.17
  57.8 6.0 %copy-start.18 = (f32[3,64,256]{2,1,0:T(8,128)S(1)}, f32[3,64,256]{2,1,0:T(8,128)}, u32[]{:S(2)}) copy-start(f32[3,64,256]{2,1,0:T(8,128)} %param.34) | copy-start | bytes 589828
  57.8 28.6 %all-to-all-start = ((bf16[8,784,128]{2,1,0:T(8,128)(2,1)}), bf16[8,784,128]{2,1,0:T(8,128)(2,1)S(1)}, u32[]{:S(2)}, u32[]{:S(2)}) async-start(bf16[8,784,128]{2,1,0:T(8,128)(2,1)} %bitcast.89), calls=%async_computation | async-start | bytes 3211264 | tf_op jit(solution)/shard_map/all_to_all | solution.py:369
  159.0 5.2 %copy-start.20 = (f32[2,768]{1,0:T(2,128)S(1)}, f32[2,768]{1,0:T(2,128)}, u32[]{:S(2)}) copy-start(f32[2,768]{1,0:T(2,128)} %get-tuple-element.96) | copy-start | bytes 18436
  159.0 17.6 %all-to-all-start.1 = ((bf16[32,64,128]{2,1,0:T(8,128)(2,1)}), bf16[32,64,128]{2,1,0:T(8,128)(2,1)S(1)}, u32[]{:S(2)}, u32[]{:S(2)}) async-start(bf16[32,64,128]{2,1,0:T(8,128)(2,1)} %bitcast.99), calls=%async_computation.1 | async-start | bytes 1048576 | tf_op jit(solution)/shard_map/all_to_all | solution.py:369
  189.8 18.6 %all-to-all-start.2 = ((bf16[32,64,128]{2,1,0:T(8,128)(2,1)}), bf16[32,64,128]{2,1,0:T(8,128)(2,1)S(1)}, u32[]{:S(2)}, u32[]{:S(2)}) async-start(bf16[32,64,128]{2,1,0:T(8,128)(2,1)} %bitcast.101), calls=%async_computation.2 | async-start | bytes 1048576 | tf_op jit(solution)/shard_map/all_to_all | solution.py:369
  193.9 104.1 %reduce-scatter.2.cloned.1.call-start = ((), (), s32[]{:S(2)}) async-start(), calls=%async_computation.9 | async-start | bytes 13271040 | tf_op jit(solution)/shard_map/reduce_scatter | solution.py:878
  298.0 3.8 copy-start.21
  298.0 4.0 copy-start.25
  298.0 4.0 copy-start.24
  298.0 4.1 copy-start.22
  298.0 4.2 copy-start.9
  298.0 4.2 copy-start.15
  298.0 25.0 %all-to-all-start.3 = ((bf16[8,784,128]{2,1,0:T(8,128)(2,1)}), bf16[8,784,128]{2,1,0:T(8,128)(2,1)S(1)}, u32[]{:S(2)}, u32[]{:S(2)}) async-start(bf16[8,784,128]{2,1,0:T(8,128)(2,1)} %get-tuple-element.116), calls=%async_computation.4 | async-start | bytes 3211264 | tf_op jit(solution)/shard_map/all_to_all | solution.py:369
  301.8 78.2 %all-reduce.5.cloned.1.call-start = ((), (), s32[]{:S(2)}) async-start(), calls=%async_computation.10 | async-start | bytes 2949120 | tf_op jit(solution)/shard_map/psum | solution.py:886
  324.3 6.1 %copy-start.16 = (bf16[4,4,64,768]{3,2,1,0:T(8,128)(2,1)S(1)}, bf16[4,4,64,768]{3,2,1,0:T(8,128)(2,1)}, u32[]{:S(2)}) copy-start(bf16[4,4,64,768]{3,2,1,0:T(8,128)(2,1)} %get-tuple-element.90) | copy-start | bytes 4718596
  379.9 39.9 %all-to-all-start.5 = ((bf16[4,256,768]{2,1,0:T(8,128)(2,1)}), bf16[4,256,768]{2,1,0:T(8,128)(2,1)S(1)}, u32[]{:S(2)}, u32[]{:S(2)}) async-start(bf16[4,256,768]{2,1,0:T(8,128)(2,1)} %bitcast.90), calls=%async_computation.6 | async-start | bytes 3145728 | tf_op jit(solution)/shard_map/all_to_all | solution.py:369
  383.5 2.9 copy-start.5
  383.5 2.9 copy-start.30
  398.0 10.9 %copy-start.19 = (f32[96,12]{1,0:T(8,128)S(1)}, f32[96,12]{1,0:T(8,128)}, u32[]{:S(2)}) copy-start(f32[96,12]{1,0:T(8,128)} %get-tuple-element.198) | copy-start | bytes 13828
  (9 other events, 8.4 us)
Sparse Core Ops, SparseCore 0:
  9.6 39.7 all-gather.9
  51.3 41.6 all-gather.7
  94.9 54.6 all-gather.5
  208.6 89.4 reduce-scatter.1
  304.8 75.0 all-reduce.4

commit v8 on v7

--- a/solution.py
+++ b/solution.py
@@ -627,7 +627,7 @@
     own = width // S
     starts = (width // 256, 2 * width // 256, rhs.shape[1] // 256)
     blocks = starts[2] + width * hidden.shape[1] // S // 256 // own
-    per_step = 2 - blocks % 2
+    per_step = next(n for n in (5, 3, 2, 1) if blocks % n == 0)
     full = lambda a: pl.BlockSpec(a.shape, lambda n: (0,) * a.ndim, pipeline_mode=pl.Buffered(1))
     return pl.pallas_call(
         functools.partial(rear_grad_kernel, starts, per_step),

time: 432 us -> 430 us (level)
  transfers between devices with their start and end apart: 10 -> 10, of which waited for: 7 -> 8; matrix products, arithmetic and copies ran while one was open for 9% -> 9% of each run, Pallas kernels for 44% -> 43%
where the time goes in v8:
time: 430 us; the launch traced here: 429 us
  Pallas kernels  202 us (47%)
  waiting for transfers between devices  85.3 us (20%)
  blocking collectives  63.7 us (15%)
  local copies, waits for them, and re-layouts  19.8 us (5%)
  starting transfers between devices  18.8 us (4%)
  matrix products  16.7 us (4%)
  between operations  14.5 us (3%)
  other arithmetic  8.82 us (2%)
    pallas_call x1, Pallas kernels, bwd_call(): pl.pallas_call(functools.partial(bwd_kernel, slots, count, unroll, piece,...  83.5 us
    pallas_call x1, Pallas kernels, fwd_call(): pl.pallas_call(functools.partial(fwd_kernel, slots, count, unroll, piece,...  71.4 us
    all_to_all x5, waiting for transfers between devices, swap(): return lax.all_to_all(block, axes, split_axis=0, concat_axis=0, tiled=True)  53.9 us
    all_gather x1, blocking collectives, shards(): weight_all = lax.all_gather(got_sum, 'sp', axis=0)  22.3 us
    all_gather x1, waiting for transfers between devices, shards(): all_tokens = lax.all_gather(tokens[:, 0], 'sp', axis=0)  20.8 us
    all_to_all x1, blocking collectives, swap(): return lax.all_to_all(block, axes, split_axis=0, concat_axis=0, tiled=True)  18.8 us
    all_to_all x5, starting transfers between devices, swap(): return lax.all_to_all(block, axes, split_axis=0, concat_axis=0, tiled=True)  18.4 us
    all_gather x1, blocking collectives, gather(): return lax.all_gather(block, 'fsdp', axis=0, tiled=True)  13.3 us
  transfers between devices with their start and end apart: 10, of which 8 were waited for; matrix products, arithmetic and copies ran while one was open for 9% of the time, Pallas kernels for 43%

profile of v8, /device:TPU:0, one launch (start us, length us, event | category | flops | bytes accessed | tf_op | source)
XLA Modules:
  0.0 429.1 jit_solution(17375867317915535115)
XLA Ops:
  14.2 13.3 %all_gather.21.w_ref.front_ref = bf16[768,640]{1,0:T(8,128)(2,1)} all-gather(bf16[96,640]{1,0:T(8,128)(2,1)S(1)} %pad.13), channel_id=1, replica_groups=mesh['sp'=4,'fsdp'=8] {'fsdp'}, dimensions={0}, use_global_device_ids=true | all-gather | bytes 1105920 | tf_op jit(solution)/shard_map/all_gather | solution.py:365
  28.6 20.8 %all-gather.10.cloned.1.call-done = bf16[16,1,64,768]{3,2,1,0:T(8,128)(2,1)} async-done(((bf16[4,1,64,768]{3,2,1,0:T(8,128)(2,1)}), bf16[16,1,64,768]{3,2,1,0:T(8,128)(2,1)}) %all-gather.10.cloned.1.call-update) | async-done | bytes 1572880 | tf_op jit(solution)/shard_map/all_gather | solution.py:825
  51.6 6.2 %front.1 = (bf16[4,4,64,768]{3,2,1,0:T(8,128)(2,1)}, f32[4,4,64,128]{3,2,1,0:T(8,128)}, bf16[2,4,784,128]{3,2,1,0:T(8,128)(2,1)}, f32[2,768]{1,0:T(2,128)}) custom-call(bf16[4,4,64,768]{3,2,1,0:T(8,128)(2,1)} %bitcast.132, bf16[768,640]{1,0:T(8,128)(2,1)} %all_gather.21.w_ref.front_ref), custom_call_target="tpu_custom_call" | custom-call | flops 1000000000 | bytes 7000000 | tf_op jit(solution)/shard_map/front/pallas_call | solution.py:754
  57.8 3.8 all-to-all-start
  66.6 19.8 %all-to-all-done.x_ref = bf16[8,784,128]{2,1,0:T(8,128)(2,1)S(1)} async-done(((bf16[8,784,128]{2,1,0:T(8,128)(2,1)}), bf16[8,784,128]{2,1,0:T(8,128)(2,1)S(1)}, u32[]{:S(2)}, u32[]{:S(2)}) %all-to-all-start) | async-done | bytes 1605664 | tf_op jit(solution)/shard_map/all_to_all | solution.py:369
  87.5 71.4 %inner_forward.1 = (bf16[2048,128]{1,0:T(8,128)(2,1)}, bf16[2,128,64,256]{3,2,1,0:T(8,128)(2,1)}, bf16[2,128,64,256]{3,2,1,0:T(8,128)(2,1)}, bf16[2,2048,256]{2,...) custom-call(bf16[8,784,128]{2,1,0:T(8,128)(2,1)} %copy-done.1, ...), custom_call_target="tpu_custom_call" | custom-call | flops 89999998976 | bytes 40000000 | tf_op jit(solution)/shard_map/inner_forward/pallas_call | solution.py:171
  159.0 3.2 all-to-all-start.1
  164.8 4.3 fusion.15.gh_ref
  169.0 3.1 multiply_add_fusion
  172.1 4.4 %all-to-all-done.1 = bf16[32,64,128]{2,1,0:T(8,128)(2,1)S(1)} async-done(((bf16[32,64,128]{2,1,0:T(8,128)(2,1)}), bf16[32,64,128]{2,1,0:T(8,128)(2,1)S(1)}, u32[]{:S(2)}, u32[]{:S(2)}) %all-to-all-start.1) | async-done | bytes 524320 | tf_op jit(solution)/shard_map/all_to_all | solution.py:369
  177.4 12.4 %rear.1 = (bf16[8,4,64,128]{3,2,1,0:T(8,128)(2,1)}, bf16[2,768,256]{2,1,0:T(8,128)(2,1)}, bf16[256,5632]{1,0:T(8,128)(2,1)}, bf16[256,2048]{1,0:T(8,128)(2,1)}, f32[256,768]{1,0:T(8,128)}, /*index=5*/f32[256,768]{1,0:T(8,128)}) custom-call(bf16[8,4,64,128]{3,2,1,0:T(8,128)(2,1)} %bitcast.100, f32[256,768]{1,0:T(8,128)} %get-tuple-element.94.act_ref, ...), custom_call_target="tpu_custom_call" | custom-call | flops 5000000000 | bytes 16000000 | tf_op jit(solution)/shard_map/rear/pallas_call | solution.py:571
  189.8 4.1 all-to-all-start.2
  194.1 12.6 %rear_gradients.1 = bf16[8,2880,256]{2,1,0:T(8,128)(2,1)} custom-call(bf16[2,768,256]{2,1,0:T(8,128)(2,1)} %get-tuple-element.101.lhs_ref, bf16[768,256]{1,0:T(8,128)(2,1)} %bitcast.93, bf16[768,256]{1,0:T(8,128)(2,1)} %fusion.23.low_ref, bf16[256,5632]{1,0:T(8,128)(2,1)} %get-tuple-element.104.rhs_ref, bf16[256,2048]{1,0:T(8,128)(2,1)} %get-tuple-element.99.hid_ref), custom_call_target="tpu_custom_call" | custom-call | flops 4000000000 | bytes 16000000 | tf_op jit(solution)/shard_map/rear_gradients/pallas_call | solution.py:632
  206.7 1.5 all-to-all-done.2
  209.1 83.5 %inner_backward.1 = (bf16[8,784,128]{2,1,0:T(8,128)(2,1)}, f32[2,64,256]{2,1,0:T(8,128)}, f32[2,1,256]{2,1,0:T(1,128)}, f32[2,64,256]{2,1,0:T(8,128)}, f32[2,1,6...) custom-call(bf16[8,784,128]{2,1,0:T(8,128)(2,1)} %copy-done.1, bf16[2048,128]{1,0:T(8,128)(2,1)} %bitcast.98, ...), custom_call_target="tpu_custom_call" | custom-call | flops 109999996928 | bytes 40000000 | tf_op jit(solution)/shard_map/inner_backward/pallas_call | solution.py:346
  292.6 3.7 reduce-scatter.2.cloned.1.call-done
  296.4 3.7 all-to-all-start.3
  300.8 20.6 %all-to-all-done.3.a_ref = bf16[8,784,128]{2,1,0:T(8,128)(2,1)S(1)} async-done(((bf16[8,784,128]{2,1,0:T(8,128)(2,1)}), bf16[8,784,128]{2,1,0:T(8,128)(2,1)S(1)}, u32[]{:S(2)}, u32[]{:S(2)}) %all-to-all-start.3) | async-done | bytes 1605664 | tf_op jit(solution)/shard_map/all_to_all | solution.py:369
  322.6 6.1 %projection_gradients.1 = (bf16[4,4,64,640]{3,2,1,0:T(8,128)(2,1)}, bf16[4,4,64,768]{3,2,1,0:T(8,128)(2,1)}) custom-call(bf16[8,784,128]{2,1,0:T(8,128)(2,1)} %copy-done.2, f32[4,4,64,128]{3,2,1,0:T(8,128)} %get-tuple-element.117.slope_ref, bf16[768,640]{1,0:T(8,128)(2,1)} %all_gather.21.w_ref.front_ref), custom_call_target="tpu_custom_call" | custom-call | flops 1000000000 | bytes 8000000 | tf_op jit(solution)/shard_map/projection_gradients/pallas_call | solution.py:432
  328.7 2.7 bitcast_convert_fusion
  331.6 18.8 %all_to_all.30 = bf16[8,110,640]{2,1,0:T(8,128)(2,1)S(1)} all-to-all(bf16[8,110,640]{2,1,0:T(8,128)(2,1)S(1)} %pad_maximum_fusion), channel_id=1, replica_groups=mesh['sp'=4,'fsdp'=8] {'fsdp'}, dimensions={0} | all-to-all | bytes 2252800 | tf_op jit(solution)/shard_map/all_to_all | solution.py:369
  350.5 22.3 %all-gather.1 = bf16[384,640]{1,0:T(8,128)(2,1)} all-gather(bf16[96,640]{1,0:T(8,128)(2,1)S(1)} %slice_reduce_fusion), channel_id=3, replica_groups=mesh['sp'=4,'fsdp'=8] {'sp'}, dimensions={0}, use_global_device_ids=true | all-gather | bytes 614400 | tf_op jit(solution)/shard_map/all_gather | solution.py:904
  372.8 5.5 %all-reduce.5.cloned.1.call-done.sum_ref = bf16[2880,256]{1,0:T(8,128)(2,1)} async-done(((bf16[2880,256]{1,0:T(8,128)(2,1)}), bf16[2880,256]{1,0:T(8,128)(2,1)}) %all-reduce.5.cloned.1.call-update) | async-done | bytes 1474576 | tf_op jit(solution)/shard_map/psum | solution.py:886
  378.3 3.6 all-to-all-start.5
  381.9 2.9 fusion.1.gate_ref
  384.8 3.6 fusion
  388.9 3.5 rear_unpack.1
  393.8 2.5 weight_gradients.1
  396.3 1.4 reduce.6
  397.8 9.3 %all_gather.27 = bf16[3,136,256]{2,0,1:T(4,128)(2,1)S(1)} all-gather(bf16[3,17,256]{2,0,1:T(4,128)(2,1)S(1)} %bitcast.107), channel_id=1, replica_groups=mesh['sp'=4,'fsdp'=8] {'fsdp'}, dimensions={1}, use_global_device_ids=true | all-gather | bytes 235008 | tf_op jit(solution)/shard_map/all_gather | solution.py:921
  410.6 7.5 %all-to-all-done.5.parts_ref = bf16[4,256,768]{2,1,0:T(8,128)(2,1)S(1)} async-done(((bf16[4,256,768]{2,1,0:T(8,128)(2,1)}), bf16[4,256,768]{2,1,0:T(8,128)(2,1)S(1)}, u32[]{:S(2)}, u32[]{:S(2)}) %all-to-all-start.5) | async-done | bytes 1572896 | tf_op jit(solution)/shard_map/all_to_all | solution.py:369
  419.3 3.2 token_gradients.1
  (166 shorter events, 28.9 us)
Async XLA Ops:
  7.2 42.2 %all-gather.10.cloned.1.call-start = ((), (), s32[]{:S(2)}) async-start(), calls=%async_computation.11 | async-start | bytes 1966080 | tf_op jit(solution)/shard_map/all_gather | solution.py:825
  7.9 156.8 %all-gather.8.cloned.1.call-start = ((), (), s32[]{:S(2)}) async-start(), calls=%async_computation.8 | async-start | bytes 3538944 | tf_op jit(solution)/shard_map/all_gather | solution.py:365
  8.0 19.5 %copy-start.3 = (bf16[96,2048]{1,0:T(8,128)(2,1)S(1)}, bf16[96,2048]{1,0:T(8,128)(2,1)}, u32[]{:S(2)}) copy-start(bf16[96,2048]{1,0:T(8,128)(2,1)} %fup_w.1) | copy-start | bytes 1179652
  8.0 19.5 %copy-start.4 = (bf16[96,2048]{1,0:T(8,128)(2,1)S(1)}, bf16[96,2048]{1,0:T(8,128)(2,1)}, u32[]{:S(2)}) copy-start(bf16[96,2048]{1,0:T(8,128)(2,1)} %fgate_w.1) | copy-start | bytes 1179652
  8.0 19.5 %copy-start.6 = (bf16[96,768]{1,0:T(8,128)(2,1)S(1)}, bf16[96,768]{1,0:T(8,128)(2,1)}, u32[]{:S(2)}) copy-start(bf16[96,768]{1,0:T(8,128)(2,1)} %gate_w.1) | copy-start | bytes 442372
  8.0 19.5 %copy-start.14 = (bf16[96,768]{1,0:T(8,128)(2,1)S(1)}, bf16[96,768]{1,0:T(8,128)(2,1)}, u32[]{:S(2)}) copy-start(bf16[96,768]{1,0:T(8,128)(2,1)} %param.29) | copy-start | bytes 442372
  8.9 19.7 %copy-start.12 = (bf16[96,1]{1,0:T(8,128)(2,1)}, bf16[96,1]{1,0:T(8,128)(2,1)S(1)}, u32[]{:S(2)}) copy-start(bf16[96,1]{1,0:T(8,128)(2,1)S(1)} %copy.101.pre_ref) | copy-start | bytes 580
  9.7 4.3 %copy-start.13 = (bf16[96,12]{1,0:T(8,128)(2,1)}, bf16[96,12]{1,0:T(8,128)(2,1)S(1)}, u32[]{:S(2)}) copy-start(bf16[96,12]{1,0:T(8,128)(2,1)S(1)} %copy.100.r_ref) | copy-start | bytes 6916
  10.5 18.1 %copy-start.11 = (bf16[96,1]{1,0:T(8,128)(2,1)}, bf16[96,1]{1,0:T(8,128)(2,1)S(1)}, u32[]{:S(2)}) copy-start(bf16[96,1]{1,0:T(8,128)(2,1)S(1)} %copy.102.post_ref) | copy-start | bytes 580
  27.5 22.8 %copy-start.29 = (s32[4]{0:T(128)S(1)}, s32[4]{0:T(128)}, u32[]{:S(2)}) copy-start(s32[4]{0:T(128)} %param.21) | copy-start | bytes 52
  27.5 22.9 %copy-start.10 = (bf16[4,1,64,768]{3,2,1,0:T(8,128)(2,1)S(1)}, bf16[4,1,64,768]{3,2,1,0:T(8,128)(2,1)}, u32[]{:S(2)}) copy-start(bf16[4,1,64,768]{3,2,1,0:T(8,128)(2,1)} %param.22) | copy-start | bytes 1179652
  49.4 119.6 %all-gather.6.cloned.1.call-start = ((), (), s32[]{:S(2)}) async-start(), calls=%async_computation.7 | async-start | bytes 9732096 | tf_op jit(solution)/shard_map/all_gather | solution.py:365
  50.2 1.3 copy-start.17
  57.8 6.0 %copy-start.18 = (f32[3,64,256]{2,1,0:T(8,128)S(1)}, f32[3,64,256]{2,1,0:T(8,128)}, u32[]{:S(2)}) copy-start(f32[3,64,256]{2,1,0:T(8,128)} %param.34) | copy-start | bytes 589828
  57.8 28.6 %all-to-all-start = ((bf16[8,784,128]{2,1,0:T(8,128)(2,1)}), bf16[8,784,128]{2,1,0:T(8,128)(2,1)S(1)}, u32[]{:S(2)}, u32[]{:S(2)}) async-start(bf16[8,784,128]{2,1,0:T(8,128)(2,1)} %bitcast.89), calls=%async_computation | async-start | bytes 3211264 | tf_op jit(solution)/shard_map/all_to_all | solution.py:369
  159.0 5.2 %copy-start.20 = (f32[2,768]{1,0:T(2,128)S(1)}, f32[2,768]{1,0:T(2,128)}, u32[]{:S(2)}) copy-start(f32[2,768]{1,0:T(2,128)} %get-tuple-element.96) | copy-start | bytes 18436
  159.0 17.6 %all-to-all-start.1 = ((bf16[32,64,128]{2,1,0:T(8,128)(2,1)}), bf16[32,64,128]{2,1,0:T(8,128)(2,1)S(1)}, u32[]{:S(2)}, u32[]{:S(2)}) async-start(bf16[32,64,128]{2,1,0:T(8,128)(2,1)} %bitcast.99), calls=%async_computation.1 | async-start | bytes 1048576 | tf_op jit(solution)/shard_map/all_to_all | solution.py:369
  189.8 18.5 %all-to-all-start.2 = ((bf16[32,64,128]{2,1,0:T(8,128)(2,1)}), bf16[32,64,128]{2,1,0:T(8,128)(2,1)S(1)}, u32[]{:S(2)}, u32[]{:S(2)}) async-start(bf16[32,64,128]{2,1,0:T(8,128)(2,1)} %bitcast.101), calls=%async_computation.2 | async-start | bytes 1048576 | tf_op jit(solution)/shard_map/all_to_all | solution.py:369
  193.9 102.4 %reduce-scatter.2.cloned.1.call-start = ((), (), s32[]{:S(2)}) async-start(), calls=%async_computation.9 | async-start | bytes 13271040 | tf_op jit(solution)/shard_map/reduce_scatter | solution.py:878
  296.4 3.8 copy-start.21
  296.4 4.0 copy-start.25
  296.4 4.0 copy-start.24
  296.4 4.1 copy-start.22
  296.4 4.2 copy-start.9
  296.4 4.2 copy-start.15
  296.4 25.0 %all-to-all-start.3 = ((bf16[8,784,128]{2,1,0:T(8,128)(2,1)}), bf16[8,784,128]{2,1,0:T(8,128)(2,1)S(1)}, u32[]{:S(2)}, u32[]{:S(2)}) async-start(bf16[8,784,128]{2,1,0:T(8,128)(2,1)} %get-tuple-element.116), calls=%async_computation.4 | async-start | bytes 3211264 | tf_op jit(solution)/shard_map/all_to_all | solution.py:369
  300.1 78.2 %all-reduce.5.cloned.1.call-start = ((), (), s32[]{:S(2)}) async-start(), calls=%async_computation.10 | async-start | bytes 2949120 | tf_op jit(solution)/shard_map/psum | solution.py:886
  322.6 6.1 %copy-start.16 = (bf16[4,4,64,768]{3,2,1,0:T(8,128)(2,1)S(1)}, bf16[4,4,64,768]{3,2,1,0:T(8,128)(2,1)}, u32[]{:S(2)}) copy-start(bf16[4,4,64,768]{3,2,1,0:T(8,128)(2,1)} %get-tuple-element.90) | copy-start | bytes 4718596
  378.3 39.9 %all-to-all-start.5 = ((bf16[4,256,768]{2,1,0:T(8,128)(2,1)}), bf16[4,256,768]{2,1,0:T(8,128)(2,1)S(1)}, u32[]{:S(2)}, u32[]{:S(2)}) async-start(bf16[4,256,768]{2,1,0:T(8,128)(2,1)} %bitcast.90), calls=%async_computation.6 | async-start | bytes 3145728 | tf_op jit(solution)/shard_map/all_to_all | solution.py:369
  381.8 2.9 copy-start.5
  381.8 2.9 copy-start.30
  396.3 10.9 %copy-start.19 = (f32[96,12]{1,0:T(8,128)S(1)}, f32[96,12]{1,0:T(8,128)}, u32[]{:S(2)}) copy-start(f32[96,12]{1,0:T(8,128)} %get-tuple-element.198) | copy-start | bytes 13828
  (9 other events, 8.4 us)
Sparse Core Ops, SparseCore 0:
  9.6 39.7 all-gather.9
  51.3 41.6 all-gather.7
  94.9 54.6 all-gather.5
  208.4 87.8 reduce-scatter.1
  303.2 75.0 all-reduce.4
